TPU v7x, 32 devices: a whole 2x2x4 slice. The times are simulated.
32 devices in a mesh: groups: 2 (over x), shard: 8 (over z, y), tensor: 2 (over core).
Axes of the slice: x: 2, y: 2, z: 4, core: 2. Of those that a mesh axis runs over, the one named last changes fastest.
Arguments:
- hidden: bfloat16 [2048, 16384], P(('groups', 'shard'), 'tensor'), parts along dimension 0, may hold values from -6 to 6
- codes: bfloat16 [16384, 1024], P('tensor', 'shard'), may hold values from -448 to 448
- scales: float32 [128, 8], P('tensor'), may hold values from 3.6621095e-05 to 0.00036621094
- queries: bfloat16 [2048, 8192], P(('groups', 'shard'), 'tensor'), parts along dimension 0, may hold values from -160 to 160
- segment_ids: int32 [2048], P(('groups', 'shard')), parts along dimension 0, may hold values from 0 to 2, never falling along the last dimension, each value on 1 to 640 neighbouring positions
Outputs:
- attended: bfloat16 [2048, 8192], P(('groups', 'shard'), 'tensor'), parts along dimension 0
There are 2 independent parts, one for each index of `groups`. A program takes and returns all parts, laid end to end along the dimension named above; an argument that names none is the same for every part. Nothing has to cross between parts.
All inputs are finite; a program needn't handle non-finite values.
Results may differ from a plain program's by a relative error of at most 0.006.
The roundings to bfloat16 on the way count: a program that leaves them out, or rounds other values in their place, can miss the bound.
Values may be sent and summed in bfloat16 or wider, within the bound.
No kernel may reach another device: no remote copies, remote signals or barrier semaphores. Data moves between devices by JAX's collectives and lax.ppermute only.
A program may use at most 192 MiB of HBM per device.

v0:
```python
import math

import jax
import jax.numpy as jnp
from jax import lax
from jax.sharding import PartitionSpec as P

KVH = 4
HD = 128
QPK = 16
BLK = 128
KVW = 1024


def on_device(hidden, codes, scales, queries, segment_ids):
    rows = hidden.shape[0]
    local_heads = KVH // lax.axis_size("tensor")
    half = KVW // lax.axis_size("tensor")
    first_row = lax.axis_index("shard") * rows
    scale_blocks = scales.shape[1]
    longest = (lax.axis_size("shard") // 2 + 1) * rows
    piece = lax.all_gather(codes, "shard", axis=1, tiled=True)
    width = piece.shape[1]
    column_block = jnp.arange(width, dtype=jnp.int32) // BLK
    picker = (column_block[None, :] == jnp.arange(scale_blocks, dtype=jnp.int32)[:, None]).astype(
        jnp.float32
    )
    column_scale = jnp.dot(scales, picker, precision=lax.Precision.HIGHEST)
    blocked = (
        piece.astype(jnp.float32).reshape(scales.shape[0], BLK, width) * column_scale[:, None, :]
    )
    weight = blocked.reshape(piece.shape[0], width).astype(jnp.bfloat16)
    partial_kv = jnp.dot(hidden, weight, preferred_element_type=jnp.float32)
    summed = lax.psum(partial_kv, "tensor")
    mine = lax.dynamic_slice_in_dim(summed, lax.axis_index("tensor") * half, half, 1)
    keyval = mine.astype(jnp.bfloat16)
    query_local = queries.reshape(rows, local_heads, QPK, HD)
    scaling = 1.0 / math.sqrt(HD)
    rowpos = first_row + jnp.arange(rows, dtype=jnp.int32)
    initial = (
        jnp.full((local_heads, QPK, rows), -jnp.inf, jnp.float32),
        jnp.zeros((local_heads, QPK, rows), jnp.float32),
        jnp.zeros((rows, local_heads, QPK, HD), jnp.float32),
    )
    start = jnp.int32(0)
    kv_piece = lax.all_gather(keyval, "shard", axis=0, tiled=True)
    seg_piece = lax.all_gather(segment_ids, "shard", axis=0, tiled=True)
    count = seg_piece.shape[0]
    colpos = jnp.arange(count, dtype=jnp.int32)
    allowed = (
        (segment_ids[:, None] == seg_piece[None, :])
        & (colpos[None, :] <= rowpos[:, None])
        & (colpos[None, :] >= 0)
    )
    split_kv = kv_piece.reshape(count, local_heads, 2, HD)

    def compute(state):
        best, total, accum = state
        new_best, new_total, new_accum = ([], [], [])
        for group in range(local_heads):
            scores = (
                jnp.einsum(
                    "qph,kh->pqk",
                    query_local[:, group],
                    split_kv[:, group, 0],
                    preferred_element_type=jnp.float32,
                )
                * scaling
            )
            scores = jnp.where(allowed[None], scores, -jnp.inf)
            peak = jnp.max(scores, axis=-1)
            safe = jnp.where(peak == -jnp.inf, 0.0, peak)
            weights = jnp.exp(scores - safe[..., None])
            shrink = jnp.exp(best[group] - safe)
            new_total.append(total[group] * shrink + jnp.sum(weights, axis=-1))
            update = jnp.einsum(
                "pqk,kh->qph",
                weights.astype(jnp.bfloat16),
                split_kv[:, group, 1],
                preferred_element_type=jnp.float32,
            )
            new_accum.append(accum[:, group] * jnp.transpose(shrink)[..., None] + update)
            new_best.append(peak)
        return (jnp.stack(new_best), jnp.stack(new_total), jnp.stack(new_accum, axis=1))

    needed = (start <= first_row + rows - 1) & (start + count - 1 >= first_row - longest + 1)
    best, total, accum = lax.cond(needed, compute, lambda state: state, initial)
    result = accum / jnp.transpose(total, (2, 0, 1))[..., None]
    return result.astype(jnp.bfloat16).reshape(rows, local_heads * QPK * HD)


def solution(mesh):
    in_specs = (
        P(("groups", "shard"), "tensor"),
        P("tensor", "shard"),
        P("tensor", None),
        P(("groups", "shard"), "tensor"),
        P(("groups", "shard")),
    )
    out_specs = P(("groups", "shard"), "tensor")
    return jax.shard_map(
        on_device, mesh=mesh, in_specs=in_specs, out_specs=out_specs, check_vma=False
    )
```

profile of v0, /device:TPU:28, one launch (start us, length us, event | category | flops | bytes accessed | tf_op | source)
XLA Modules:
  0.0 320.4 jit_solution(14389092913333780112)
XLA Ops:
  6.5 0.0 copy-start
  6.5 0.0 all-gather.4.cloned.1.call-start
  6.5 0.7 all-gather.4.cloned.1.call-update
  7.3 0.0 all-gather.6.cloned.1.call-start
  7.3 1.0 convolution_bitcast_fusion.1
  8.3 227.0 %all-gather.4.cloned.1.call-done = bf16[8192,1024]{1,0:T(8,128)(2,1)} async-done(((bf16[8192,128]{1,0:T(8,128)(2,1)}), bf16[8192,1024]{1,0:T(8,128)(2,1)}) %all-gather.4.cloned.1.call-update) | async-done | bytes 16777232 | tf_op jit(solution)/shard_map/all_gather | solution.py:22
  235.3 9.9 %fusion.50 = bf16[8192,1024]{1,0:T(8,128)(2,1)S(1)} fusion(bf16[8192,1024]{1,0:T(8,128)(2,1)} %all-gather.4.cloned.1.call-done, f32[64,1024]{1,0:T(8,128)S(1)} %convolution_bitcast_fusion.1), kind=kLoop, calls=%fused_computation.57 | loop fusion | flops 25165824 | bytes 33816576 | tf_op jit(solution)/shard_map/convert_element_type | solution.py:32
  245.2 0.0 copy-done
  245.2 0.0 copy-start.2
  245.3 4.6 %convolution_bitcast_fusion = f32[128,1024]{0,1:T(8,128)S(1)} fusion(bf16[8192,1024]{1,0:T(8,128)(2,1)S(1)} %fusion.50, bf16[128,8192]{1,0:T(8,128)(2,1)S(1)} %copy-done), kind=kOutput, calls=%fused_computation.59 | convolution fusion | flops 2147483648 | bytes 19398656 | tf_op jit(solution)/shard_map/dot_general | solution.py:33
  249.8 4.8 %all-reduce.1 = bf16[128,1024]{0,1:T(8,128)(2,1)S(1)} all-reduce(f32[128,1024]{0,1:T(8,128)S(1)} %convolution_bitcast_fusion), channel_id=1, replica_groups=mesh['groups'=2,'shard'=8,'tensor'=2] {'tensor'}, use_global_device_ids=true, to_apply=%region_0.1 | all-reduce | flops 131072 | bytes 786432 | tf_op jit(solution)/shard_map/psum | solution.py:34
  254.6 0.7 dynamic-slice_convert_fusion
  255.3 0.0 all-gather.6.cloned.1.call-update
  255.4 0.0 copy-done.2
  255.4 17.1 %all-gather = s32[8,1,128]{2,1,0:T(1,128)S(1)} all-gather(s32[1,1,128]{2,1,0:T(1,128)S(1)} %bitcast.130), channel_id=1, replica_groups=mesh['groups'=2,'shard'=8,'tensor'=2] {'shard'}, dimensions={0}, use_global_device_ids=true | all-gather | bytes 4608 | tf_op jit(solution)/shard_map/all_gather | solution.py:47
  272.4 21.7 %all-gather.6.cloned.1.call-done = bf16[1024,512]{0,1:T(8,128)(2,1)} async-done(((bf16[128,512]{0,1:T(8,128)(2,1)}), bf16[1024,512]{0,1:T(8,128)(2,1)}) %all-gather.6.cloned.1.call-update) | async-done | bytes 1048592 | tf_op jit(solution)/shard_map/all_gather | solution.py:46
  294.2 15.3 %conditional.1 = (f32[2,16,128]{2,1,0:T(8,128)S(1)}, f32[128,2,16,128]{3,0,2,1:T(8,128)}) conditional(s32[]{:T(128)} %convert_element_type.22, () %tuple.13, (s32[128]{0:T(128)S(1)}, s32[1024]{0:T(1024)S(1)}, s32[]{:T(128)}, s32[128,1]{0,1:T(1,128)S(1)}, s32[128,1024]{0,1:T(8,128)S(1)}, /*index=5*/bf16[1024,512]{0,1:T(8,128)(2,1)}, ...), branch_computations={%region_1.2_spmd, %region_2.7_spmd} | conditional | flops 2195103744 | bytes 66558000 | solution.py:87
  294.2 0.2 compare_and_fusion
  294.4 1.6 copy.29
  296.1 0.0 copy-start.1
  296.1 2.3 fusion.4
  298.4 0.0 copy-done.1
  298.4 2.3 fusion.27
  300.8 3.1 fusion.1
  303.9 2.3 fusion.21
  306.2 1.6 pad_maximum_fusion
  307.8 1.7 fusion.3
  309.5 2.0 divide_convert_fusion
  311.5 0.7 copy.30
  312.2 1.4 copy.41
  (10 shorter events, 0.1 us)
Async XLA Ops:
  6.5 238.7 %copy-start = (bf16[128,8192]{1,0:T(8,128)(2,1)S(1)}, bf16[128,8192]{1,0:T(8,128)(2,1)}, u32[]{:S(2)}) copy-start(bf16[128,8192]{1,0:T(8,128)(2,1)} %param.7) | copy-start | bytes 6291460
  6.5 228.8 %all-gather.4.cloned.1.call-start = ((), (), s32[]{:S(2)}) async-start(), calls=%async_computation | async-start | bytes 18874368 | tf_op jit(solution)/shard_map/all_gather | solution.py:22
  7.3 286.9 %all-gather.6.cloned.1.call-start = ((), (), s32[]{:S(2)}) async-start(), calls=%async_computation.1 | async-start | bytes 1179648 | tf_op jit(solution)/shard_map/all_gather | solution.py:46
  245.2 10.1 %copy-start.2 = (s32[128]{0:T(128)S(1)}, s32[128]{0:T(128)}, u32[]{:S(2)}) copy-start(s32[128]{0:T(128)} %param.11) | copy-start | bytes 1540
  296.1 2.4 copy-start.1
Sparse Core Ops, SparseCore 0:
  9.4 225.8 all-gather.3
  255.5 38.6 all-gather.5
where the time goes:
time: 325 us; the launch traced here: 320 us
  waiting for transfers between devices  249 us (77%)
  blocking collectives  21.9 us (7%)
  matrix products  15.6 us (5%)
  other arithmetic  15.4 us (5%)
  between operations  13.5 us (4%)
  local copies, waits for them, and re-layouts  4.44 us (1%)
    all_gather x1, waiting for transfers between devices, on_device(): piece = lax.all_gather(codes, 'shard', axis=1, tiled=True)  227 us
    all_gather x1, waiting for transfers between devices, on_device(): kv_piece = lax.all_gather(keyval, 'shard', axis=0, tiled=True)  21.7 us
    all_gather x1, blocking collectives, on_device(): seg_piece = lax.all_gather(segment_ids, 'shard', axis=0, tiled=True)  17.1 us
    convert_element_type x1, other arithmetic, on_device(): weight = blocked.reshape(piece.shape[0], width).astype(jnp.bfloat16)  9.92 us
  transfers between devices with their start and end apart: 2, of which 2 were waited for; matrix products, arithmetic and copies ran while one was open for 0% of the time, Pallas kernels for 0%

commit v1 on v0

v1 whole, which is shorter than its diff:
```python
import functools
import math

import jax
import jax.numpy as jnp
from jax import lax
from jax.experimental import pallas as pl
from jax.experimental.pallas import tpu as pltpu
from jax.sharding import Mesh
from jax.sharding import PartitionSpec as P

KVH = 4
HD = 128
QPK = 16
BLK = 128
KVW = 1024
PAD = 16
ALL = ("groups", "hi", "lo", "tensor")
BLOCK = ("groups", "lo")
SHARD = ("hi", "lo")
VMEM_LIMIT = 56 * 2**20


def flat_pairs(sizes, move):
    groups, shards, cores = sizes
    pairs = []
    for g in range(groups):
        for s in range(shards):
            for c in range(cores):
                to = move(g, s, c)
                if to is not None:
                    pairs.append(((g * shards + s) * cores + c, (to[0] * shards + to[1]) * cores + to[2]))
    return pairs


def turns_of(sizes, low, depth):
    if (sizes[0], low) != (2, 4) or depth % 128 or depth < 384:
        return None
    first = 128 * ((depth // 128 + 2) // 3)
    turns, start = [], 0
    for turn, width in enumerate((first, first, depth - 2 * first)):
        turns.append((start, width, tuple((turn + step) % 3 for step in range(3))))
        start += 8 * width
    return turns


def slice_index(place, axes):
    return place[axes[0]] * 4 + place[axes[1]] * 2 + place[axes[2]]


def scale_kernel(turns, place_ref, codes_ref, scales_ref, ids_ref, out_ref):
    lows = 4
    for lo in range(lows):
        place, at = (place_ref[0], lo // 2, lo % 2), 0
        for start, width, axes in turns:
            first = start + slice_index(place, axes) * width
            for k in range(width // BLK):
                row = pl.multiple_of(first + k * BLK, BLK)
                scale = scales_ref[row // BLK, place_ref[4]]
                block = codes_ref[pl.ds(row, BLK), :].astype(jnp.float32) * scale
                block = block.astype(jnp.bfloat16)
                for copy in range(lo, out_ref.shape[0], lows):
                    out_ref[copy, at : at + BLK, :] = block
                at += BLK
        for copy in range(lo, out_ref.shape[0], lows):
            out_ref[copy, at:, :] = ids_ref[...]


def scaled_weight(turns, place, low, shards, codes, scales, ids):
    group, column = place[0], place[4]
    width = codes.shape[1]
    if turns is not None and width == BLK:
        depth = sum(turn[1] for turn in turns)
        return pl.pallas_call(
            functools.partial(scale_kernel, turns),
            in_specs=[
                pl.BlockSpec(memory_space=pltpu.SMEM),
                pl.BlockSpec(memory_space=pltpu.VMEM),
                pl.BlockSpec(memory_space=pltpu.SMEM),
                pl.BlockSpec(memory_space=pltpu.VMEM),
            ],
            out_specs=pl.BlockSpec(memory_space=pltpu.VMEM),
            out_shape=jax.ShapeDtypeStruct((shards, depth + PAD, width), jnp.bfloat16),
            compiler_params=pltpu.CompilerParams(vmem_limit_bytes=VMEM_LIMIT),
            name="scale",
        )(place, codes, scales, ids)
    features = codes.shape[0]
    groups = lax.axis_size("groups")
    depth = features // (groups * low)
    if turns is not None:
        rows = []
        for lo in range(low):
            for start, size, axes in turns:
                first = start + slice_index((group, lo // 2, lo % 2), axes) * size
                rows.append(first + jnp.arange(size, dtype=jnp.int32))
        rows = jnp.concatenate(rows)
    else:
        rows = group * low * depth + jnp.arange(low * depth, dtype=jnp.int32)
    scale = lax.dynamic_slice_in_dim(scales, column, 1, 1)[rows // BLK]
    weight = (codes[rows].astype(jnp.float32) * scale).astype(jnp.bfloat16)
    weight = weight.reshape(low, depth, width)
    weight = jnp.concatenate([weight, jnp.broadcast_to(ids, (low, PAD, width))], axis=1)
    weight = jnp.broadcast_to(weight[None], (shards // low, low, depth + PAD, width))
    return weight.reshape(shards, depth + PAD, width)


def spread_hidden(turns, place, sizes, low, hidden):
    members = sizes[0] * low
    rows, features = hidden.shape
    depth = features // members
    if turns is None:
        sliced = jnp.moveaxis(hidden.reshape(rows, members, depth), 1, 0)
        got = lax.all_to_all(sliced, BLOCK, 0, 0, tiled=True).reshape(members * rows, depth)
        return [got], [(0, m * rows, None, depth, m, 0) for m in range(members)]
    moves = (
        lambda g, s, c: (1 - g, s, c),
        lambda g, s, c: (g, s ^ 2, c),
        lambda g, s, c: (g, s ^ 1, c),
    )
    bits = (4, 2, 1)
    states = []
    for start, width, axes in turns:
        states.append([(hidden, start, [0])])
    for step in range(3):
        for (start, width, axes), state in zip(turns, states):
            axis = axes[step]
            size = width * (4 >> step)
            here = place[axis]
            sends = [
                lax.dynamic_slice_in_dim(array, first + (1 - here) * size, size, 1)
                for array, first, _ in state
            ]
            got = lax.ppermute(
                jnp.concatenate(sends, axis=0) if len(sends) > 1 else sends[0],
                ALL,
                flat_pairs(sizes, moves[axis]),
            )
            distances = [b | bits[axis] for _, _, held in state for b in held]
            state[:] = [(array, first + here * size, held) for array, first, held in state]
            state.append((got, 0, distances))
    arrays, copies, column = [hidden], [], 0
    for (start, width, axes), state in zip(turns, states):
        for array, first, held in state:
            if array is not hidden:
                arrays.append(array)
            at = 0 if array is hidden else len(arrays) - 1
            for k, distance in enumerate(held):
                copies.append((at, k * rows, first, width, distance, column))
        column += width
    return arrays, copies


def project_kernel(copies, sources, wide, firsts_ref, place_ref, *refs):
    hidden_refs, (weight_ref, other_ref, mine_ref, left, halves, sems) = refs[:sources], refs[sources:]
    step = pl.program_id(0)
    rows = mine_ref.shape[1]
    depth, columns = halves.shape[1:]
    core, member = place_ref[3], place_ref[5]

    @pl.when(step == 0)
    def _():
        started = []
        for k, (at, row, _, width, distance, column) in enumerate(copies):
            first = pl.multiple_of(firsts_ref[k], 128)
            block = distance if wide else jnp.bitwise_xor(member, distance)
            to = pl.multiple_of(block * rows, rows)
            started.append(
                pltpu.make_async_copy(
                    hidden_refs[at].at[pl.ds(row, rows), pl.ds(first, width)],
                    left.at[pl.ds(to, rows), pl.ds(column, width)],
                    sems.at[k],
                )
            )
        shards = weight_ref.shape[0]
        width = weight_ref.shape[2]
        for s in range(shards):
            half = jnp.bitwise_xor(core, s * width // columns)
            started.append(
                pltpu.make_async_copy(
                    weight_ref.at[s, pl.ds(0, depth), :],
                    halves.at[half, :, pl.ds(s * width % columns, width)],
                    sems.at[len(copies) + s],
                )
            )
        for copy in started:
            copy.start()
        for copy in started:
            copy.wait()

    size = mine_ref.shape[2]
    per_half = columns // size
    for half, out_ref in ((1, other_ref), (0, mine_ref)):
        for k in range(per_half):

            @pl.when(step == (1 - half) * per_half + k)
            def _():
                total = jnp.dot(
                    left[...],
                    halves[half, :, k * size : (k + 1) * size],
                    preferred_element_type=jnp.float32,
                )
                out_ref[...] = total.reshape(out_ref.shape)


def project(turns, arrays, copies, weight, place):
    members = max(copy[4] for copy in copies) + 1
    rows = arrays[0].shape[0] if turns is not None else arrays[0].shape[0] // members
    shards, deep, width = weight.shape
    depth = deep - PAD
    columns = shards * width // 2
    if width % 128:
        weight = jnp.moveaxis(weight[:, :depth].reshape(2, shards // 2, depth, width), 1, 2)
        weight = weight.reshape(2, depth, columns)
    firsts = jnp.stack([jnp.asarray(0 if c[2] is None else c[2], jnp.int32) for c in copies])
    size = 256
    per_half = columns // size
    out = jax.ShapeDtypeStruct((members, rows, columns), jnp.float32)
    return pl.pallas_call(
        functools.partial(project_kernel, copies, len(arrays), turns is None),
        grid_spec=pltpu.PrefetchScalarGridSpec(
            num_scalar_prefetch=2,
            grid=(2 * per_half,),
            in_specs=[pl.BlockSpec(memory_space=pl.ANY)] * (len(arrays) + 1),
            out_specs=[
                pl.BlockSpec((members, rows, size), lambda i, f, p: (0, 0, jnp.minimum(i, per_half - 1))),
                pl.BlockSpec((members, rows, size), lambda i, f, p: (0, 0, jnp.maximum(i - per_half, 0))),
            ],
            scratch_shapes=[
                pltpu.VMEM((members * rows, depth), jnp.bfloat16),
                pltpu.VMEM((2, depth, columns), jnp.bfloat16),
                pltpu.SemaphoreType.DMA((len(copies) + weight.shape[0],)),
            ],
        ),
        out_shape=[out, out],
        compiler_params=pltpu.CompilerParams(vmem_limit_bytes=VMEM_LIMIT),
        name="project",
    )(firsts, place, *arrays, weight)


def split_kernel(mine_ref, got_ref, out_ref):
    total = mine_ref[...] + got_ref[...]
    columns = total.shape[2]
    out_ref[:, :, :columns] = total.astype(jnp.bfloat16)
    for head in range(columns // (2 * HD)):
        keys = total[:, :, 2 * head * HD : (2 * head + 1) * HD]
        rest = keys - keys.astype(jnp.bfloat16).astype(jnp.float32)
        at = columns + head * HD
        out_ref[:, :, at : at + HD] = rest.astype(jnp.bfloat16)


def split(mine, got):
    members, rows, columns = mine.shape
    spec = pl.BlockSpec((2, rows, columns), lambda i: (i, 0, 0))
    wide = columns + columns // 2
    return pl.pallas_call(
        split_kernel,
        grid=(members // 2,),
        in_specs=[spec, spec],
        out_specs=pl.BlockSpec((2, rows, wide), lambda i: (i, 0, 0)),
        out_shape=jax.ShapeDtypeStruct((members, rows, wide), jnp.bfloat16),
        compiler_params=pltpu.CompilerParams(vmem_limit_bytes=VMEM_LIMIT),
        name="split",
    )(mine, got)


def attend_kernel(pieces, heads, stack, query_ref, allowed_ref, *refs):
    kv_refs, (out_ref, keys, values) = refs[:pieces], refs[pieces:]
    rows = query_ref.shape[0]
    scaling = 1.0 / math.sqrt(HD)
    for d, ref in enumerate(kv_refs):
        keys[d * rows : (d + 1) * rows, :] = ref[:, :HD]
        values[d * rows : (d + 1) * rows, :] = ref[:, HD:]
    allowed = allowed_ref[...]
    allowed = jnp.concatenate([allowed] * stack, axis=0) > 0.0
    for part in range(heads // stack):
        columns = [slice((part * stack + h) * HD, (part * stack + h + 1) * HD) for h in range(stack)]
        query = jnp.concatenate([query_ref[:, c] for c in columns], axis=0)
        scores = lax.dot_general(
            query, keys[...], (((1,), (1,)), ((), ())), preferred_element_type=jnp.float32
        )
        scores = jnp.where(allowed, scores * scaling, -jnp.inf)
        weights = jnp.exp(scores - jnp.max(scores, axis=1, keepdims=True))
        totals = jnp.sum(weights, axis=1, keepdims=True)
        result = jnp.dot(
            weights.astype(jnp.bfloat16), values[...], preferred_element_type=jnp.float32
        )
        result = (result / totals).astype(jnp.bfloat16)
        for h, c in enumerate(columns):
            out_ref[:, c] = result[h * rows : (h + 1) * rows]


def attend(queries, allowed, pieces):
    rows, width = queries.shape
    window = allowed.shape[1]
    group = QPK * HD
    stack = 4 if window <= 1024 else 1
    return pl.pallas_call(
        functools.partial(attend_kernel, len(pieces), QPK, stack),
        grid=(width // group,),
        in_specs=[
            pl.BlockSpec((rows, group), lambda i: (0, i)),
            pl.BlockSpec((rows, window), lambda i: (0, 0)),
        ]
        + [pl.BlockSpec((rows, 2 * HD), lambda i: (0, i))] * len(pieces),
        out_specs=pl.BlockSpec((rows, group), lambda i: (0, i)),
        out_shape=jax.ShapeDtypeStruct((rows, width), jnp.bfloat16),
        scratch_shapes=[pltpu.VMEM((window, HD), jnp.bfloat16)] * 2,
        compiler_params=pltpu.CompilerParams(vmem_limit_bytes=VMEM_LIMIT),
        name="attend",
    )(queries, allowed, *pieces)


def on_device(sizes, low, hidden, codes, scales, queries, segment_ids):
    groups, shards, cores = sizes
    rows = hidden.shape[0]
    features, width = codes.shape
    members = groups * low
    depth = features // members
    group = lax.axis_index("groups")
    lo = lax.axis_index("lo")
    shard = lax.axis_index("hi") * low + lo
    core = lax.axis_index("tensor")

    turns = turns_of(sizes, low, depth)
    place = (group, lo // 2, lo % 2, core, (shard * width) // BLK, group * low + lo)
    table = jnp.stack([jnp.asarray(p, jnp.int32) for p in place])

    ids = segment_ids.astype(jnp.bfloat16).reshape(rows // width, width)
    ids = jnp.pad(ids, ((0, PAD - rows // width), (0, 0)))
    weight = scaled_weight(turns, table, low, shards, codes, scales, ids)
    weight = lax.all_to_all(weight, SHARD, 0, 0, tiled=True)

    arrays, copies = spread_hidden(turns, place, sizes, low, hidden)
    other, mine = project(turns, arrays, copies, weight, table)
    swap = flat_pairs(sizes, lambda g, s, c: (g, s, 1 - c))
    partial = split(mine, lax.ppermute(other, ALL, swap))
    partial = lax.all_to_all(partial, BLOCK, 0, 0, tiled=True)
    total = jnp.sum(partial.astype(jnp.float32), axis=0)
    columns = mine.shape[2]
    rest = total[:, columns:].reshape(rows, -1, 1, HD)
    rest = jnp.concatenate([rest, jnp.zeros_like(rest)], axis=2).reshape(rows, columns)
    keyval = (total[:, :columns] + rest).astype(jnp.bfloat16)

    back = min(shards // 2 + 1, shards - 1)
    known = weight[:, depth : depth + rows // width, :].reshape(shards, rows)
    from_shard = shard - jnp.arange(back + 1, dtype=jnp.int32)
    seen = known[jnp.maximum(from_shard, 0)].reshape(-1)
    offset = jnp.arange(rows, dtype=jnp.int32)
    keypos = (from_shard[:, None] * rows + offset[None, :]).reshape(-1)
    rowpos = shard * rows + offset
    allowed = (
        (segment_ids.astype(jnp.bfloat16)[:, None] == seen[None, :])
        & (keypos[None, :] <= rowpos[:, None])
        & (keypos[None, :] >= 0)
    ).astype(jnp.float32)

    pieces = [keyval]
    for d in range(1, back + 1):
        up = flat_pairs(sizes, lambda g, s, c: (g, s + d, c) if s + d < shards else None)
        pieces.append(lax.ppermute(keyval, ALL, up))
    return attend(queries, allowed, pieces)


def solution(mesh):
    sizes = tuple(mesh.shape[name] for name in ("groups", "shard", "tensor"))
    groups, shards, cores = sizes
    low = math.gcd(shards, 4)
    fine = Mesh(mesh.devices.reshape(groups, shards // low, low, cores), ALL)
    tokens = ("groups", "hi", "lo")
    in_specs = (
        P(tokens, "tensor"),
        P("tensor", ("hi", "lo")),
        P("tensor", None),
        P(tokens, "tensor"),
        P(tokens),
    )
    return jax.shard_map(
        functools.partial(on_device, sizes, low),
        mesh=fine,
        in_specs=in_specs,
        out_specs=P(tokens, "tensor"),
        check_vma=False,
    )
```

time: 325 us -> 159 us (0.49); the launches traced: 320 us -> 158 us
  waiting for transfers between devices: 249 us -> 83.3 us
  starting transfers between devices: 0.04 us -> 27.3 us
  Pallas kernels: 0 us -> 23.5 us
  blocking collectives: 21.9 us -> 0 us
  matrix products: 15.6 us -> 0 us
  local copies, waits for them, and re-layouts: 4.44 us -> 18.5 us
  between operations: 13.5 us -> 0.38 us
  other arithmetic: 15.4 us -> 4.76 us
    all_gather x2 -> x0, waiting for transfers between devices: 249 us -> none  [the longest x1 227 us: on_device(): piece = lax.all_gather(codes, 'shard', axis=1, tiled=True)]
    ppermute x0 -> x15, waiting for transfers between devices: none -> 65.7 us  [the longest x9 41.3 us: spread_hidden(): lax.ppermute(jnp.concatenate(sends, axis=0) if len(sends) > 1 else sends[...]
    pallas_call x0 -> x4, Pallas kernels: none -> 23.5 us  [the longest x1 8.26 us: attend(): pl.pallas_call(functools.partial(attend_kernel, len(pieces), QPK, stack),...]
    all_to_all x0 -> x2, waiting for transfers between devices: none -> 17.6 us  [the longest x1 17.6 us: on_device(): partial = lax.all_to_all(partial, BLOCK, 0, 0, tiled=True)]
    all_gather x1 -> x0, blocking collectives: 17.1 us -> none  [on_device(): seg_piece = lax.all_gather(segment_ids, 'shard', axis=0, tiled=True)]
    ppermute x0 -> x15, starting transfers between devices: none -> 16.2 us  [the longest x9 9.67 us: spread_hidden(): lax.ppermute(jnp.concatenate(sends, axis=0) if len(sends) > 1 else sends[...]
    dot_general x6 -> x0, matrix products: 15.6 us -> none  [the longest x2 5.44 us: compute(): jnp.einsum('qph,kh->pqk', query_local[:, group], split_kv[:, group, 0], p...]
    all_to_all x0 -> x2, starting transfers between devices: none -> 11.1 us  [the longest x1 6 us: on_device(): weight = lax.all_to_all(weight, SHARD, 0, 0, tiled=True)]
  transfers between devices with their start and end apart: 2 -> 17, of which waited for: 2 -> 11; matrix products, arithmetic and copies ran while one was open for 0% -> 10% of each run, Pallas kernels for 0% -> 0%
where the time goes in v1:
time: 159 us; the launch traced here: 158 us
  waiting for transfers between devices  83.3 us (52%)
  starting transfers between devices  27.3 us (17%)
  Pallas kernels  23.5 us (15%)
  local copies, waits for them, and re-layouts  18.5 us (12%)
  other arithmetic  4.76 us (3%)
    ppermute x9, waiting for transfers between devices, spread_hidden(): lax.ppermute(jnp.concatenate(sends, axis=0) if len(sends) > 1 else sends[...  41.3 us
    ppermute x5, waiting for transfers between devices, on_device(): pieces.append(lax.ppermute(keyval, ALL, up))  20 us
    all_to_all x1, waiting for transfers between devices, on_device(): partial = lax.all_to_all(partial, BLOCK, 0, 0, tiled=True)  17.6 us
    ppermute x9, starting transfers between devices, spread_hidden(): lax.ppermute(jnp.concatenate(sends, axis=0) if len(sends) > 1 else sends[...  9.67 us
    dynamic_slice x15, local copies, waits for them, and re-layouts, spread_hidden(): lax.dynamic_slice_in_dim(array, first + (1 - here) * size, size, 1)  9.63 us
    pallas_call x1, Pallas kernels, attend(): pl.pallas_call(functools.partial(attend_kernel, len(pieces), QPK, stack),...  8.26 us
    pallas_call x1, Pallas kernels, project(): pl.pallas_call(functools.partial(project_kernel, copies, len(arrays), tur...  7.92 us
    ppermute x5, starting transfers between devices, on_device(): pieces.append(lax.ppermute(keyval, ALL, up))  6.46 us
  transfers between devices with their start and end apart: 17, of which 11 were waited for; matrix products, arithmetic and copies ran while one was open for 10% of the time, Pallas kernels for 0%

profile of v1, /device:TPU:28, one launch (start us, length us, event | category | flops | bytes accessed | tf_op | source)
XLA Modules:
  0.0 157.8 jit_solution(18069552504983445550)
XLA Ops:
  0.7 1.4 copy.8.scales_ref
  3.2 3.2 %scale.1 = bf16[8,1040,128]{2,1,0:T(8,128)(2,1)} custom-call(s32[6]{0:T(128)} %stack.60.place_ref, bf16[8192,128]{1,0:T(8,128)(2,1)} %codes_ref.1, f32[64,8]{1,0:T(8,128)} %copy.8.scales_ref, bf16[16,128]{1,0:T(8,128)(2,1)} %pad.5.ids_ref), custom_call_target="tpu_custom_call" | custom-call | tf_op jit(solution)/shard_map/scale/pallas_call | solution.py:74
  6.4 6.0 %all-to-all-start = ((bf16[8,1040,128]{2,1,0:T(8,128)(2,1)}), bf16[8,1040,128]{2,1,0:T(8,128)(2,1)S(1)}, u32[]{:S(2)}, u32[]{:S(2)}) async-start(bf16[8,1040,128]{2,1,0:T(8,128)(2,1)} %scale.1), calls=%async_computation | async-start | bytes 4259840 | tf_op jit(solution)/shard_map/all_to_all | solution.py:331
  12.4 2.1 %constant_dynamic-slice_fusion.11 = (bf16[128,1536]{1,0:T(8,128)(2,1)}, bf16[128,1536]{1,0:T(8,128)(2,1)}) fusion(bf16[128,8192]{1,0:T(8,128)(2,1)} %refs_0_.1, s32[]{:T(128)S(6)} %select_n.78, s32[]{:T(128)S(6)} %select_n.72), kind=kLoop, calls=%fused_computation.22 | loop fusion | bytes 1572872 | tf_op jit(solution)/shard_map/dynamic_slice | solution.py:130
  14.5 1.5 collective-permute-start
  16.5 1.7 %constant_dynamic-slice_fusion.5 = bf16[128,1024]{1,0:T(8,128)(2,1)} fusion(bf16[128,8192]{1,0:T(8,128)(2,1)} %refs_0_.1, s32[]{:T(128)S(6)} %select_n.84), kind=kLoop, calls=%fused_computation.16 | loop fusion | bytes 524292 | tf_op jit(solution)/shard_map/dynamic_slice | solution.py:130
  18.7 1.7 %constant_dynamic-slice_fusion.8 = (bf16[128,384]{1,0:T(8,128)(2,1)}, bf16[128,384]{1,0:T(8,128)(2,1)}) fusion(bf16[128,8192]{1,0:T(8,128)(2,1)} %refs_0_.1, s32[]{:T(128)S(6)} %select_n.81, s32[]{:T(128)S(6)} %select_n.75), kind=kLoop, calls=%fused_computation.19 | loop fusion | bytes 393224 | tf_op jit(solution)/shard_map/dynamic_slice | solution.py:130
  21.4 1.7 %constant_dynamic-slice_fusion.10 = (bf16[128,768]{1,0:T(8,128)(2,1)S(1)}, bf16[128,768]{1,0:T(8,128)(2,1)}) fusion(bf16[128,8192]{1,0:T(8,128)(2,1)} %refs_0_.1, s32[]{:T(128)S(6)} %select_n.79, s32[]{:T(128)S(6)} %select_n.73), kind=kLoop, calls=%fused_computation.21 | loop fusion | bytes 786440 | tf_op jit(solution)/shard_map/dynamic_slice | solution.py:130
  23.1 1.5 constant_dynamic-slice_fusion.2
  24.6 11.2 %collective-permute-done.6.refs_7_ = bf16[128,1024]{1,0:T(8,128)(2,1)S(1)} collective-permute-done((bf16[128,1024]{1,0:T(8,128)(2,1)}, bf16[128,1024]{1,0:T(8,128)(2,1)S(1)}, u32[]{:S(2)}, u32[]{:S(2)}) %collective-permute-start.6) | collective-permute-done | bytes 262176 | tf_op jit(solution)/shard_map/ppermute | solution.py:133
  35.8 1.6 collective-permute-start.7
  39.7 16.9 %collective-permute-done.3.refs_4_ = bf16[128,1536]{1,0:T(8,128)(2,1)S(1)} collective-permute-done((bf16[128,1536]{1,0:T(8,128)(2,1)}, bf16[128,1536]{1,0:T(8,128)(2,1)S(1)}, u32[]{:S(2)}, u32[]{:S(2)}) %collective-permute-start.3) | collective-permute-done | bytes 393248 | tf_op jit(solution)/shard_map/ppermute | solution.py:133
  57.3 7.1 %collective-permute-done.1.refs_2_ = bf16[256,768]{1,0:T(8,128)(2,1)S(1)} collective-permute-done((bf16[256,768]{1,0:T(8,128)(2,1)S(1)}, bf16[256,768]{1,0:T(8,128)(2,1)S(1)}, u32[]{:S(2)}, u32[]{:S(2)}) %collective-permute-start.1) | collective-permute-done | bytes 393248 | tf_op jit(solution)/shard_map/ppermute | solution.py:133
  65.7 1.6 collective-permute-start.5
  68.1 1.8 %collective-permute-start.8 = (bf16[512,256]{1,0:T(8,128)(2,1)}, bf16[512,256]{1,0:T(8,128)(2,1)S(1)}, u32[]{:S(2)}, u32[]{:S(2)}) collective-permute-start(bf16[512,256]{1,0:T(8,128)(2,1)} %pad_maximum_fusion.5), channel_id=1, source_target_pairs={{0,4},{1,5},{2,6},{3,7},{4,0},{5,1},{6,2},{7,3},{8,12},{9,13},{10,... | collective-permute-start | bytes 786440 | tf_op jit(solution)/shard_map/ppermute | solution.py:133
  70.5 5.4 %collective-permute-done.8.refs_9_ = bf16[512,256]{1,0:T(8,128)(2,1)S(1)} collective-permute-done((bf16[512,256]{1,0:T(8,128)(2,1)}, bf16[512,256]{1,0:T(8,128)(2,1)S(1)}, u32[]{:S(2)}, u32[]{:S(2)}) %collective-permute-start.8) | collective-permute-done | bytes 262176 | tf_op jit(solution)/shard_map/ppermute | solution.py:133
  76.7 1.4 copy-done
  78.0 7.9 %project.1 = (f32[8,128,512]{2,1,0:T(8,128)}, f32[8,128,512]{2,1,0:T(8,128)}) custom-call(s32[24]{0:T(128)} %stack.70.firsts_ref, s32[6]{0:T(128)} %stack.60.place_ref, bf16[128,8192]{1,0:T(8,128)(2,1)} %refs_0_.1, bf16[128,1536]{1,0:T(8,128)(2,1)} %copy-done.2, bf16[256,768]{1,0:T(8,128)(2,1)} %copy-done.4, ...), custom_call_target="tpu_custom_call" | custom-call | tf_op jit(solution)/shard_map/project/pallas_call | solution.py:218
  86.0 4.4 %collective-permute-done.9.got_ref = f32[8,128,512]{2,1,0:T(8,128)S(1)} collective-permute-done((f32[8,128,512]{2,1,0:T(8,128)}, f32[8,128,512]{2,1,0:T(8,128)S(1)}, u32[]{:S(2)}, u32[]{:S(2)}) %collective-permute-start.9) | collective-permute-done | bytes 2097184 | tf_op jit(solution)/shard_map/ppermute | solution.py:336
  90.4 1.4 copy-done.1
  91.8 4.2 %split.1 = bf16[8,128,768]{2,1,0:T(8,128)(2,1)} custom-call(f32[8,128,512]{2,1,0:T(8,128)} %get-tuple-element.7.mine_ref, f32[8,128,512]{2,1,0:T(8,128)} %copy-done.1), custom_call_target="tpu_custom_call" | custom-call | tf_op jit(solution)/shard_map/split/pallas_call | solution.py:255
  95.9 5.1 %all-to-all-start.1 = ((bf16[8,128,768]{2,1,0:T(8,128)(2,1)}), bf16[8,128,768]{2,1,0:T(8,128)(2,1)S(1)}, u32[]{:S(2)}, u32[]{:S(2)}) async-start(bf16[8,128,768]{2,1,0:T(8,128)(2,1)} %split.1), calls=%async_computation.1 | async-start | bytes 3145728 | tf_op jit(solution)/shard_map/all_to_all | solution.py:337
  102.5 17.6 %all-to-all-done.1 = bf16[8,128,768]{2,1,0:T(8,128)(2,1)S(1)} async-done(((bf16[8,128,768]{2,1,0:T(8,128)(2,1)}), bf16[8,128,768]{2,1,0:T(8,128)(2,1)S(1)}, u32[]{:S(2)}, u32[]{:S(2)}) %all-to-all-start.1) | async-done | bytes 1572896 | tf_op jit(solution)/shard_map/all_to_all | solution.py:337
  120.8 1.3 collective-permute-start.10
  122.1 1.3 collective-permute-start.11
  123.4 1.3 collective-permute-start.12
  124.7 1.3 collective-permute-start.13
  128.2 1.6 collective-permute-done.10.refs_1_
  129.7 4.5 %collective-permute-done.11.refs_2_ = bf16[128,512]{1,0:T(8,128)(2,1)S(1)} collective-permute-done((bf16[128,512]{1,0:T(8,128)(2,1)S(1)}, bf16[128,512]{1,0:T(8,128)(2,1)S(1)}, u32[]{:S(2)}, u32[]{:S(2)}) %collective-permute-start.11) | collective-permute-done | bytes 131104 | tf_op jit(solution)/shard_map/ppermute | solution.py:360
  134.2 1.5 collective-permute-done.12.refs_3_
  135.7 12.5 %collective-permute-done.13.refs_4_ = bf16[128,512]{1,0:T(8,128)(2,1)S(1)} collective-permute-done((bf16[128,512]{1,0:T(8,128)(2,1)S(1)}, bf16[128,512]{1,0:T(8,128)(2,1)S(1)}, u32[]{:S(2)}, u32[]{:S(2)}) %collective-permute-start.13) | collective-permute-done | bytes 131104 | tf_op jit(solution)/shard_map/ppermute | solution.py:360
  149.5 8.3 %attend.1 = bf16[128,4096]{1,0:T(8,128)(2,1)} custom-call(bf16[128,4096]{1,0:T(8,128)(2,1)} %query_ref.1, f32[128,768]{1,0:T(8,128)} %and_convert_fusion.allowed_ref, bf16[128,512]{1,0:T(8,128)(2,1)} %copy-done.8, bf16[128,512]{1,0:T(8,128)(2,1)} %copy-done.13, bf16[128,512]{1,0:T(8,128)(2,1)} %copy-done.14, bf16[128,512]{1,0:T(8,128)(2,1)} %copy-done.15, ...), custom_call_target="tpu_custom_call" | custom-call | tf_op jit(solution)/shard_map/attend/pallas_call | solution.py:297
  (85 shorter events, 15.9 us)
Async XLA Ops:
  6.4 70.2 %all-to-all-start = ((bf16[8,1040,128]{2,1,0:T(8,128)(2,1)}), bf16[8,1040,128]{2,1,0:T(8,128)(2,1)S(1)}, u32[]{:S(2)}, u32[]{:S(2)}) async-start(bf16[8,1040,128]{2,1,0:T(8,128)(2,1)} %scale.1), calls=%async_computation | async-start | bytes 4259840 | tf_op jit(solution)/shard_map/all_to_all | solution.py:331
  14.5 22.9 %collective-permute-start = (bf16[128,1536]{1,0:T(8,128)(2,1)}, bf16[128,1536]{1,0:T(8,128)(2,1)S(1)}, u32[]{:S(2)}, u32[]{:S(2)}) collective-permute-start(bf16[128,1536]{1,0:T(8,128)(2,1)} %get-tuple-element.14), channel_id=1, source_target_pairs={{0,16},{1,17},{2,18},{3,19},{4,20},{5,21},{6,22},{7,23},{8,24},{9,... | collective-permute-start | bytes 1179656 | tf_op jit(solution)/shard_map/ppermute | solution.py:133
  16.0 40.6 %collective-permute-start.3 = (bf16[128,1536]{1,0:T(8,128)(2,1)}, bf16[128,1536]{1,0:T(8,128)(2,1)S(1)}, u32[]{:S(2)}, u32[]{:S(2)}) collective-permute-start(bf16[128,1536]{1,0:T(8,128)(2,1)} %get-tuple-element.13), channel_id=1, source_target_pairs={{0,4},{1,5},{2,6},{3,7},{4,0},{5,1},{6,2},{7,3},{8,12},{9,13},{10,... | collective-permute-start | bytes 1179656 | tf_op jit(solution)/shard_map/ppermute | solution.py:133
  18.2 17.6 %collective-permute-start.6 = (bf16[128,1024]{1,0:T(8,128)(2,1)}, bf16[128,1024]{1,0:T(8,128)(2,1)S(1)}, u32[]{:S(2)}, u32[]{:S(2)}) collective-permute-start(bf16[128,1024]{1,0:T(8,128)(2,1)} %constant_dynamic-slice_fusion.5), channel_id=1, source_target_pairs={{0,2},{1,3},{2,0},{3,1},{4,6},{5,7},{6,4},{7,5},{8,10},{9,11},{10,... | collective-permute-start | bytes 786440 | tf_op jit(solution)/shard_map/ppermute | solution.py:133
  24.6 39.9 %copy-start.10 = (bf16[128,384]{1,0:T(8,128)(2,1)S(1)}, bf16[128,384]{1,0:T(8,128)(2,1)}, u32[]{:S(2)}) copy-start(bf16[128,384]{1,0:T(8,128)(2,1)} %get-tuple-element.10) | copy-start | bytes 294916
  35.7 1.7 %copy-start.6 = (bf16[128,1024]{1,0:T(8,128)(2,1)}, bf16[128,1024]{1,0:T(8,128)(2,1)S(1)}, u32[]{:S(2)}) copy-start(bf16[128,1024]{1,0:T(8,128)(2,1)S(1)} %collective-permute-done.6.refs_7_) | copy-start | bytes 786436
  35.8 31.5 %collective-permute-start.7 = (bf16[256,512]{1,0:T(8,128)(2,1)S(1)}, bf16[256,512]{1,0:T(8,128)(2,1)S(1)}, u32[]{:S(2)}, u32[]{:S(2)}) collective-permute-start(bf16[256,512]{1,0:T(8,128)(2,1)S(1)} %pad_maximum_fusion.4), channel_id=1, source_target_pairs={{0,16},{1,17},{2,18},{3,19},{4,20},{5,21},{6,22},{7,23},{8,24},{9,... | collective-permute-start | bytes 786440 | tf_op jit(solution)/shard_map/ppermute | solution.py:133
  37.4 28.3 %copy-start.9 = (bf16[128,384]{1,0:T(8,128)(2,1)S(1)}, bf16[128,384]{1,0:T(8,128)(2,1)}, u32[]{:S(2)}) copy-start(bf16[128,384]{1,0:T(8,128)(2,1)} %get-tuple-element.9) | copy-start | bytes 294916
  37.4 28.3 %copy-start.2 = (bf16[128,1536]{1,0:T(8,128)(2,1)}, bf16[128,1536]{1,0:T(8,128)(2,1)S(1)}, u32[]{:S(2)}) copy-start(bf16[128,1536]{1,0:T(8,128)(2,1)S(1)} %collective-permute-done.refs_1_) | copy-start | bytes 1179652
  38.5 28.8 %copy-start.12 = (bf16[128,256]{1,0:T(8,128)(2,1)S(1)}, bf16[128,256]{1,0:T(8,128)(2,1)}, u32[]{:S(2)}) copy-start(bf16[128,256]{1,0:T(8,128)(2,1)} %constant_dynamic-slice_fusion.2) | copy-start | bytes 196612
  38.5 25.9 %collective-permute-start.1 = (bf16[256,768]{1,0:T(8,128)(2,1)S(1)}, bf16[256,768]{1,0:T(8,128)(2,1)S(1)}, u32[]{:S(2)}, u32[]{:S(2)}) collective-permute-start(bf16[256,768]{1,0:T(8,128)(2,1)S(1)} %pad_maximum_fusion), channel_id=1, source_target_pairs={{0,4},{1,5},{2,6},{3,7},{4,0},{5,1},{6,2},{7,3},{8,12},{9,13},{10,... | collective-permute-start | bytes 1179656 | tf_op jit(solution)/shard_map/ppermute | solution.py:133
  56.6 10.7 %copy-start.3 = (bf16[128,1536]{1,0:T(8,128)(2,1)}, bf16[128,1536]{1,0:T(8,128)(2,1)S(1)}, u32[]{:S(2)}) copy-start(bf16[128,1536]{1,0:T(8,128)(2,1)S(1)} %collective-permute-done.3.refs_4_) | copy-start | bytes 1179652
  56.7 8.9 %collective-permute-start.4 = (bf16[256,768]{1,0:T(8,128)(2,1)S(1)}, bf16[256,768]{1,0:T(8,128)(2,1)S(1)}, u32[]{:S(2)}, u32[]{:S(2)}) collective-permute-start(bf16[256,768]{1,0:T(8,128)(2,1)S(1)} %pad_maximum_fusion.2), channel_id=1, source_target_pairs={{0,2},{1,3},{2,0},{3,1},{4,6},{5,7},{6,4},{7,5},{8,10},{9,11},{10,... | collective-permute-start | bytes 1179656 | tf_op jit(solution)/shard_map/ppermute | solution.py:133
  64.4 12.2 %copy-start.4 = (bf16[256,768]{1,0:T(8,128)(2,1)}, bf16[256,768]{1,0:T(8,128)(2,1)S(1)}, u32[]{:S(2)}) copy-start(bf16[256,768]{1,0:T(8,128)(2,1)S(1)} %collective-permute-done.1.refs_2_) | copy-start | bytes 1179652
  65.3 10.6 %collective-permute-start.2 = (bf16[512,384]{1,0:T(8,128)(2,1)}, bf16[512,384]{1,0:T(8,128)(2,1)}, u32[]{:S(2)}, u32[]{:S(2)}) collective-permute-start(bf16[512,384]{1,0:T(8,128)(2,1)} %pad_maximum_fusion.1), channel_id=1, source_target_pairs={{0,2},{1,3},{2,0},{3,1},{4,6},{5,7},{6,4},{7,5},{8,10},{9,11},{10,... | collective-permute-start | bytes 1179656 | tf_op jit(solution)/shard_map/ppermute | solution.py:133
  65.6 2.5 %copy-start.5 = (bf16[256,768]{1,0:T(8,128)(2,1)}, bf16[256,768]{1,0:T(8,128)(2,1)S(1)}, u32[]{:S(2)}) copy-start(bf16[256,768]{1,0:T(8,128)(2,1)S(1)} %collective-permute-done.4.refs_5_) | copy-start | bytes 1179652
  65.7 10.9 %collective-permute-start.5 = (bf16[512,384]{1,0:T(8,128)(2,1)S(1)}, bf16[512,384]{1,0:T(8,128)(2,1)}, u32[]{:S(2)}, u32[]{:S(2)}) collective-permute-start(bf16[512,384]{1,0:T(8,128)(2,1)S(1)} %pad_maximum_fusion.3), channel_id=1, source_target_pairs={{0,16},{1,17},{2,18},{3,19},{4,20},{5,21},{6,22},{7,23},{8,24},{9,... | collective-permute-start | bytes 1179656 | tf_op jit(solution)/shard_map/ppermute | solution.py:133
  67.3 0.8 copy-start.7
  68.1 7.9 %collective-permute-start.8 = (bf16[512,256]{1,0:T(8,128)(2,1)}, bf16[512,256]{1,0:T(8,128)(2,1)S(1)}, u32[]{:S(2)}, u32[]{:S(2)}) collective-permute-start(bf16[512,256]{1,0:T(8,128)(2,1)} %pad_maximum_fusion.5), channel_id=1, source_target_pairs={{0,4},{1,5},{2,6},{3,7},{4,0},{5,1},{6,2},{7,3},{8,12},{9,13},{10,... | collective-permute-start | bytes 786440 | tf_op jit(solution)/shard_map/ppermute | solution.py:133
  76.7 1.4 copy-start
  85.9 4.4 %collective-permute-start.9 = (f32[8,128,512]{2,1,0:T(8,128)}, f32[8,128,512]{2,1,0:T(8,128)S(1)}, u32[]{:S(2)}, u32[]{:S(2)}) collective-permute-start(f32[8,128,512]{2,1,0:T(8,128)} %get-tuple-element.8), channel_id=1, source_target_pairs={{0,1},{1,0},{2,3},{3,2},{4,5},{5,4},{6,7},{7,6},{8,9},{9,8},{10,11... | collective-permute-start | bytes 6291464 | tf_op jit(solution)/shard_map/ppermute | solution.py:336
  90.4 1.4 copy-start.1
  95.9 24.2 %all-to-all-start.1 = ((bf16[8,128,768]{2,1,0:T(8,128)(2,1)}), bf16[8,128,768]{2,1,0:T(8,128)(2,1)S(1)}, u32[]{:S(2)}, u32[]{:S(2)}) async-start(bf16[8,128,768]{2,1,0:T(8,128)(2,1)} %split.1), calls=%async_computation.1 | async-start | bytes 3145728 | tf_op jit(solution)/shard_map/all_to_all | solution.py:337
  120.8 27.5 %copy-start.8 = (bf16[128,512]{1,0:T(8,128)(2,1)}, bf16[128,512]{1,0:T(8,128)(2,1)S(1)}, u32[]{:S(2)}) copy-start(bf16[128,512]{1,0:T(8,128)(2,1)S(1)} %fusion.refs_0_) | copy-start | bytes 393220
  120.8 9.0 %collective-permute-start.10 = (bf16[128,512]{1,0:T(8,128)(2,1)S(1)}, bf16[128,512]{1,0:T(8,128)(2,1)S(1)}, u32[]{:S(2)}, u32[]{:S(2)}) collective-permute-start(bf16[128,512]{1,0:T(8,128)(2,1)S(1)} %fusion.refs_0_), channel_id=1, source_target_pairs={{0,2},{1,3},{2,4},{3,5},{4,6},{5,7},{6,8},{7,9},{8,10},{9,11},{10,... | collective-permute-start | bytes 393224 | tf_op jit(solution)/shard_map/ppermute | solution.py:360
  122.1 12.1 %collective-permute-start.11 = (bf16[128,512]{1,0:T(8,128)(2,1)S(1)}, bf16[128,512]{1,0:T(8,128)(2,1)S(1)}, u32[]{:S(2)}, u32[]{:S(2)}) collective-permute-start(bf16[128,512]{1,0:T(8,128)(2,1)S(1)} %fusion.refs_0_), channel_id=1, source_target_pairs={{0,4},{1,5},{2,6},{3,7},{4,8},{5,9},{6,10},{7,11},{8,12},{9,13},{1... | collective-permute-start | bytes 393224 | tf_op jit(solution)/shard_map/ppermute | solution.py:360
  123.4 12.3 %collective-permute-start.12 = (bf16[128,512]{1,0:T(8,128)(2,1)S(1)}, bf16[128,512]{1,0:T(8,128)(2,1)S(1)}, u32[]{:S(2)}, u32[]{:S(2)}) collective-permute-start(bf16[128,512]{1,0:T(8,128)(2,1)S(1)} %fusion.refs_0_), channel_id=1, source_target_pairs={{0,6},{1,7},{2,8},{3,9},{4,10},{5,11},{6,12},{7,13},{8,14},{9,15},... | collective-permute-start | bytes 393224 | tf_op jit(solution)/shard_map/ppermute | solution.py:360
  124.7 23.6 %collective-permute-start.13 = (bf16[128,512]{1,0:T(8,128)(2,1)S(1)}, bf16[128,512]{1,0:T(8,128)(2,1)S(1)}, u32[]{:S(2)}, u32[]{:S(2)}) collective-permute-start(bf16[128,512]{1,0:T(8,128)(2,1)S(1)} %fusion.refs_0_), channel_id=1, source_target_pairs={{0,8},{1,9},{2,10},{3,11},{4,12},{5,13},{6,14},{7,15},{16,24},{17,... | collective-permute-start | bytes 393224 | tf_op jit(solution)/shard_map/ppermute | solution.py:360
  126.0 22.3 %collective-permute-start.14 = (bf16[128,512]{1,0:T(8,128)(2,1)S(1)}, bf16[128,512]{1,0:T(8,128)(2,1)S(1)}, u32[]{:S(2)}, u32[]{:S(2)}) collective-permute-start(bf16[128,512]{1,0:T(8,128)(2,1)S(1)} %fusion.refs_0_), channel_id=1, source_target_pairs={{0,10},{1,11},{2,12},{3,13},{4,14},{5,15},{16,26},{17,27},{18,28},... | collective-permute-start | bytes 393224 | tf_op jit(solution)/shard_map/ppermute | solution.py:360
  129.7 18.5 %copy-start.13 = (bf16[128,512]{1,0:T(8,128)(2,1)}, bf16[128,512]{1,0:T(8,128)(2,1)S(1)}, u32[]{:S(2)}) copy-start(bf16[128,512]{1,0:T(8,128)(2,1)S(1)} %collective-permute-done.10.refs_1_) | copy-start | bytes 393220
  134.2 14.0 %copy-start.14 = (bf16[128,512]{1,0:T(8,128)(2,1)}, bf16[128,512]{1,0:T(8,128)(2,1)S(1)}, u32[]{:S(2)}) copy-start(bf16[128,512]{1,0:T(8,128)(2,1)S(1)} %collective-permute-done.11.refs_2_) | copy-start | bytes 393220
  135.7 12.6 %copy-start.15 = (bf16[128,512]{1,0:T(8,128)(2,1)}, bf16[128,512]{1,0:T(8,128)(2,1)S(1)}, u32[]{:S(2)}) copy-start(bf16[128,512]{1,0:T(8,128)(2,1)S(1)} %collective-permute-done.12.refs_3_) | copy-start | bytes 393220
  (3 other events, 2.0 us)

commit v2 on v1

v2 whole, which is shorter than its diff:
```python
import functools
import math

import jax
import jax.numpy as jnp
from jax import lax
from jax.experimental import pallas as pl
from jax.experimental.pallas import tpu as pltpu
from jax.sharding import Mesh
from jax.sharding import PartitionSpec as P

KVH = 4
HD = 128
QPK = 16
BLK = 128
KVW = 1024
PAD = 16
SHARD = ("hi", "zz", "y")
ALL = ("groups",) + SHARD + ("tensor",)
BLOCK = ("groups", "zz")
MIB = 2**20


def after(value, *others):
    return lax.optimization_barrier((value,) + others)[0]


def flat_pairs(sizes, move):
    groups, shards, cores = sizes
    pairs = []
    for g in range(groups):
        for s in range(shards):
            for c in range(cores):
                to = move(g, s, c)
                if to is not None:
                    pairs.append(((g * shards + s) * cores + c, (to[0] * shards + to[1]) * cores + to[2]))
    return pairs


def scale_kernel(first_ref, codes_ref, scales_ref, ids_ref, near_ref, far_ref):
    depth = near_ref.shape[0] - PAD
    blocks = depth // BLK
    own, column, block = first_ref[0], first_ref[1], first_ref[2]
    for out_ref, which in ((near_ref, own), (far_ref, 1 - own)):
        for k in range(blocks):
            row = pl.multiple_of((which * blocks + k) * BLK, BLK)
            scale = scales_ref[column, block + which * blocks + k]
            part = codes_ref[pl.ds(row, BLK), :].astype(jnp.float32) * scale
            out_ref[k * BLK : (k + 1) * BLK, :] = part.astype(jnp.bfloat16)
        ids = ids_ref[...].astype(jnp.float32)
        out_ref[depth:, :] = jnp.broadcast_to(ids, (PAD, ids.shape[1])).astype(jnp.bfloat16)


def scaled_weight(codes, scales, segment_ids, depth, group, zz, column):
    width = codes.shape[1]
    share = 2 * depth
    first = jnp.stack([zz, column, group * (share // BLK), group]).astype(jnp.int32)
    out = jax.ShapeDtypeStruct((depth + PAD, width), jnp.bfloat16)
    whole = pl.BlockSpec((depth + PAD, width), lambda i, f: (0, 0))
    return pl.pallas_call(
        scale_kernel,
        grid_spec=pltpu.PrefetchScalarGridSpec(
            num_scalar_prefetch=1,
            grid=(1,),
            in_specs=[
                pl.BlockSpec((share, width), lambda i, f: (f[3], 0)),
                pl.BlockSpec(memory_space=pltpu.SMEM),
                pl.BlockSpec((1, width), lambda i, f: (0, 0)),
            ],
            out_specs=[whole, whole],
        ),
        out_shape=[out, out],
        compiler_params=pltpu.CompilerParams(vmem_limit_bytes=8 * MIB),
        name="scale",
    )(first, codes, scales.T, segment_ids.reshape(1, -1))


def gather_by_steps(sizes, hidden, codes, scales, segment_ids):
    rows, features = hidden.shape
    depth = features // 4
    group, zz, y = lax.axis_index("groups"), lax.axis_index("zz"), lax.axis_index("y")
    shard = (lax.axis_index("hi") * 2 + zz) * 2 + y
    member = group * 2 + zz

    def send(value, move):
        return lax.ppermute(value, ALL, flat_pairs(sizes, move))

    def along_shard(distance):
        return lambda g, s, c: (g, s ^ distance, c)

    near, far = scaled_weight(
        codes, scales, segment_ids, depth, group, zz, shard * codes.shape[1] // BLK
    )
    piece = {0: near}
    piece[6] = send(far, along_shard(6))
    piece[2] = send(far, along_shard(2))
    piece[1] = send(near, along_shard(1))
    sent = lax.dynamic_slice_in_dim(after(hidden, near), (1 - group) * 2 * depth, 2 * depth, 1)
    across = send(sent, lambda g, s, c: (1 - g, s, c))
    piece[4] = send(after(near, piece[2], piece[1]), along_shard(4))
    piece[3] = send(piece[2], along_shard(1))
    pair = jnp.concatenate(
        [
            lax.dynamic_slice_in_dim(hidden, (group * 2 + 1 - zz) * depth, depth, 1),
            lax.dynamic_slice_in_dim(across, (1 - zz) * depth, depth, 1),
        ],
        axis=0,
    )
    pair = send(pair, along_shard(2))
    piece[7] = send(after(piece[6], piece[3]), along_shard(1))
    piece[5] = send(after(piece[4], piece[7]), along_shard(1))
    order = sorted(piece)
    shards = jnp.stack([jnp.bitwise_xor(shard, d) for d in order]).astype(jnp.int32)
    arrays = [hidden, across, pair]
    copies = [
        (0, 0, member * depth, member),
        (1, 0, zz * depth, jnp.bitwise_xor(member, 2)),
        (2, 0, 0, jnp.bitwise_xor(member, 1)),
        (2, rows, 0, jnp.bitwise_xor(member, 3)),
    ]
    ids = [piece[d][depth : depth + 1] for d in order]
    known = jnp.concatenate(ids, axis=0)
    spot = jnp.bitwise_xor(shard, jnp.arange(8, dtype=jnp.int32))
    return arrays, copies, [piece[d] for d in order], shards, known[spot]


def gather_whole(sizes, hidden, codes, scales, segment_ids):
    groups = sizes[0]
    pair = lax.axis_size("zz")
    members = groups * pair
    rows, features = hidden.shape
    depth = features // members
    width = codes.shape[1]
    shards = sizes[1]
    shard = lax.axis_index(SHARD)
    share = pair * depth
    sliced = jnp.moveaxis(hidden.reshape(rows, members, depth), 1, 0)
    got = lax.all_to_all(sliced, BLOCK, 0, 0, tiled=True).reshape(members * rows, depth)
    copies = [(0, m * rows, 0, m) for m in range(members)]

    blocks = share // BLK
    group = lax.axis_index("groups")
    column = lax.dynamic_slice_in_dim(scales, (shard * width) // BLK, 1, 1)
    column = lax.dynamic_slice_in_dim(column, group * blocks, blocks, 0)
    held = lax.dynamic_slice_in_dim(codes, group * share, share, 0)
    weight = (held.astype(jnp.float32).reshape(blocks, BLK, width) * column[:, :, None]).astype(
        jnp.bfloat16
    )
    weight = weight.reshape(pair, depth, width)
    ids = segment_ids.astype(jnp.bfloat16).reshape(rows // width, width)
    ids = jnp.pad(ids, ((0, PAD - rows // width), (0, 0)))
    weight = jnp.concatenate([weight, jnp.broadcast_to(ids, (pair, PAD, width))], axis=1)
    high = lax.axis_size("hi")
    weight = jnp.broadcast_to(weight[None], (high,) + weight.shape)
    weight = weight.reshape(high * pair, depth + PAD, width)
    weight = lax.all_to_all(weight, ("hi", "zz"), 0, 0, tiled=True)
    weight = lax.all_gather(weight, "y", axis=1).reshape(shards, depth + PAD, width)
    known = weight[:, depth : depth + rows // width, :].reshape(shards, rows)
    weight = jnp.moveaxis(weight[:, :depth].reshape(2, shards // 2, depth, width), 1, 2)
    halves = weight.reshape(2, depth, shards * width // 2)
    return [got], copies, [halves[0], halves[1]], jnp.arange(2, dtype=jnp.int32), known


def project_kernel(copies, sources, columns, rows_ref, first_ref, member_ref, shard_ref, core_ref, *refs):
    hidden_refs, refs = refs[:sources], refs[sources:]
    weight_refs, (other_ref, mine_ref, left, halves, sems) = refs[:-5], refs[-5:]
    step = pl.program_id(0)
    rows = mine_ref.shape[1]
    depth = left.shape[1]
    core = core_ref[0]

    @pl.when(step == 0)
    def _():
        started = []
        for k, at in enumerate(copies):
            first = pl.multiple_of(first_ref[k], 128)
            row = pl.multiple_of(rows_ref[k], 16)
            to = pl.multiple_of(member_ref[k] * rows, rows)
            started.append(
                pltpu.make_async_copy(
                    hidden_refs[at].at[pl.ds(row, rows), pl.ds(first, depth)],
                    left.at[pl.ds(to, rows), :],
                    sems.at[k],
                )
            )
        for k, ref in enumerate(weight_refs):
            width = ref.shape[1]
            first = shard_ref[k] * width
            half = jnp.bitwise_xor(core, first // columns)
            at = pl.multiple_of(first % columns, 128)
            started.append(
                pltpu.make_async_copy(
                    ref.at[pl.ds(0, depth), :],
                    halves.at[half, :, pl.ds(at, width)],
                    sems.at[len(copies) + k],
                )
            )
        for copy in started:
            copy.start()
        for copy in started:
            copy.wait()

    size = mine_ref.shape[2]
    per_half = columns // size
    for half, out_ref in ((1, other_ref), (0, mine_ref)):
        for k in range(per_half):

            @pl.when(step == (1 - half) * per_half + k)
            def _():
                total = jnp.dot(
                    left[...],
                    halves[half, :, k * size : (k + 1) * size],
                    preferred_element_type=jnp.float32,
                )
                out_ref[...] = total.reshape(out_ref.shape)


def project(arrays, copies, pieces, shards, core, rows):
    members = len(copies)
    width = pieces[0].shape[1]
    columns = len(pieces) * width // 2
    depth = arrays[-1].shape[1]
    table = [jnp.stack([jnp.asarray(c[i], jnp.int32) for c in copies]) for i in (1, 2, 3)]
    size = 256
    per_half = columns // size
    out = jax.ShapeDtypeStruct((members, rows, columns), jnp.float32)
    return pl.pallas_call(
        functools.partial(project_kernel, [c[0] for c in copies], len(arrays), columns),
        grid_spec=pltpu.PrefetchScalarGridSpec(
            num_scalar_prefetch=5,
            grid=(2 * per_half,),
            in_specs=[pl.BlockSpec(memory_space=pl.ANY)] * (len(arrays) + len(pieces)),
            out_specs=[
                pl.BlockSpec((members, rows, size), lambda i, *_: (0, 0, jnp.minimum(i, per_half - 1))),
                pl.BlockSpec((members, rows, size), lambda i, *_: (0, 0, jnp.maximum(i - per_half, 0))),
            ],
            scratch_shapes=[
                pltpu.VMEM((members * rows, depth), jnp.bfloat16),
                pltpu.VMEM((2, depth, columns), jnp.bfloat16),
                pltpu.SemaphoreType.DMA((len(copies) + len(pieces),)),
            ],
        ),
        out_shape=[out, out],
        compiler_params=pltpu.CompilerParams(vmem_limit_bytes=24 * MIB),
        name="project",
    )(*table, shards, core, *arrays, *pieces)


def split_kernel(mine_ref, got_ref, out_ref):
    total = mine_ref[...] + got_ref[...]
    columns = total.shape[2]
    out_ref[:, :, :columns] = total.astype(jnp.bfloat16)
    for head in range(columns // (2 * HD)):
        keys = total[:, :, 2 * head * HD : (2 * head + 1) * HD]
        rest = keys - keys.astype(jnp.bfloat16).astype(jnp.float32)
        at = columns + head * HD
        out_ref[:, :, at : at + HD] = rest.astype(jnp.bfloat16)


def split(mine, got):
    members, rows, columns = mine.shape
    spec = pl.BlockSpec((1, rows, columns), lambda i: (i, 0, 0))
    wide = columns + columns // 2
    return pl.pallas_call(
        split_kernel,
        grid=(members,),
        in_specs=[spec, spec],
        out_specs=pl.BlockSpec((1, rows, wide), lambda i: (i, 0, 0)),
        out_shape=jax.ShapeDtypeStruct((members, rows, wide), jnp.bfloat16),
        compiler_params=pltpu.CompilerParams(vmem_limit_bytes=24 * MIB),
        name="split",
    )(mine, got)


def attend_kernel(pieces, heads, stack, query_ref, allowed_ref, *refs):
    kv_refs, (out_ref, keys, values) = refs[:pieces], refs[pieces:]
    rows = query_ref.shape[0]
    scaling = 1.0 / math.sqrt(HD)
    for d, ref in enumerate(kv_refs):
        keys[d * rows : (d + 1) * rows, :] = ref[:, :HD]
        values[d * rows : (d + 1) * rows, :] = ref[:, HD:]
    allowed = allowed_ref[...]
    allowed = jnp.concatenate([allowed] * stack, axis=0) > 0.0
    for part in range(heads // stack):
        columns = [slice((part * stack + h) * HD, (part * stack + h + 1) * HD) for h in range(stack)]
        query = jnp.concatenate([query_ref[:, c] for c in columns], axis=0)
        scores = lax.dot_general(
            query, keys[...], (((1,), (1,)), ((), ())), preferred_element_type=jnp.float32
        )
        scores = jnp.where(allowed, scores * scaling, -jnp.inf)
        weights = jnp.exp(scores - jnp.max(scores, axis=1, keepdims=True))
        totals = jnp.sum(weights, axis=1, keepdims=True)
        result = jnp.dot(
            weights.astype(jnp.bfloat16), values[...], preferred_element_type=jnp.float32
        )
        result = (result / totals).astype(jnp.bfloat16)
        for h, c in enumerate(columns):
            out_ref[:, c] = result[h * rows : (h + 1) * rows]


def attend(queries, allowed, pieces):
    rows, width = queries.shape
    window = allowed.shape[1]
    group = QPK * HD
    stack = 4 if window <= 1024 else 1
    return pl.pallas_call(
        functools.partial(attend_kernel, len(pieces), QPK, stack),
        grid=(width // group,),
        in_specs=[
            pl.BlockSpec((rows, group), lambda i: (0, i)),
            pl.BlockSpec((rows, window), lambda i: (0, 0)),
        ]
        + [pl.BlockSpec((rows, 2 * HD), lambda i: (0, i))] * len(pieces),
        out_specs=pl.BlockSpec((rows, group), lambda i: (0, i)),
        out_shape=jax.ShapeDtypeStruct((rows, width), jnp.bfloat16),
        scratch_shapes=[pltpu.VMEM((window, HD), jnp.bfloat16)] * 2,
        compiler_params=pltpu.CompilerParams(vmem_limit_bytes=24 * MIB),
        name="attend",
    )(queries, allowed, *pieces)


def on_device(sizes, hidden, codes, scales, queries, segment_ids):
    groups, shards, cores = sizes
    rows = hidden.shape[0]
    shard = lax.axis_index(SHARD)
    core = lax.axis_index("tensor").astype(jnp.int32)
    by_steps = groups == 2 and shards == 8 and codes.shape[1] == BLK and rows == BLK
    gather = gather_by_steps if by_steps else gather_whole
    arrays, copies, pieces, where, known = gather(sizes, hidden, codes, scales, segment_ids)
    other, mine = project(arrays, copies, pieces, where, core[None], rows)
    swap = flat_pairs(sizes, lambda g, s, c: (g, s, 1 - c))
    partial = split(mine, lax.ppermute(other, ALL, swap))
    partial = lax.all_to_all(partial, BLOCK, 0, 0, tiled=True)
    total = jnp.sum(partial.astype(jnp.float32), axis=0)
    columns = mine.shape[2]
    rest = total[:, columns:].reshape(rows, -1, 1, HD)
    rest = jnp.concatenate([rest, jnp.zeros_like(rest)], axis=2).reshape(rows, columns)
    keyval = (total[:, :columns] + rest).astype(jnp.bfloat16)

    back = min(shards // 2 + 1, shards - 1)
    from_shard = shard - jnp.arange(back + 1, dtype=jnp.int32)
    seen = known[jnp.maximum(from_shard, 0)].reshape(-1)
    offset = jnp.arange(rows, dtype=jnp.int32)
    keypos = (from_shard[:, None] * rows + offset[None, :]).reshape(-1)
    rowpos = shard * rows + offset
    allowed = (
        (segment_ids.astype(jnp.bfloat16)[:, None] == seen[None, :])
        & (keypos[None, :] <= rowpos[:, None])
        & (keypos[None, :] >= 0)
    ).astype(jnp.float32)

    pieces = [keyval]
    for d in range(1, back + 1):
        up = flat_pairs(sizes, lambda g, s, c: (g, s + d, c) if s + d < shards else None)
        pieces.append(lax.ppermute(keyval, ALL, up))
    return attend(queries, allowed, pieces)


def solution(mesh):
    sizes = tuple(mesh.shape[name] for name in ("groups", "shard", "tensor"))
    groups, shards, cores = sizes
    y = math.gcd(shards, 2)
    zz = math.gcd(shards // y, 2)
    fine = Mesh(mesh.devices.reshape(groups, shards // (y * zz), zz, y, cores), ALL)
    tokens = ("groups",) + SHARD
    in_specs = (
        P(tokens, "tensor"),
        P("tensor", SHARD),
        P("tensor", None),
        P(tokens, "tensor"),
        P(tokens),
    )
    return jax.shard_map(
        functools.partial(on_device, sizes),
        mesh=fine,
        in_specs=in_specs,
        out_specs=P(tokens, "tensor"),
        check_vma=False,
    )
```

time: 159 us -> 138 us (0.87)
  starting transfers between devices: 27.3 us -> 20.1 us
  Pallas kernels: 23.5 us -> 16.9 us
  local copies, waits for them, and re-layouts: 18.5 us -> 13.2 us
  other arithmetic: 4.76 us -> 1.72 us
  waiting for transfers between devices: 83.3 us -> 85.4 us
    ppermute x9, waiting for transfers between devices: 41.3 us -> 60.9 us  [send(): return lax.ppermute(value, ALL, flat_pairs(sizes, move))]
    all_to_all x1, waiting for transfers between devices: 17.6 us -> 3.46 us  [on_device(): partial = lax.all_to_all(partial, BLOCK, 0, 0, tiled=True)]
    dynamic_slice x15 -> x3, local copies, waits for them, and re-layouts: 9.63 us -> 1.12 us  [the longest x1 1.04 us: gather_by_steps(): lax.dynamic_slice_in_dim(after(hidden, near), (1 - group) * 2 * depth, 2...]
    all_to_all x1 -> x0, starting transfers between devices: 6 us -> none  [on_device(): weight = lax.all_to_all(weight, SHARD, 0, 0, tiled=True)]
    pallas_call x3, Pallas kernels: 15.3 us -> 10 us  [the longest x1 6.32 us: project(): pl.pallas_call(functools.partial(project_kernel, [c[0] for c in copies],...]
    slice x1 -> x8, local copies, waits for them, and re-layouts: 0.72 us -> 5.47 us  [gather_by_steps(): ids = [piece[d][depth:depth + 1] for d in order]]
    ppermute x1, waiting for transfers between devices: 4.36 us -> 2.64 us  [on_device(): partial = split(mine, lax.ppermute(other, ALL, swap))]
    concatenate x6 -> x1, other arithmetic: 2.79 us -> 1.08 us  [gather_by_steps(): jnp.concatenate([lax.dynamic_slice_in_dim(hidden, (group * 2 + 1 - zz) *...]
  transfers between devices with their start and end apart: 17 -> 16, of which waited for: 11 -> 12; matrix products, arithmetic and copies ran while one was open for 10% -> 6% of each run, Pallas kernels for 0% -> 0%
where the time goes in v2:
time: 138 us; the launch traced here: 137 us
  waiting for transfers between devices  85.4 us (62%)
  starting transfers between devices  20.1 us (15%)
  Pallas kernels  16.9 us (12%)
  local copies, waits for them, and re-layouts  13.2 us (10%)
  other arithmetic  1.72 us (1%)
    ppermute x9, waiting for transfers between devices, send(): return lax.ppermute(value, ALL, flat_pairs(sizes, move))  60.9 us
    ppermute x5, waiting for transfers between devices, on_device(): pieces.append(lax.ppermute(keyval, ALL, up))  18.4 us
    ppermute x9, starting transfers between devices, send(): return lax.ppermute(value, ALL, flat_pairs(sizes, move))  10.1 us
    pallas_call x1, Pallas kernels, attend(): pl.pallas_call(functools.partial(attend_kernel, len(pieces), QPK, stack),...  6.87 us
    ppermute x5, starting transfers between devices, on_device(): pieces.append(lax.ppermute(keyval, ALL, up))  6.46 us
    pallas_call x1, Pallas kernels, project(): pl.pallas_call(functools.partial(project_kernel, [c[0] for c in copies],...  6.32 us
    slice x8, local copies, waits for them, and re-layouts, gather_by_steps(): ids = [piece[d][depth:depth + 1] for d in order]  5.47 us
    unnamed x18, local copies, waits for them, and re-layouts  4.94 us
  transfers between devices with their start and end apart: 16, of which 12 were waited for; matrix products, arithmetic and copies ran while one was open for 6% of the time, Pallas kernels for 0%

profile of v2, /device:TPU:28, one launch (start us, length us, event | category | flops | bytes accessed | tf_op | source)
XLA Modules:
  0.0 137.5 jit_solution(7794007093159712339)
XLA Ops:
  0.1 1.7 %copy-done.1 = bf16[8192,128]{1,0:T(8,128)(2,1)S(1)} copy-done((bf16[8192,128]{1,0:T(8,128)(2,1)S(1)}, bf16[8192,128]{1,0:T(8,128)(2,1)}, u32[]{:S(2)}) %copy-start.1) | copy-done | bytes 2097176
  1.8 0.7 copy-done.5
  3.2 2.2 %scale.1 = (bf16[2064,128]{1,0:T(8,128)(2,1)}, bf16[2064,128]{1,0:T(8,128)(2,1)}) custom-call(s32[4]{0:T(128)S(1)} %pad_add_fusion.first_ref, bf16[8192,128]{1,0:T(8,128)(2,1)S(1)} %copy-done.1, f32[8,64]{1,0:T(8,128)S(1)} %bitcast.31, s32[1,128]{1,0:T(1,128)S(1)} %bitcast.32), custom_call_target="tpu_custom_call" | custom-call | tf_op jit(solution)/shard_map/scale/pallas_call | solution.py:60
  5.4 1.0 constant_dynamic-slice_fusion.2
  6.4 1.5 %collective-permute-start.7 = (bf16[128,4096]{1,0:T(8,128)(2,1)}, bf16[128,4096]{1,0:T(8,128)(2,1)S(1)}, u32[]{:S(2)}, u32[]{:S(2)}) collective-permute-start(bf16[128,4096]{1,0:T(8,128)(2,1)} %constant_dynamic-slice_fusion.2), channel_id=1, source_target_pairs={{0,16},{1,17},{2,18},{3,19},{4,20},{5,21},{6,22},{7,23},{8,24},{9,... | collective-permute-start | bytes 3145736 | tf_op jit(solution)/shard_map/ppermute | solution.py:86
  8.9 1.3 collective-permute-start.4
  10.2 21.5 %collective-permute-done.1.refs_5_ = bf16[2064,128]{1,0:T(8,128)(2,1)} collective-permute-done((bf16[2064,128]{1,0:T(8,128)(2,1)}, bf16[2064,128]{1,0:T(8,128)(2,1)}, u32[]{:S(2)}, u32[]{:S(2)}) %collective-permute-start.1) | collective-permute-done | bytes 528416 | tf_op jit(solution)/shard_map/ppermute | solution.py:86
  32.4 2.0 %collective-permute-done.4.refs_9_ = bf16[2064,128]{1,0:T(8,128)(2,1)} collective-permute-done((bf16[2064,128]{1,0:T(8,128)(2,1)}, bf16[2064,128]{1,0:T(8,128)(2,1)}, u32[]{:S(2)}, u32[]{:S(2)}) %collective-permute-start.4) | collective-permute-done | bytes 528416 | tf_op jit(solution)/shard_map/ppermute | solution.py:86
  34.4 11.4 %collective-permute-done.2.refs_6_ = bf16[2064,128]{1,0:T(8,128)(2,1)} collective-permute-done((bf16[2064,128]{1,0:T(8,128)(2,1)}, bf16[2064,128]{1,0:T(8,128)(2,1)}, u32[]{:S(2)}, u32[]{:S(2)}) %collective-permute-start.2) | collective-permute-done | bytes 528416 | tf_op jit(solution)/shard_map/ppermute | solution.py:86
  46.2 1.1 pad_maximum_fusion
  47.3 3.7 %collective-permute-start.8 = (bf16[256,2048]{1,0:T(8,128)(2,1)}, bf16[256,2048]{1,0:T(8,128)(2,1)}, u32[]{:S(2)}, u32[]{:S(2)}) collective-permute-start(bf16[256,2048]{1,0:T(8,128)(2,1)} %pad_maximum_fusion), channel_id=1, source_target_pairs={{0,4},{1,5},{2,6},{3,7},{4,0},{5,1},{6,2},{7,3},{8,12},{9,13},{10,... | collective-permute-start | bytes 3145736 | tf_op jit(solution)/shard_map/ppermute | solution.py:86
  51.0 6.2 %collective-permute-done.3.refs_7_ = bf16[2064,128]{1,0:T(8,128)(2,1)} collective-permute-done((bf16[2064,128]{1,0:T(8,128)(2,1)}, bf16[2064,128]{1,0:T(8,128)(2,1)}, u32[]{:S(2)}, u32[]{:S(2)}) %collective-permute-start.3) | collective-permute-done | bytes 528416 | tf_op jit(solution)/shard_map/ppermute | solution.py:86
  57.2 0.8 copy-done.3
  58.0 1.5 %collective-permute-start.6 = (bf16[2064,128]{1,0:T(8,128)(2,1)}, bf16[2064,128]{1,0:T(8,128)(2,1)}, u32[]{:S(2)}, u32[]{:S(2)}) collective-permute-start(bf16[2064,128]{1,0:T(8,128)(2,1)} %collective-permute-done.3.refs_7_), channel_id=1, source_target_pairs={{0,2},{1,3},{2,0},{3,1},{4,6},{5,7},{6,4},{7,5},{8,10},{9,11},{10,... | collective-permute-start | bytes 1585160 | tf_op jit(solution)/shard_map/ppermute | solution.py:86
  59.7 19.9 %collective-permute-done.8.refs_2_ = bf16[256,2048]{1,0:T(8,128)(2,1)} collective-permute-done((bf16[256,2048]{1,0:T(8,128)(2,1)}, bf16[256,2048]{1,0:T(8,128)(2,1)}, u32[]{:S(2)}, u32[]{:S(2)}) %collective-permute-start.8) | collective-permute-done | bytes 1048608 | tf_op jit(solution)/shard_map/ppermute | solution.py:86
  79.6 1.0 copy-done.4
  80.6 6.3 %project.1 = (f32[4,128,512]{2,1,0:T(8,128)S(1)}, f32[4,128,512]{2,1,0:T(8,128)S(1)}) custom-call(s32[4]{0:T(128)S(1)} %copy-done.6, s32[4]{0:T(128)S(1)} %get-tuple-element.21.first_ref, s32[4]{0:T(128)S(1)} %get-tuple-element.22.member_ref, s32[8]{0:T(128)S(1)} %stack.87.shard_ref, s32[1]{0:T(128)} %bitcast.24.core_ref, bf16[128,8192]{1,0:T(8,128)(2,1)S(1)} %copy-done, ...), custom_call_target="tpu_custom_call" | custom-call | tf_op jit(solution)/shard_map/project/pallas_call | solution.py:227
  87.0 2.6 %collective-permute-done.9.got_ref = f32[4,128,512]{2,1,0:T(8,128)S(1)} collective-permute-done((f32[4,128,512]{2,1,0:T(8,128)S(1)}, f32[4,128,512]{2,1,0:T(8,128)S(1)}, u32[]{:S(2)}, u32[]{:S(2)}) %collective-permute-start.9) | collective-permute-done | bytes 1048608 | tf_op jit(solution)/shard_map/ppermute | solution.py:332
  89.7 1.5 %split.1 = bf16[4,128,768]{2,1,0:T(8,128)(2,1)} custom-call(f32[4,128,512]{2,1,0:T(8,128)S(1)} %get-tuple-element.19.mine_ref, f32[4,128,512]{2,1,0:T(8,128)S(1)} %collective-permute-done.9.got_ref), custom_call_target="tpu_custom_call" | custom-call | tf_op jit(solution)/shard_map/split/pallas_call | solution.py:264
  91.1 3.5 %all-to-all-start = ((bf16[4,128,768]{2,1,0:T(8,128)(2,1)}), bf16[4,128,768]{2,1,0:T(8,128)(2,1)S(1)}, u32[]{:S(2)}, u32[]{:S(2)}) async-start(bf16[4,128,768]{2,1,0:T(8,128)(2,1)} %split.1), calls=%async_computation | async-start | bytes 1572864 | tf_op jit(solution)/shard_map/all_to_all | solution.py:333
  94.7 0.8 slice.30
  95.6 0.7 slice.44
  101.5 3.5 %all-to-all-done = bf16[4,128,768]{2,1,0:T(8,128)(2,1)S(1)} async-done(((bf16[4,128,768]{2,1,0:T(8,128)(2,1)}), bf16[4,128,768]{2,1,0:T(8,128)(2,1)S(1)}, u32[]{:S(2)}, u32[]{:S(2)}) %all-to-all-start) | async-done | bytes 786464 | tf_op jit(solution)/shard_map/all_to_all | solution.py:333
  105.5 1.3 collective-permute-start.10
  106.8 1.3 collective-permute-start.11
  108.1 1.3 collective-permute-start.12
  109.4 1.3 collective-permute-start.13
  110.7 1.3 collective-permute-start.14
  112.4 3.4 %collective-permute-done.11.refs_2_ = bf16[128,512]{1,0:T(8,128)(2,1)S(1)} collective-permute-done((bf16[128,512]{1,0:T(8,128)(2,1)S(1)}, bf16[128,512]{1,0:T(8,128)(2,1)S(1)}, u32[]{:S(2)}, u32[]{:S(2)}) %collective-permute-start.11) | collective-permute-done | bytes 131104 | tf_op jit(solution)/shard_map/ppermute | solution.py:355
  115.8 3.0 %collective-permute-done.12.refs_3_ = bf16[128,512]{1,0:T(8,128)(2,1)S(1)} collective-permute-done((bf16[128,512]{1,0:T(8,128)(2,1)S(1)}, bf16[128,512]{1,0:T(8,128)(2,1)S(1)}, u32[]{:S(2)}, u32[]{:S(2)}) %collective-permute-start.12) | collective-permute-done | bytes 131104 | tf_op jit(solution)/shard_map/ppermute | solution.py:355
  118.9 11.6 %collective-permute-done.13.refs_4_ = bf16[128,512]{1,0:T(8,128)(2,1)S(1)} collective-permute-done((bf16[128,512]{1,0:T(8,128)(2,1)S(1)}, bf16[128,512]{1,0:T(8,128)(2,1)S(1)}, u32[]{:S(2)}, u32[]{:S(2)}) %collective-permute-start.13) | collective-permute-done | bytes 131104 | tf_op jit(solution)/shard_map/ppermute | solution.py:355
  130.6 6.9 %attend.1 = bf16[128,4096]{1,0:T(8,128)(2,1)} custom-call(bf16[128,4096]{1,0:T(8,128)(2,1)S(1)} %copy-done.2, f32[128,768]{1,0:T(8,128)S(1)} %and_convert_fusion.allowed_ref, bf16[128,512]{1,0:T(8,128)(2,1)S(1)} %fusion.refs_0_, bf16[128,512]{1,0:T(8,128)(2,1)S(1)} %collective-permute-done.10.refs_1_, bf16[128,512]{1,0:T(8,128)(2,1)S(1)} %collective-permute-done.11.refs_2_, ...), custom_call_target="tpu_custom_call" | custom-call | tf_op jit(solution)/shard_map/attend/pallas_call | solution.py:306
  (57 shorter events, 9.5 us)
Async XLA Ops:
  0.0 5.4 %copy-start = (bf16[128,8192]{1,0:T(8,128)(2,1)S(1)}, bf16[128,8192]{1,0:T(8,128)(2,1)}, u32[]{:S(2)}) copy-start(bf16[128,8192]{1,0:T(8,128)(2,1)} %refs_0_.1) | copy-start | bytes 6291460
  0.1 1.7 %copy-start.1 = (bf16[8192,128]{1,0:T(8,128)(2,1)S(1)}, bf16[8192,128]{1,0:T(8,128)(2,1)}, u32[]{:S(2)}) copy-start(bf16[8192,128]{1,0:T(8,128)(2,1)} %codes_ref.1) | copy-start | bytes 6291460
  1.8 0.7 copy-start.5
  2.5 0.7 copy-start.7
  6.4 25.9 %collective-permute-start.7 = (bf16[128,4096]{1,0:T(8,128)(2,1)}, bf16[128,4096]{1,0:T(8,128)(2,1)S(1)}, u32[]{:S(2)}, u32[]{:S(2)}) collective-permute-start(bf16[128,4096]{1,0:T(8,128)(2,1)} %constant_dynamic-slice_fusion.2), channel_id=1, source_target_pairs={{0,16},{1,17},{2,18},{3,19},{4,20},{5,21},{6,22},{7,23},{8,24},{9,... | collective-permute-start | bytes 3145736 | tf_op jit(solution)/shard_map/ppermute | solution.py:86
  7.9 23.8 %collective-permute-start.1 = (bf16[2064,128]{1,0:T(8,128)(2,1)}, bf16[2064,128]{1,0:T(8,128)(2,1)}, u32[]{:S(2)}, u32[]{:S(2)}) collective-permute-start(bf16[2064,128]{1,0:T(8,128)(2,1)} %get-tuple-element.14), channel_id=1, source_target_pairs={{0,4},{1,5},{2,6},{3,7},{4,0},{5,1},{6,2},{7,3},{8,12},{9,13},{10,... | collective-permute-start | bytes 1585160 | tf_op jit(solution)/shard_map/ppermute | solution.py:86
  8.4 23.9 %collective-permute-start = (bf16[2064,128]{1,0:T(8,128)(2,1)}, bf16[2064,128]{1,0:T(8,128)(2,1)}, u32[]{:S(2)}, u32[]{:S(2)}) collective-permute-start(bf16[2064,128]{1,0:T(8,128)(2,1)} %get-tuple-element.15.refs_3_), channel_id=1, source_target_pairs={{0,2},{1,3},{2,0},{3,1},{4,6},{5,7},{6,4},{7,5},{8,10},{9,11},{10,... | collective-permute-start | bytes 1585160 | tf_op jit(solution)/shard_map/ppermute | solution.py:86
  8.9 25.5 %collective-permute-start.4 = (bf16[2064,128]{1,0:T(8,128)(2,1)}, bf16[2064,128]{1,0:T(8,128)(2,1)}, u32[]{:S(2)}, u32[]{:S(2)}) collective-permute-start(bf16[2064,128]{1,0:T(8,128)(2,1)} %get-tuple-element.14), channel_id=1, source_target_pairs={{0,12},{1,13},{2,14},{3,15},{4,8},{5,9},{6,10},{7,11},{8,4},{9,5},... | collective-permute-start | bytes 1585160 | tf_op jit(solution)/shard_map/ppermute | solution.py:86
  31.7 14.1 %collective-permute-start.2 = (bf16[2064,128]{1,0:T(8,128)(2,1)}, bf16[2064,128]{1,0:T(8,128)(2,1)}, u32[]{:S(2)}, u32[]{:S(2)}) collective-permute-start(bf16[2064,128]{1,0:T(8,128)(2,1)} %collective-permute-done.1.refs_5_), channel_id=1, source_target_pairs={{0,2},{1,3},{2,0},{3,1},{4,6},{5,7},{6,4},{7,5},{8,10},{9,11},{10,... | collective-permute-start | bytes 1585160 | tf_op jit(solution)/shard_map/ppermute | solution.py:86
  32.2 47.4 %copy-start.6 = (s32[4]{0:T(128)S(1)}, s32[4]{0:T(128)}, u32[]{:S(2)}) copy-start(s32[4]{0:T(128)} %constant.63.clone.1.rows_ref) | copy-start | bytes 52
  32.2 24.9 %collective-permute-start.3 = (bf16[2064,128]{1,0:T(8,128)(2,1)}, bf16[2064,128]{1,0:T(8,128)(2,1)}, u32[]{:S(2)}, u32[]{:S(2)}) collective-permute-start(bf16[2064,128]{1,0:T(8,128)(2,1)} %get-tuple-element.15.refs_3_), channel_id=1, source_target_pairs={{0,8},{1,9},{2,10},{3,11},{4,12},{5,13},{6,14},{7,15},{8,0},{9,1},... | collective-permute-start | bytes 1585160 | tf_op jit(solution)/shard_map/ppermute | solution.py:86
  45.7 11.5 %collective-permute-start.5 = (bf16[2064,128]{1,0:T(8,128)(2,1)}, bf16[2064,128]{1,0:T(8,128)(2,1)S(1)}, u32[]{:S(2)}, u32[]{:S(2)}) collective-permute-start(bf16[2064,128]{1,0:T(8,128)(2,1)} %collective-permute-done.4.refs_9_), channel_id=1, source_target_pairs={{0,2},{1,3},{2,0},{3,1},{4,6},{5,7},{6,4},{7,5},{8,10},{9,11},{10,... | collective-permute-start | bytes 1585160 | tf_op jit(solution)/shard_map/ppermute | solution.py:86
  47.3 32.2 %collective-permute-start.8 = (bf16[256,2048]{1,0:T(8,128)(2,1)}, bf16[256,2048]{1,0:T(8,128)(2,1)}, u32[]{:S(2)}, u32[]{:S(2)}) collective-permute-start(bf16[256,2048]{1,0:T(8,128)(2,1)} %pad_maximum_fusion), channel_id=1, source_target_pairs={{0,4},{1,5},{2,6},{3,7},{4,0},{5,1},{6,2},{7,3},{8,12},{9,13},{10,... | collective-permute-start | bytes 3145736 | tf_op jit(solution)/shard_map/ppermute | solution.py:86
  57.2 0.8 copy-start.3
  58.0 21.6 %collective-permute-start.6 = (bf16[2064,128]{1,0:T(8,128)(2,1)}, bf16[2064,128]{1,0:T(8,128)(2,1)}, u32[]{:S(2)}, u32[]{:S(2)}) collective-permute-start(bf16[2064,128]{1,0:T(8,128)(2,1)} %collective-permute-done.3.refs_7_), channel_id=1, source_target_pairs={{0,2},{1,3},{2,0},{3,1},{4,6},{5,7},{6,4},{7,5},{8,10},{9,11},{10,... | collective-permute-start | bytes 1585160 | tf_op jit(solution)/shard_map/ppermute | solution.py:86
  79.6 1.0 copy-start.4
  86.9 2.7 %collective-permute-start.9 = (f32[4,128,512]{2,1,0:T(8,128)S(1)}, f32[4,128,512]{2,1,0:T(8,128)S(1)}, u32[]{:S(2)}, u32[]{:S(2)}) collective-permute-start(f32[4,128,512]{2,1,0:T(8,128)S(1)} %get-tuple-element.20), channel_id=1, source_target_pairs={{0,1},{1,0},{2,3},{3,2},{4,5},{5,4},{6,7},{7,6},{8,9},{9,8},{10,11... | collective-permute-start | bytes 3145736 | tf_op jit(solution)/shard_map/ppermute | solution.py:332
  89.7 5.8 %copy-start.8 = (s32[128]{0:T(128)S(1)}, s32[128]{0:T(128)}, u32[]{:S(2)}) copy-start(s32[128]{0:T(128)} %param.9) | copy-start | bytes 1540
  91.1 13.8 %all-to-all-start = ((bf16[4,128,768]{2,1,0:T(8,128)(2,1)}), bf16[4,128,768]{2,1,0:T(8,128)(2,1)S(1)}, u32[]{:S(2)}, u32[]{:S(2)}) async-start(bf16[4,128,768]{2,1,0:T(8,128)(2,1)} %split.1), calls=%async_computation | async-start | bytes 1572864 | tf_op jit(solution)/shard_map/all_to_all | solution.py:333
  94.6 36.0 %copy-start.2 = (bf16[128,4096]{1,0:T(8,128)(2,1)S(1)}, bf16[128,4096]{1,0:T(8,128)(2,1)}, u32[]{:S(2)}) copy-start(bf16[128,4096]{1,0:T(8,128)(2,1)} %query_ref.1) | copy-start | bytes 3145732
  105.5 6.9 %collective-permute-start.10 = (bf16[128,512]{1,0:T(8,128)(2,1)S(1)}, bf16[128,512]{1,0:T(8,128)(2,1)S(1)}, u32[]{:S(2)}, u32[]{:S(2)}) collective-permute-start(bf16[128,512]{1,0:T(8,128)(2,1)S(1)} %fusion.refs_0_), channel_id=1, source_target_pairs={{0,2},{1,3},{2,4},{3,5},{4,6},{5,7},{6,8},{7,9},{8,10},{9,11},{10,... | collective-permute-start | bytes 393224 | tf_op jit(solution)/shard_map/ppermute | solution.py:355
  106.8 9.0 %collective-permute-start.11 = (bf16[128,512]{1,0:T(8,128)(2,1)S(1)}, bf16[128,512]{1,0:T(8,128)(2,1)S(1)}, u32[]{:S(2)}, u32[]{:S(2)}) collective-permute-start(bf16[128,512]{1,0:T(8,128)(2,1)S(1)} %fusion.refs_0_), channel_id=1, source_target_pairs={{0,4},{1,5},{2,6},{3,7},{4,8},{5,9},{6,10},{7,11},{8,12},{9,13},{1... | collective-permute-start | bytes 393224 | tf_op jit(solution)/shard_map/ppermute | solution.py:355
  108.1 10.7 %collective-permute-start.12 = (bf16[128,512]{1,0:T(8,128)(2,1)S(1)}, bf16[128,512]{1,0:T(8,128)(2,1)S(1)}, u32[]{:S(2)}, u32[]{:S(2)}) collective-permute-start(bf16[128,512]{1,0:T(8,128)(2,1)S(1)} %fusion.refs_0_), channel_id=1, source_target_pairs={{0,6},{1,7},{2,8},{3,9},{4,10},{5,11},{6,12},{7,13},{8,14},{9,15},... | collective-permute-start | bytes 393224 | tf_op jit(solution)/shard_map/ppermute | solution.py:355
  109.4 21.0 %collective-permute-start.13 = (bf16[128,512]{1,0:T(8,128)(2,1)S(1)}, bf16[128,512]{1,0:T(8,128)(2,1)S(1)}, u32[]{:S(2)}, u32[]{:S(2)}) collective-permute-start(bf16[128,512]{1,0:T(8,128)(2,1)S(1)} %fusion.refs_0_), channel_id=1, source_target_pairs={{0,8},{1,9},{2,10},{3,11},{4,12},{5,13},{6,14},{7,15},{16,24},{17,... | collective-permute-start | bytes 393224 | tf_op jit(solution)/shard_map/ppermute | solution.py:355
  110.7 19.9 %collective-permute-start.14 = (bf16[128,512]{1,0:T(8,128)(2,1)S(1)}, bf16[128,512]{1,0:T(8,128)(2,1)S(1)}, u32[]{:S(2)}, u32[]{:S(2)}) collective-permute-start(bf16[128,512]{1,0:T(8,128)(2,1)S(1)} %fusion.refs_0_), channel_id=1, source_target_pairs={{0,10},{1,11},{2,12},{3,13},{4,14},{5,15},{16,26},{17,27},{18,28},... | collective-permute-start | bytes 393224 | tf_op jit(solution)/shard_map/ppermute | solution.py:355

commit v3 on v2

--- a/solution.py
+++ b/solution.py
@@ -37,39 +37,46 @@
     return pairs
 
 
-def scale_kernel(first_ref, codes_ref, scales_ref, ids_ref, near_ref, far_ref):
+def scale_kernel(first_ref, codes_ref, scales_ref, ids_ref, near_ref, far_ref, held, sems):
     depth = near_ref.shape[0] - PAD
     blocks = depth // BLK
     own, column, block = first_ref[0], first_ref[1], first_ref[2]
-    for out_ref, which in ((near_ref, own), (far_ref, 1 - own)):
-        for k in range(blocks):
-            row = pl.multiple_of((which * blocks + k) * BLK, BLK)
-            scale = scales_ref[column, block + which * blocks + k]
-            part = codes_ref[pl.ds(row, BLK), :].astype(jnp.float32) * scale
-            out_ref[k * BLK : (k + 1) * BLK, :] = part.astype(jnp.bfloat16)
-        ids = ids_ref[...].astype(jnp.float32)
-        out_ref[depth:, :] = jnp.broadcast_to(ids, (PAD, ids.shape[1])).astype(jnp.bfloat16)
+    copies = []
+    for k, which in enumerate((1 - own, own)):
+        row = pl.multiple_of((block + which * blocks) * BLK, BLK)
+        copies.append(
+            pltpu.make_async_copy(codes_ref.at[pl.ds(row, depth), :], held.at[k], sems.at[k])
+        )
+        copies[k].start()
+    ids = ids_ref[...].astype(jnp.float32)
+    ids = jnp.broadcast_to(ids, (PAD, ids.shape[1])).astype(jnp.bfloat16)
+    for k, (out_ref, which) in enumerate(((far_ref, 1 - own), (near_ref, own))):
+        copies[k].wait()
+        for b in range(blocks):
+            scale = scales_ref[column, block + which * blocks + b]
+            part = held[k, b * BLK : (b + 1) * BLK, :].astype(jnp.float32) * scale
+            out_ref[b * BLK : (b + 1) * BLK, :] = part.astype(jnp.bfloat16)
+        out_ref[depth:, :] = ids
 
 
 def scaled_weight(codes, scales, segment_ids, depth, group, zz, column):
     width = codes.shape[1]
-    share = 2 * depth
-    first = jnp.stack([zz, column, group * (share // BLK), group]).astype(jnp.int32)
+    first = jnp.stack([zz, column, group * (2 * depth // BLK)]).astype(jnp.int32)
     out = jax.ShapeDtypeStruct((depth + PAD, width), jnp.bfloat16)
-    whole = pl.BlockSpec((depth + PAD, width), lambda i, f: (0, 0))
     return pl.pallas_call(
         scale_kernel,
-        grid_spec=pltpu.PrefetchScalarGridSpec(
-            num_scalar_prefetch=1,
-            grid=(1,),
-            in_specs=[
-                pl.BlockSpec((share, width), lambda i, f: (f[3], 0)),
-                pl.BlockSpec(memory_space=pltpu.SMEM),
-                pl.BlockSpec((1, width), lambda i, f: (0, 0)),
-            ],
-            out_specs=[whole, whole],
-        ),
+        in_specs=[
+            pl.BlockSpec(memory_space=pltpu.SMEM),
+            pl.BlockSpec(memory_space=pltpu.HBM),
+            pl.BlockSpec(memory_space=pltpu.SMEM),
+            pl.BlockSpec(memory_space=pltpu.VMEM),
+        ],
+        out_specs=[pl.BlockSpec(memory_space=pltpu.VMEM)] * 2,
         out_shape=[out, out],
+        scratch_shapes=[
+            pltpu.VMEM((2, depth, width), jnp.bfloat16),
+            pltpu.SemaphoreType.DMA((2,)),
+        ],
         compiler_params=pltpu.CompilerParams(vmem_limit_bytes=8 * MIB),
         name="scale",
     )(first, codes, scales.T, segment_ids.reshape(1, -1))
@@ -88,17 +95,15 @@
     def along_shard(distance):
         return lambda g, s, c: (g, s ^ distance, c)
 
+    sent = lax.dynamic_slice_in_dim(hidden, (1 - group) * 2 * depth, 2 * depth, 1)
+    across = send(sent, lambda g, s, c: (1 - g, s, c))
     near, far = scaled_weight(
-        codes, scales, segment_ids, depth, group, zz, shard * codes.shape[1] // BLK
+        after(codes, sent), scales, segment_ids, depth, group, zz, shard * codes.shape[1] // BLK
     )
     piece = {0: near}
     piece[6] = send(far, along_shard(6))
     piece[2] = send(far, along_shard(2))
     piece[1] = send(near, along_shard(1))
-    sent = lax.dynamic_slice_in_dim(after(hidden, near), (1 - group) * 2 * depth, 2 * depth, 1)
-    across = send(sent, lambda g, s, c: (1 - g, s, c))
-    piece[4] = send(after(near, piece[2], piece[1]), along_shard(4))
-    piece[3] = send(piece[2], along_shard(1))
     pair = jnp.concatenate(
         [
             lax.dynamic_slice_in_dim(hidden, (group * 2 + 1 - zz) * depth, depth, 1),
@@ -106,7 +111,9 @@
         ],
         axis=0,
     )
+    piece[4] = send(after(near, pair, piece[2], piece[1]), along_shard(4))
     pair = send(pair, along_shard(2))
+    piece[3] = send(piece[2], along_shard(1))
     piece[7] = send(after(piece[6], piece[3]), along_shard(1))
     piece[5] = send(after(piece[4], piece[7]), along_shard(1))
     order = sorted(piece)

time: 138 us -> 130 us (0.942)
  waiting for transfers between devices: 85.4 us -> 77.9 us
  starting transfers between devices: 20.1 us -> 17.7 us
    ppermute x9, waiting for transfers between devices: 60.9 us -> 53.6 us  [send(): return lax.ppermute(value, ALL, flat_pairs(sizes, move))]
    ppermute x9, starting transfers between devices: 10.1 us -> 6.89 us  [send(): return lax.ppermute(value, ALL, flat_pairs(sizes, move))]
    unnamed x18 -> x16, local copies, waits for them, and re-layouts: 4.94 us -> 3.46 us
    dynamic_slice x1, local copies, waits for them, and re-layouts: 1.04 us -> 2.44 us  [gather_by_steps(): lax.dynamic_slice_in_dim(hidden, (1 - group) * 2 * depth, 2 * depth, 1)]
  transfers between devices with their start and end apart: 16 -> 16, of which waited for: 12 -> 12; matrix products, arithmetic and copies ran while one was open for 6% -> 8% of each run, Pallas kernels for 0% -> 1%
where the time goes in v3:
time: 130 us; the launch traced here: 129 us
  waiting for transfers between devices  77.9 us (60%)
  starting transfers between devices  17.7 us (14%)
  Pallas kernels  16.5 us (13%)
  local copies, waits for them, and re-layouts  13.8 us (11%)
  other arithmetic  2.81 us (2%)
    ppermute x9, waiting for transfers between devices, send(): return lax.ppermute(value, ALL, flat_pairs(sizes, move))  53.6 us
    ppermute x5, waiting for transfers between devices, on_device(): pieces.append(lax.ppermute(keyval, ALL, up))  17.9 us
    ppermute x9, starting transfers between devices, send(): return lax.ppermute(value, ALL, flat_pairs(sizes, move))  6.89 us
    pallas_call x1, Pallas kernels, attend(): pl.pallas_call(functools.partial(attend_kernel, len(pieces), QPK, stack),...  6.88 us
    ppermute x5, starting transfers between devices, on_device(): pieces.append(lax.ppermute(keyval, ALL, up))  6.46 us
    pallas_call x1, Pallas kernels, project(): pl.pallas_call(functools.partial(project_kernel, [c[0] for c in copies],...  6.32 us
    slice x8, local copies, waits for them, and re-layouts, gather_by_steps(): ids = [piece[d][depth:depth + 1] for d in order]  5.41 us
    all_to_all x1, starting transfers between devices, on_device(): partial = lax.all_to_all(partial, BLOCK, 0, 0, tiled=True)  4.3 us
  transfers between devices with their start and end apart: 16, of which 12 were waited for; matrix products, arithmetic and copies ran while one was open for 8% of the time, Pallas kernels for 1%

profile of v3, /device:TPU:28, one launch (start us, length us, event | category | flops | bytes accessed | tf_op | source)
XLA Modules:
  0.0 129.0 jit_solution(14985437270247040412)
XLA Ops:
  0.0 2.4 %constant_dynamic-slice_fusion.2 = bf16[128,4096]{1,0:T(8,128)(2,1)} fusion(bf16[128,8192]{1,0:T(8,128)(2,1)} %refs_0_.1, s32[]{:T(128)S(6)} %select_n.26), kind=kLoop, calls=%fused_computation.14 | loop fusion | bytes 2097156 | tf_op jit(solution)/shard_map/dynamic_slice | solution.py:98
  2.5 1.5 %collective-permute-start.3 = (bf16[128,4096]{1,0:T(8,128)(2,1)}, bf16[128,4096]{1,0:T(8,128)(2,1)S(1)}, u32[]{:S(2)}, u32[]{:S(2)}) collective-permute-start(bf16[128,4096]{1,0:T(8,128)(2,1)} %constant_dynamic-slice_fusion.2), channel_id=1, source_target_pairs={{0,16},{1,17},{2,18},{3,19},{4,20},{5,21},{6,22},{7,23},{8,24},{9,... | collective-permute-start | bytes 3145736 | tf_op jit(solution)/shard_map/ppermute | solution.py:93
  4.0 1.6 %copy-done.1 = bf16[8192,128]{1,0:T(8,128)(2,1)S(1)} copy-done((bf16[8192,128]{1,0:T(8,128)(2,1)S(1)}, bf16[8192,128]{1,0:T(8,128)(2,1)}, u32[]{:S(2)}) %copy-start.1) | copy-done | bytes 2097176
  5.6 1.8 %scale.1 = (bf16[2064,128]{1,0:T(8,128)(2,1)}, bf16[2064,128]{1,0:T(8,128)(2,1)}) custom-call(s32[3]{0:T(128)S(1)} %pad_add_fusion.first_ref, bf16[8192,128]{1,0:T(8,128)(2,1)S(1)} %copy-done.1, f32[8,64]{1,0:T(8,128)S(1)} %bitcast.30, s32[1,128]{1,0:T(1,128)S(1)} %bitcast.31), custom_call_target="tpu_custom_call" | custom-call | tf_op jit(solution)/shard_map/scale/pallas_call | solution.py:66
  7.9 1.3 %collective-permute-start.5 = (bf16[2064,128]{1,0:T(8,128)(2,1)}, bf16[2064,128]{1,0:T(8,128)(2,1)}, u32[]{:S(2)}, u32[]{:S(2)}) collective-permute-start(bf16[2064,128]{1,0:T(8,128)(2,1)} %get-tuple-element.15), channel_id=1, source_target_pairs={{0,12},{1,13},{2,14},{3,15},{4,8},{5,9},{6,10},{7,11},{8,4},{9,5},... | collective-permute-start | bytes 1585160 | tf_op jit(solution)/shard_map/ppermute | solution.py:93
  9.8 22.8 %collective-permute-done.1.refs_5_ = bf16[2064,128]{1,0:T(8,128)(2,1)} collective-permute-done((bf16[2064,128]{1,0:T(8,128)(2,1)}, bf16[2064,128]{1,0:T(8,128)(2,1)}, u32[]{:S(2)}, u32[]{:S(2)}) %collective-permute-start.1) | collective-permute-done | bytes 528416 | tf_op jit(solution)/shard_map/ppermute | solution.py:93
  33.1 0.9 constant_dynamic-slice_fusion.1
  34.0 2.2 %pad_maximum_fusion = bf16[256,2048]{1,0:T(8,128)(2,1)} fusion(bf16[128,2048]{1,0:T(8,128)(2,1)S(1)} %constant_dynamic-slice_fusion, bf16[128,2048]{1,0:T(8,128)(2,1)} %constant_dynamic-slice_fusion.1), kind=kLoop, calls=%fused_computation.3 | loop fusion | flops 2097152 | bytes 2097152 | tf_op jit(solution)/shard_map/concatenate | solution.py:107
  36.2 9.1 %collective-permute-done.2.refs_6_ = bf16[2064,128]{1,0:T(8,128)(2,1)} collective-permute-done((bf16[2064,128]{1,0:T(8,128)(2,1)}, bf16[2064,128]{1,0:T(8,128)(2,1)}, u32[]{:S(2)}, u32[]{:S(2)}) %collective-permute-start.2) | collective-permute-done | bytes 528416 | tf_op jit(solution)/shard_map/ppermute | solution.py:93
  45.8 1.5 %collective-permute-start.8 = (bf16[256,2048]{1,0:T(8,128)(2,1)}, bf16[256,2048]{1,0:T(8,128)(2,1)}, u32[]{:S(2)}, u32[]{:S(2)}) collective-permute-start(bf16[256,2048]{1,0:T(8,128)(2,1)} %pad_maximum_fusion), channel_id=1, source_target_pairs={{0,4},{1,5},{2,6},{3,7},{4,0},{5,1},{6,2},{7,3},{8,12},{9,13},{10,... | collective-permute-start | bytes 3145736 | tf_op jit(solution)/shard_map/ppermute | solution.py:93
  47.3 9.2 %collective-permute-done.4.refs_7_ = bf16[2064,128]{1,0:T(8,128)(2,1)} collective-permute-done((bf16[2064,128]{1,0:T(8,128)(2,1)}, bf16[2064,128]{1,0:T(8,128)(2,1)}, u32[]{:S(2)}, u32[]{:S(2)}) %collective-permute-start.4) | collective-permute-done | bytes 528416 | tf_op jit(solution)/shard_map/ppermute | solution.py:93
  56.5 0.8 copy-done.3
  58.0 10.0 %collective-permute-done.8.refs_2_ = bf16[256,2048]{1,0:T(8,128)(2,1)} collective-permute-done((bf16[256,2048]{1,0:T(8,128)(2,1)}, bf16[256,2048]{1,0:T(8,128)(2,1)}, u32[]{:S(2)}, u32[]{:S(2)}) %collective-permute-start.8) | collective-permute-done | bytes 1048608 | tf_op jit(solution)/shard_map/ppermute | solution.py:93
  68.0 2.5 %collective-permute-done.7.refs_8_ = bf16[2064,128]{1,0:T(8,128)(2,1)} collective-permute-done((bf16[2064,128]{1,0:T(8,128)(2,1)}, bf16[2064,128]{1,0:T(8,128)(2,1)}, u32[]{:S(2)}, u32[]{:S(2)}) %collective-permute-start.7) | collective-permute-done | bytes 528416 | tf_op jit(solution)/shard_map/ppermute | solution.py:93
  70.5 1.0 copy-done.4
  71.5 6.3 %project.1 = (f32[4,128,512]{2,1,0:T(8,128)S(1)}, f32[4,128,512]{2,1,0:T(8,128)S(1)}) custom-call(s32[4]{0:T(128)S(1)} %copy-done.6, s32[4]{0:T(128)S(1)} %get-tuple-element.21.first_ref, s32[4]{0:T(128)S(1)} %get-tuple-element.22.member_ref, s32[8]{0:T(128)S(1)} %stack.83.shard_ref, s32[1]{0:T(128)} %bitcast.23.core_ref, bf16[128,8192]{1,0:T(8,128)(2,1)S(1)} %copy-done, ...), custom_call_target="tpu_custom_call" | custom-call | tf_op jit(solution)/shard_map/project/pallas_call | solution.py:234
  77.9 2.6 %collective-permute-done.9.got_ref = f32[4,128,512]{2,1,0:T(8,128)S(1)} collective-permute-done((f32[4,128,512]{2,1,0:T(8,128)S(1)}, f32[4,128,512]{2,1,0:T(8,128)S(1)}, u32[]{:S(2)}, u32[]{:S(2)}) %collective-permute-start.9) | collective-permute-done | bytes 1048608 | tf_op jit(solution)/shard_map/ppermute | solution.py:339
  80.6 1.5 %split.1 = bf16[4,128,768]{2,1,0:T(8,128)(2,1)} custom-call(f32[4,128,512]{2,1,0:T(8,128)S(1)} %get-tuple-element.19.mine_ref, f32[4,128,512]{2,1,0:T(8,128)S(1)} %collective-permute-done.9.got_ref), custom_call_target="tpu_custom_call" | custom-call | tf_op jit(solution)/shard_map/split/pallas_call | solution.py:271
  82.1 4.3 %all-to-all-start = ((bf16[4,128,768]{2,1,0:T(8,128)(2,1)}), bf16[4,128,768]{2,1,0:T(8,128)(2,1)S(1)}, u32[]{:S(2)}, u32[]{:S(2)}) async-start(bf16[4,128,768]{2,1,0:T(8,128)(2,1)} %split.1), calls=%async_computation | async-start | bytes 1572864 | tf_op jit(solution)/shard_map/all_to_all | solution.py:340
  86.4 0.8 slice.30
  90.0 0.7 slice.47
  90.7 0.7 slice.50
  93.2 3.7 %all-to-all-done = bf16[4,128,768]{2,1,0:T(8,128)(2,1)S(1)} async-done(((bf16[4,128,768]{2,1,0:T(8,128)(2,1)}), bf16[4,128,768]{2,1,0:T(8,128)(2,1)S(1)}, u32[]{:S(2)}, u32[]{:S(2)}) %all-to-all-start) | async-done | bytes 786464 | tf_op jit(solution)/shard_map/all_to_all | solution.py:340
  97.5 1.3 %collective-permute-start.10 = (bf16[128,512]{1,0:T(8,128)(2,1)S(1)}, bf16[128,512]{1,0:T(8,128)(2,1)S(1)}, u32[]{:S(2)}, u32[]{:S(2)}) collective-permute-start(bf16[128,512]{1,0:T(8,128)(2,1)S(1)} %fusion.refs_0_), channel_id=1, source_target_pairs={{0,2},{1,3},{2,4},{3,5},{4,6},{5,7},{6,8},{7,9},{8,10},{9,11},{10,... | collective-permute-start | bytes 393224 | tf_op jit(solution)/shard_map/ppermute | solution.py:362
  98.8 1.3 %collective-permute-start.11 = (bf16[128,512]{1,0:T(8,128)(2,1)S(1)}, bf16[128,512]{1,0:T(8,128)(2,1)S(1)}, u32[]{:S(2)}, u32[]{:S(2)}) collective-permute-start(bf16[128,512]{1,0:T(8,128)(2,1)S(1)} %fusion.refs_0_), channel_id=1, source_target_pairs={{0,4},{1,5},{2,6},{3,7},{4,8},{5,9},{6,10},{7,11},{8,12},{9,13},{1... | collective-permute-start | bytes 393224 | tf_op jit(solution)/shard_map/ppermute | solution.py:362
  100.1 1.3 %collective-permute-start.12 = (bf16[128,512]{1,0:T(8,128)(2,1)S(1)}, bf16[128,512]{1,0:T(8,128)(2,1)S(1)}, u32[]{:S(2)}, u32[]{:S(2)}) collective-permute-start(bf16[128,512]{1,0:T(8,128)(2,1)S(1)} %fusion.refs_0_), channel_id=1, source_target_pairs={{0,6},{1,7},{2,8},{3,9},{4,10},{5,11},{6,12},{7,13},{8,14},{9,15},... | collective-permute-start | bytes 393224 | tf_op jit(solution)/shard_map/ppermute | solution.py:362
  101.4 1.3 %collective-permute-start.13 = (bf16[128,512]{1,0:T(8,128)(2,1)S(1)}, bf16[128,512]{1,0:T(8,128)(2,1)S(1)}, u32[]{:S(2)}, u32[]{:S(2)}) collective-permute-start(bf16[128,512]{1,0:T(8,128)(2,1)S(1)} %fusion.refs_0_), channel_id=1, source_target_pairs={{0,8},{1,9},{2,10},{3,11},{4,12},{5,13},{6,14},{7,15},{16,24},{17,... | collective-permute-start | bytes 393224 | tf_op jit(solution)/shard_map/ppermute | solution.py:362
  102.7 1.3 %collective-permute-start.14 = (bf16[128,512]{1,0:T(8,128)(2,1)S(1)}, bf16[128,512]{1,0:T(8,128)(2,1)S(1)}, u32[]{:S(2)}, u32[]{:S(2)}) collective-permute-start(bf16[128,512]{1,0:T(8,128)(2,1)S(1)} %fusion.refs_0_), channel_id=1, source_target_pairs={{0,10},{1,11},{2,12},{3,13},{4,14},{5,15},{16,26},{17,27},{18,28},... | collective-permute-start | bytes 393224 | tf_op jit(solution)/shard_map/ppermute | solution.py:362
  104.4 3.5 %collective-permute-done.11.refs_2_ = bf16[128,512]{1,0:T(8,128)(2,1)S(1)} collective-permute-done((bf16[128,512]{1,0:T(8,128)(2,1)S(1)}, bf16[128,512]{1,0:T(8,128)(2,1)S(1)}, u32[]{:S(2)}, u32[]{:S(2)}) %collective-permute-start.11) | collective-permute-done | bytes 131104 | tf_op jit(solution)/shard_map/ppermute | solution.py:362
  107.8 2.9 %collective-permute-done.12.refs_3_ = bf16[128,512]{1,0:T(8,128)(2,1)S(1)} collective-permute-done((bf16[128,512]{1,0:T(8,128)(2,1)S(1)}, bf16[128,512]{1,0:T(8,128)(2,1)S(1)}, u32[]{:S(2)}, u32[]{:S(2)}) %collective-permute-start.12) | collective-permute-done | bytes 131104 | tf_op jit(solution)/shard_map/ppermute | solution.py:362
  110.8 11.0 %collective-permute-done.13.refs_4_ = bf16[128,512]{1,0:T(8,128)(2,1)S(1)} collective-permute-done((bf16[128,512]{1,0:T(8,128)(2,1)S(1)}, bf16[128,512]{1,0:T(8,128)(2,1)S(1)}, u32[]{:S(2)}, u32[]{:S(2)}) %collective-permute-start.13) | collective-permute-done | bytes 131104 | tf_op jit(solution)/shard_map/ppermute | solution.py:362
  122.1 6.9 %attend.1 = bf16[128,4096]{1,0:T(8,128)(2,1)} custom-call(bf16[128,4096]{1,0:T(8,128)(2,1)S(1)} %copy-done.2, f32[128,768]{1,0:T(8,128)S(1)} %and_convert_fusion.allowed_ref, bf16[128,512]{1,0:T(8,128)(2,1)S(1)} %fusion.refs_0_, bf16[128,512]{1,0:T(8,128)(2,1)S(1)} %collective-permute-done.10.refs_1_, bf16[128,512]{1,0:T(8,128)(2,1)S(1)} %collective-permute-done.11.refs_2_, ...), custom_call_target="tpu_custom_call" | custom-call | tf_op jit(solution)/shard_map/attend/pallas_call | solution.py:313
  (55 shorter events, 8.8 us)
Async XLA Ops:
  0.0 4.0 %copy-start.5 = (f32[64,8]{0,1:T(8,128)S(1)}, f32[64,8]{0,1:T(8,128)}, u32[]{:S(2)}) copy-start(f32[64,8]{0,1:T(8,128)} %param.7) | copy-start | bytes 6148
  0.0 4.0 %copy-start.7 = (s32[128]{0:T(128)S(1)}, s32[128]{0:T(128)}, u32[]{:S(2)}) copy-start(s32[128]{0:T(128)} %param.9) | copy-start | bytes 1540
  0.0 33.1 %copy-start = (bf16[128,8192]{1,0:T(8,128)(2,1)S(1)}, bf16[128,8192]{1,0:T(8,128)(2,1)}, u32[]{:S(2)}) copy-start(bf16[128,8192]{1,0:T(8,128)(2,1)} %refs_0_.1) | copy-start | bytes 6291460
  2.5 31.5 %collective-permute-start.3 = (bf16[128,4096]{1,0:T(8,128)(2,1)}, bf16[128,4096]{1,0:T(8,128)(2,1)S(1)}, u32[]{:S(2)}, u32[]{:S(2)}) collective-permute-start(bf16[128,4096]{1,0:T(8,128)(2,1)} %constant_dynamic-slice_fusion.2), channel_id=1, source_target_pairs={{0,16},{1,17},{2,18},{3,19},{4,20},{5,21},{6,22},{7,23},{8,24},{9,... | collective-permute-start | bytes 3145736 | tf_op jit(solution)/shard_map/ppermute | solution.py:93
  4.0 1.6 %copy-start.1 = (bf16[8192,128]{1,0:T(8,128)(2,1)S(1)}, bf16[8192,128]{1,0:T(8,128)(2,1)}, u32[]{:S(2)}) copy-start(bf16[8192,128]{1,0:T(8,128)(2,1)} %codes_ref) | copy-start | bytes 6291460
  7.4 25.2 %collective-permute-start.1 = (bf16[2064,128]{1,0:T(8,128)(2,1)}, bf16[2064,128]{1,0:T(8,128)(2,1)}, u32[]{:S(2)}, u32[]{:S(2)}) collective-permute-start(bf16[2064,128]{1,0:T(8,128)(2,1)} %get-tuple-element.15), channel_id=1, source_target_pairs={{0,4},{1,5},{2,6},{3,7},{4,0},{5,1},{6,2},{7,3},{8,12},{9,13},{10,... | collective-permute-start | bytes 1585160 | tf_op jit(solution)/shard_map/ppermute | solution.py:93
  7.9 28.3 %collective-permute-start.5 = (bf16[2064,128]{1,0:T(8,128)(2,1)}, bf16[2064,128]{1,0:T(8,128)(2,1)}, u32[]{:S(2)}, u32[]{:S(2)}) collective-permute-start(bf16[2064,128]{1,0:T(8,128)(2,1)} %get-tuple-element.15), channel_id=1, source_target_pairs={{0,12},{1,13},{2,14},{3,15},{4,8},{5,9},{6,10},{7,11},{8,4},{9,5},... | collective-permute-start | bytes 1585160 | tf_op jit(solution)/shard_map/ppermute | solution.py:93
  9.3 26.9 %collective-permute-start = (bf16[2064,128]{1,0:T(8,128)(2,1)}, bf16[2064,128]{1,0:T(8,128)(2,1)}, u32[]{:S(2)}, u32[]{:S(2)}) collective-permute-start(bf16[2064,128]{1,0:T(8,128)(2,1)} %get-tuple-element.16.refs_3_), channel_id=1, source_target_pairs={{0,2},{1,3},{2,0},{3,1},{4,6},{5,7},{6,4},{7,5},{8,10},{9,11},{10,... | collective-permute-start | bytes 1585160 | tf_op jit(solution)/shard_map/ppermute | solution.py:93
  9.8 60.7 %copy-start.6 = (s32[4]{0:T(128)S(1)}, s32[4]{0:T(128)}, u32[]{:S(2)}) copy-start(s32[4]{0:T(128)} %constant.66.clone.1.rows_ref) | copy-start | bytes 52
  32.6 12.7 %collective-permute-start.2 = (bf16[2064,128]{1,0:T(8,128)(2,1)}, bf16[2064,128]{1,0:T(8,128)(2,1)}, u32[]{:S(2)}, u32[]{:S(2)}) collective-permute-start(bf16[2064,128]{1,0:T(8,128)(2,1)} %collective-permute-done.1.refs_5_), channel_id=1, source_target_pairs={{0,2},{1,3},{2,0},{3,1},{4,6},{5,7},{6,4},{7,5},{8,10},{9,11},{10,... | collective-permute-start | bytes 1585160 | tf_op jit(solution)/shard_map/ppermute | solution.py:93
  36.2 20.3 %collective-permute-start.4 = (bf16[2064,128]{1,0:T(8,128)(2,1)}, bf16[2064,128]{1,0:T(8,128)(2,1)}, u32[]{:S(2)}, u32[]{:S(2)}) collective-permute-start(bf16[2064,128]{1,0:T(8,128)(2,1)} %get-tuple-element.16.refs_3_), channel_id=1, source_target_pairs={{0,8},{1,9},{2,10},{3,11},{4,12},{5,13},{6,14},{7,15},{8,0},{9,1},... | collective-permute-start | bytes 1585160 | tf_op jit(solution)/shard_map/ppermute | solution.py:93
  45.3 11.2 %collective-permute-start.6 = (bf16[2064,128]{1,0:T(8,128)(2,1)}, bf16[2064,128]{1,0:T(8,128)(2,1)S(1)}, u32[]{:S(2)}, u32[]{:S(2)}) collective-permute-start(bf16[2064,128]{1,0:T(8,128)(2,1)} %collective-permute-done.5.refs_9_), channel_id=1, source_target_pairs={{0,2},{1,3},{2,0},{3,1},{4,6},{5,7},{6,4},{7,5},{8,10},{9,11},{10,... | collective-permute-start | bytes 1585160 | tf_op jit(solution)/shard_map/ppermute | solution.py:93
  45.8 22.2 %collective-permute-start.8 = (bf16[256,2048]{1,0:T(8,128)(2,1)}, bf16[256,2048]{1,0:T(8,128)(2,1)}, u32[]{:S(2)}, u32[]{:S(2)}) collective-permute-start(bf16[256,2048]{1,0:T(8,128)(2,1)} %pad_maximum_fusion), channel_id=1, source_target_pairs={{0,4},{1,5},{2,6},{3,7},{4,0},{5,1},{6,2},{7,3},{8,12},{9,13},{10,... | collective-permute-start | bytes 3145736 | tf_op jit(solution)/shard_map/ppermute | solution.py:93
  56.5 0.8 copy-start.3
  57.3 13.2 %collective-permute-start.7 = (bf16[2064,128]{1,0:T(8,128)(2,1)}, bf16[2064,128]{1,0:T(8,128)(2,1)}, u32[]{:S(2)}, u32[]{:S(2)}) collective-permute-start(bf16[2064,128]{1,0:T(8,128)(2,1)} %collective-permute-done.4.refs_7_), channel_id=1, source_target_pairs={{0,2},{1,3},{2,0},{3,1},{4,6},{5,7},{6,4},{7,5},{8,10},{9,11},{10,... | collective-permute-start | bytes 1585160 | tf_op jit(solution)/shard_map/ppermute | solution.py:93
  70.5 1.0 copy-start.4
  77.9 2.7 %collective-permute-start.9 = (f32[4,128,512]{2,1,0:T(8,128)S(1)}, f32[4,128,512]{2,1,0:T(8,128)S(1)}, u32[]{:S(2)}, u32[]{:S(2)}) collective-permute-start(f32[4,128,512]{2,1,0:T(8,128)S(1)} %get-tuple-element.20), channel_id=1, source_target_pairs={{0,1},{1,0},{2,3},{3,2},{4,5},{5,4},{6,7},{7,6},{8,9},{9,8},{10,11... | collective-permute-start | bytes 3145736 | tf_op jit(solution)/shard_map/ppermute | solution.py:339
  82.1 14.8 %all-to-all-start = ((bf16[4,128,768]{2,1,0:T(8,128)(2,1)}), bf16[4,128,768]{2,1,0:T(8,128)(2,1)S(1)}, u32[]{:S(2)}, u32[]{:S(2)}) async-start(bf16[4,128,768]{2,1,0:T(8,128)(2,1)} %split.1), calls=%async_computation | async-start | bytes 1572864 | tf_op jit(solution)/shard_map/all_to_all | solution.py:340
  86.4 35.7 %copy-start.2 = (bf16[128,4096]{1,0:T(8,128)(2,1)S(1)}, bf16[128,4096]{1,0:T(8,128)(2,1)}, u32[]{:S(2)}) copy-start(bf16[128,4096]{1,0:T(8,128)(2,1)} %query_ref.1) | copy-start | bytes 3145732
  97.5 6.9 %collective-permute-start.10 = (bf16[128,512]{1,0:T(8,128)(2,1)S(1)}, bf16[128,512]{1,0:T(8,128)(2,1)S(1)}, u32[]{:S(2)}, u32[]{:S(2)}) collective-permute-start(bf16[128,512]{1,0:T(8,128)(2,1)S(1)} %fusion.refs_0_), channel_id=1, source_target_pairs={{0,2},{1,3},{2,4},{3,5},{4,6},{5,7},{6,8},{7,9},{8,10},{9,11},{10,... | collective-permute-start | bytes 393224 | tf_op jit(solution)/shard_map/ppermute | solution.py:362
  98.8 9.0 %collective-permute-start.11 = (bf16[128,512]{1,0:T(8,128)(2,1)S(1)}, bf16[128,512]{1,0:T(8,128)(2,1)S(1)}, u32[]{:S(2)}, u32[]{:S(2)}) collective-permute-start(bf16[128,512]{1,0:T(8,128)(2,1)S(1)} %fusion.refs_0_), channel_id=1, source_target_pairs={{0,4},{1,5},{2,6},{3,7},{4,8},{5,9},{6,10},{7,11},{8,12},{9,13},{1... | collective-permute-start | bytes 393224 | tf_op jit(solution)/shard_map/ppermute | solution.py:362
  100.1 10.7 %collective-permute-start.12 = (bf16[128,512]{1,0:T(8,128)(2,1)S(1)}, bf16[128,512]{1,0:T(8,128)(2,1)S(1)}, u32[]{:S(2)}, u32[]{:S(2)}) collective-permute-start(bf16[128,512]{1,0:T(8,128)(2,1)S(1)} %fusion.refs_0_), channel_id=1, source_target_pairs={{0,6},{1,7},{2,8},{3,9},{4,10},{5,11},{6,12},{7,13},{8,14},{9,15},... | collective-permute-start | bytes 393224 | tf_op jit(solution)/shard_map/ppermute | solution.py:362
  101.4 20.3 %collective-permute-start.13 = (bf16[128,512]{1,0:T(8,128)(2,1)S(1)}, bf16[128,512]{1,0:T(8,128)(2,1)S(1)}, u32[]{:S(2)}, u32[]{:S(2)}) collective-permute-start(bf16[128,512]{1,0:T(8,128)(2,1)S(1)} %fusion.refs_0_), channel_id=1, source_target_pairs={{0,8},{1,9},{2,10},{3,11},{4,12},{5,13},{6,14},{7,15},{16,24},{17,... | collective-permute-start | bytes 393224 | tf_op jit(solution)/shard_map/ppermute | solution.py:362
  102.7 19.4 %collective-permute-start.14 = (bf16[128,512]{1,0:T(8,128)(2,1)S(1)}, bf16[128,512]{1,0:T(8,128)(2,1)S(1)}, u32[]{:S(2)}, u32[]{:S(2)}) collective-permute-start(bf16[128,512]{1,0:T(8,128)(2,1)S(1)} %fusion.refs_0_), channel_id=1, source_target_pairs={{0,10},{1,11},{2,12},{3,13},{4,14},{5,15},{16,26},{17,27},{18,28},... | collective-permute-start | bytes 393224 | tf_op jit(solution)/shard_map/ppermute | solution.py:362

commit v4 on v3

--- a/solution.py
+++ b/solution.py
@@ -21,8 +21,20 @@
 MIB = 2**20
 
 
-def after(value, *others):
-    return lax.optimization_barrier((value,) + others)[0]
+def gate_kernel(value_ref, *refs):
+    pass
+
+
+def gate(value, *others):
+    hbm = pl.BlockSpec(memory_space=pl.ANY)
+    return pl.pallas_call(
+        gate_kernel,
+        in_specs=[hbm] * (1 + len(others)),
+        out_specs=hbm,
+        out_shape=jax.ShapeDtypeStruct(value.shape, value.dtype),
+        input_output_aliases={0: 0},
+        name="gate",
+    )(value, *others)
 
 
 def flat_pairs(sizes, move):
@@ -37,7 +49,7 @@
     return pairs
 
 
-def scale_kernel(first_ref, codes_ref, scales_ref, ids_ref, near_ref, far_ref, held, sems):
+def scale_kernel(first_ref, codes_ref, scales_ref, ids_ref, near_ref, far_ref, copy_ref, held, sems):
     depth = near_ref.shape[0] - PAD
     blocks = depth // BLK
     own, column, block = first_ref[0], first_ref[1], first_ref[2]
@@ -57,6 +69,7 @@
             part = held[k, b * BLK : (b + 1) * BLK, :].astype(jnp.float32) * scale
             out_ref[b * BLK : (b + 1) * BLK, :] = part.astype(jnp.bfloat16)
         out_ref[depth:, :] = ids
+    copy_ref[...] = near_ref[...]
 
 
 def scaled_weight(codes, scales, segment_ids, depth, group, zz, column):
@@ -71,13 +84,13 @@
             pl.BlockSpec(memory_space=pltpu.SMEM),
             pl.BlockSpec(memory_space=pltpu.VMEM),
         ],
-        out_specs=[pl.BlockSpec(memory_space=pltpu.VMEM)] * 2,
-        out_shape=[out, out],
+        out_specs=[pl.BlockSpec(memory_space=pltpu.VMEM)] * 3,
+        out_shape=[out, out, out],
         scratch_shapes=[
             pltpu.VMEM((2, depth, width), jnp.bfloat16),
             pltpu.SemaphoreType.DMA((2,)),
         ],
-        compiler_params=pltpu.CompilerParams(vmem_limit_bytes=8 * MIB),
+        compiler_params=pltpu.CompilerParams(vmem_limit_bytes=56 * MIB),
         name="scale",
     )(first, codes, scales.T, segment_ids.reshape(1, -1))
 
@@ -95,15 +108,16 @@
     def along_shard(distance):
         return lambda g, s, c: (g, s ^ distance, c)
 
+    near, far, later = scaled_weight(
+        codes, scales, segment_ids, depth, group, zz, shard * codes.shape[1] // BLK
+    )
     sent = lax.dynamic_slice_in_dim(hidden, (1 - group) * 2 * depth, 2 * depth, 1)
     across = send(sent, lambda g, s, c: (1 - g, s, c))
-    near, far = scaled_weight(
-        after(codes, sent), scales, segment_ids, depth, group, zz, shard * codes.shape[1] // BLK
-    )
     piece = {0: near}
     piece[6] = send(far, along_shard(6))
     piece[2] = send(far, along_shard(2))
     piece[1] = send(near, along_shard(1))
+    piece[4] = send(gate(later, piece[2]), along_shard(4))
     pair = jnp.concatenate(
         [
             lax.dynamic_slice_in_dim(hidden, (group * 2 + 1 - zz) * depth, depth, 1),
@@ -111,24 +125,203 @@
         ],
         axis=0,
     )
-    piece[4] = send(after(near, pair, piece[2], piece[1]), along_shard(4))
     pair = send(pair, along_shard(2))
     piece[3] = send(piece[2], along_shard(1))
-    piece[7] = send(after(piece[6], piece[3]), along_shard(1))
-    piece[5] = send(after(piece[4], piece[7]), along_shard(1))
-    order = sorted(piece)
-    shards = jnp.stack([jnp.bitwise_xor(shard, d) for d in order]).astype(jnp.int32)
+    piece[6] = gate(piece[6], piece[3])
+    piece[7] = send(piece[6], along_shard(1))
+    piece[5] = send(piece[4], along_shard(1))
     arrays = [hidden, across, pair]
-    copies = [
-        (0, 0, member * depth, member),
-        (1, 0, zz * depth, jnp.bitwise_xor(member, 2)),
-        (2, 0, 0, jnp.bitwise_xor(member, 1)),
-        (2, rows, 0, jnp.bitwise_xor(member, 3)),
-    ]
-    ids = [piece[d][depth : depth + 1] for d in order]
-    known = jnp.concatenate(ids, axis=0)
-    spot = jnp.bitwise_xor(shard, jnp.arange(8, dtype=jnp.int32))
-    return arrays, copies, [piece[d] for d in order], shards, known[spot]
+    copies = [(0, 0, member * depth), (2, 0, 0), (1, 0, zz * depth), (2, rows, 0)]
+    return arrays, copies, piece
+
+
+def head_kernel(copies, heads, early, table_ref, *refs):
+    hidden_refs, refs = refs[:3], refs[3:]
+    weight_refs, refs = refs[: 2 * heads], refs[2 * heads :]
+    if early:
+        mine_ref, other_ref, own_ref, ids_ref, left, right, sems = refs
+    else:
+        own_ref, mine_ref, other_ref, ids_ref, left, right, sems = refs
+    rows, depth = mine_ref.shape[1], left.shape[1]
+    count = len(copies)
+    started = []
+    for k, (at, row) in enumerate(copies):
+        first = pl.multiple_of(table_ref[k], HD)
+        started.append(
+            pltpu.make_async_copy(
+                hidden_refs[at].at[row : row + rows, pl.ds(first, depth)],
+                left.at[k * rows : (k + 1) * rows, :],
+                sems.at[k],
+            )
+        )
+    for k, ref in enumerate(weight_refs):
+        first = pl.multiple_of(jnp.bitwise_xor(table_ref[count], k % 2) * HD, HD)
+        started.append(
+            pltpu.make_async_copy(
+                ref.at[pl.ds(0, depth), :], right.at[k // 2, :, pl.ds(first, HD)], sems.at[count + k]
+            )
+        )
+    for k, ref in enumerate(weight_refs):
+        started.append(
+            pltpu.make_async_copy(
+                ref.at[pl.ds(depth, PAD), :], ids_ref.at[k], sems.at[count + 2 * heads + k]
+            )
+        )
+    for copy in started:
+        copy.start()
+    for copy in started[:count]:
+        copy.wait()
+
+    def head(h):
+        for copy in started[count + 2 * h : count + 2 * h + 2]:
+            copy.wait()
+        total = jnp.dot(left[...], right[h], preferred_element_type=jnp.float32)
+        return total.reshape(mine_ref.shape)
+
+    def put(here, there, first, second):
+        @pl.when(table_ref[count + 1] == 1)
+        def _():
+            here[...] = first
+            if second is not None:
+                there[...] = second
+
+        @pl.when(table_ref[count + 1] == 0)
+        def _():
+            there[...] = first
+            if second is not None:
+                here[...] = second
+
+    if early:
+        put(mine_ref, other_ref, head(0), None)
+        put(other_ref, mine_ref, head(1), None)
+        own_ref[...] = head(2)
+    else:
+        put(mine_ref, other_ref, own_ref[...], head(0))
+    for copy in started[count + 2 * heads :]:
+        copy.wait()
+
+
+def project_heads(early, arrays, copies, pieces, table, rows, own=None):
+    heads = len(pieces) // 2
+    depth = arrays[-1].shape[1]
+    members = len(copies)
+    out = jax.ShapeDtypeStruct((members, rows, 2 * HD), jnp.float32)
+    ids = jax.ShapeDtypeStruct((len(pieces), PAD, HD), jnp.bfloat16)
+    vmem = pl.BlockSpec(memory_space=pltpu.VMEM)
+    extra = [] if early else [own]
+    results = [out] * (3 if early else 2) + [ids]
+    return pl.pallas_call(
+        functools.partial(head_kernel, [c[:2] for c in copies], heads, early),
+        in_specs=[pl.BlockSpec(memory_space=pltpu.SMEM)]
+        + [pl.BlockSpec(memory_space=pl.ANY)] * (len(arrays) + len(pieces))
+        + [vmem] * len(extra),
+        out_specs=[vmem] * len(results),
+        out_shape=results,
+        scratch_shapes=[
+            pltpu.VMEM((members * rows, depth), jnp.bfloat16),
+            pltpu.VMEM((heads, depth, 2 * HD), jnp.bfloat16),
+            pltpu.SemaphoreType.DMA((members + 2 * len(pieces),)),
+        ],
+        compiler_params=pltpu.CompilerParams(vmem_limit_bytes=24 * MIB),
+        cost_estimate=pl.CostEstimate(
+            flops=0 if early else 4 * members * rows * depth * heads * HD * 100,
+            bytes_accessed=0 if early else 2 * depth * (members * rows + heads * 2 * HD),
+            transcendentals=0,
+        ),
+        name="project_early" if early else "project_late",
+    )(table, *arrays, *pieces, *extra)
+
+
+def share_kernel(mine_ref, got_ref, own_ref, *out_refs):
+    own_ref[...] = mine_ref[0] + got_ref[0]
+    for k, out_ref in enumerate(out_refs):
+        total = mine_ref[k + 1] + got_ref[k + 1]
+        out_ref[:, : 2 * HD] = total.astype(jnp.bfloat16)
+        keys = total[:, :HD]
+        rest = keys - keys.astype(jnp.bfloat16).astype(jnp.float32)
+        out_ref[:, 2 * HD :] = rest.astype(jnp.bfloat16)
+
+
+def shares(mine, got):
+    members, rows, columns = mine.shape
+    out = jax.ShapeDtypeStruct((rows, columns + HD), jnp.bfloat16)
+    vmem = pl.BlockSpec(memory_space=pltpu.VMEM)
+    return pl.pallas_call(
+        share_kernel,
+        in_specs=[vmem] * 2,
+        out_specs=[vmem] * members,
+        out_shape=[jax.ShapeDtypeStruct((rows, columns), jnp.float32)] + [out] * (members - 1),
+        compiler_params=pltpu.CompilerParams(vmem_limit_bytes=16 * MIB),
+        name="shares",
+    )(mine, got)
+
+
+def sum_kernel(place_ref, *refs):
+    out_ref = refs[-1]
+    for k, group in enumerate((refs[:4], refs[4:8])):
+        keys, values = group[0][:, :HD], group[0][:, HD:]
+        for ref in group[1:]:
+            rest = ref[:, 2 * HD :].astype(jnp.float32)
+            keys = keys + (ref[:, :HD].astype(jnp.float32) + rest)
+            values = values + ref[:, HD : 2 * HD].astype(jnp.float32)
+        first = pl.multiple_of(jnp.bitwise_xor(place_ref[0], k) * 2 * HD, 2 * HD)
+        out_ref[:, pl.ds(first, HD)] = keys.astype(jnp.bfloat16)
+        out_ref[:, pl.ds(pl.multiple_of(first + HD, HD), HD)] = values.astype(jnp.bfloat16)
+
+
+def summed(zz, straight, flipped):
+    rows = straight[0].shape[0]
+    vmem = pl.BlockSpec(memory_space=pltpu.VMEM)
+    return pl.pallas_call(
+        sum_kernel,
+        in_specs=[pl.BlockSpec(memory_space=pltpu.SMEM)] + [vmem] * 8,
+        out_specs=vmem,
+        out_shape=jax.ShapeDtypeStruct((rows, 4 * HD), jnp.bfloat16),
+        compiler_params=pltpu.CompilerParams(vmem_limit_bytes=16 * MIB),
+        name="sum",
+    )(zz.astype(jnp.int32)[None], *straight, *flipped)
+
+
+def keyval_by_steps(sizes, hidden, codes, scales, segment_ids):
+    rows = hidden.shape[0]
+    hi, zz, y = lax.axis_index("hi"), lax.axis_index("zz"), lax.axis_index("y")
+    shard = (hi * 2 + zz) * 2 + y
+    same = (hi == lax.axis_index("tensor")).astype(jnp.int32)
+    arrays, copies, piece = gather_by_steps(sizes, hidden, codes, scales, segment_ids)
+    numbers = [c[2] for c in copies] + [y, same]
+    table = jnp.stack([jnp.asarray(n, jnp.int32) for n in numbers])
+    swap = flat_pairs(sizes, lambda g, s, c: (g, s, 1 - c))
+    over_z = flat_pairs(sizes, lambda g, s, c: (g, s ^ 2, c))
+    over_x = flat_pairs(sizes, lambda g, s, c: (1 - g, s, c))
+    over_both = flat_pairs(sizes, lambda g, s, c: (1 - g, s ^ 2, c))
+
+    def exchanged(mine, other):
+        own, to_z, to_x, to_both = shares(mine, lax.ppermute(other, ALL, swap))
+        return (
+            own,
+            lax.ppermute(to_both, ALL, over_both),
+            lax.ppermute(to_z, ALL, over_z),
+            lax.ppermute(to_x, ALL, over_x),
+        )
+
+    order = (2, 3, 6, 7, 0, 1)
+    mine, other, own, ids = project_heads(
+        True, arrays, copies, [piece[d] for d in order], table, rows
+    )
+    flipped = exchanged(mine, other)
+    mine, other, last = project_heads(
+        False, arrays, copies, [piece[4], piece[5]], table, rows, own
+    )
+    straight = exchanged(mine, other)
+    keyval = summed(
+        zz,
+        (straight[0], flipped[1], flipped[2], straight[3]),
+        (flipped[0], straight[1], straight[2], flipped[3]),
+    )
+    known = jnp.concatenate([ids, last], axis=0)[:, 0]
+    place = jnp.asarray([(order + (4, 5)).index(d) for d in range(8)], jnp.int32)
+    known = known[place[jnp.bitwise_xor(shard, jnp.arange(8, dtype=jnp.int32))]]
+    return keyval, known
 
 
 def gather_whole(sizes, hidden, codes, scales, segment_ids):
@@ -279,23 +472,22 @@
     )(mine, got)
 
 
-def attend_kernel(pieces, heads, stack, query_ref, allowed_ref, *refs):
+def attend_kernel(pieces, heads, stack, query_ref, bias_ref, *refs):
     kv_refs, (out_ref, keys, values) = refs[:pieces], refs[pieces:]
     rows = query_ref.shape[0]
-    scaling = 1.0 / math.sqrt(HD)
+    scaling = math.log2(math.e) / math.sqrt(HD)
     for d, ref in enumerate(kv_refs):
         keys[d * rows : (d + 1) * rows, :] = ref[:, :HD]
         values[d * rows : (d + 1) * rows, :] = ref[:, HD:]
-    allowed = allowed_ref[...]
-    allowed = jnp.concatenate([allowed] * stack, axis=0) > 0.0
+    bias = jnp.concatenate([bias_ref[...]] * stack, axis=0)
     for part in range(heads // stack):
         columns = [slice((part * stack + h) * HD, (part * stack + h + 1) * HD) for h in range(stack)]
         query = jnp.concatenate([query_ref[:, c] for c in columns], axis=0)
         scores = lax.dot_general(
             query, keys[...], (((1,), (1,)), ((), ())), preferred_element_type=jnp.float32
         )
-        scores = jnp.where(allowed, scores * scaling, -jnp.inf)
-        weights = jnp.exp(scores - jnp.max(scores, axis=1, keepdims=True))
+        scores = scores + bias
+        weights = jnp.exp2((scores - jnp.max(scores, axis=1, keepdims=True)) * scaling)
         totals = jnp.sum(weights, axis=1, keepdims=True)
         result = jnp.dot(
             weights.astype(jnp.bfloat16), values[...], preferred_element_type=jnp.float32
@@ -305,9 +497,9 @@
             out_ref[:, c] = result[h * rows : (h + 1) * rows]
 
 
-def attend(queries, allowed, pieces):
+def attend(queries, bias, pieces):
     rows, width = queries.shape
-    window = allowed.shape[1]
+    window = bias.shape[1]
     group = QPK * HD
     stack = 4 if window <= 1024 else 1
     return pl.pallas_call(
@@ -323,17 +515,13 @@
         scratch_shapes=[pltpu.VMEM((window, HD), jnp.bfloat16)] * 2,
         compiler_params=pltpu.CompilerParams(vmem_limit_bytes=24 * MIB),
         name="attend",
-    )(queries, allowed, *pieces)
-
-
-def on_device(sizes, hidden, codes, scales, queries, segment_ids):
-    groups, shards, cores = sizes
+    )(queries, bias, *pieces)
+
+
+def keyval_whole(sizes, hidden, codes, scales, segment_ids):
     rows = hidden.shape[0]
-    shard = lax.axis_index(SHARD)
     core = lax.axis_index("tensor").astype(jnp.int32)
-    by_steps = groups == 2 and shards == 8 and codes.shape[1] == BLK and rows == BLK
-    gather = gather_by_steps if by_steps else gather_whole
-    arrays, copies, pieces, where, known = gather(sizes, hidden, codes, scales, segment_ids)
+    arrays, copies, pieces, where, known = gather_whole(sizes, hidden, codes, scales, segment_ids)
     other, mine = project(arrays, copies, pieces, where, core[None], rows)
     swap = flat_pairs(sizes, lambda g, s, c: (g, s, 1 - c))
     partial = split(mine, lax.ppermute(other, ALL, swap))
@@ -342,7 +530,16 @@
     columns = mine.shape[2]
     rest = total[:, columns:].reshape(rows, -1, 1, HD)
     rest = jnp.concatenate([rest, jnp.zeros_like(rest)], axis=2).reshape(rows, columns)
-    keyval = (total[:, :columns] + rest).astype(jnp.bfloat16)
+    return (total[:, :columns] + rest).astype(jnp.bfloat16), known
+
+
+def on_device(sizes, hidden, codes, scales, queries, segment_ids):
+    groups, shards, cores = sizes
+    rows = hidden.shape[0]
+    shard = lax.axis_index(SHARD)
+    by_steps = groups == 2 and shards == 8 and codes.shape[1] == BLK and rows == BLK
+    make = keyval_by_steps if by_steps else keyval_whole
+    keyval, known = make(sizes, hidden, codes, scales, segment_ids)
 
     back = min(shards // 2 + 1, shards - 1)
     from_shard = shard - jnp.arange(back + 1, dtype=jnp.int32)
@@ -354,13 +551,14 @@
         (segment_ids.astype(jnp.bfloat16)[:, None] == seen[None, :])
         & (keypos[None, :] <= rowpos[:, None])
         & (keypos[None, :] >= 0)
-    ).astype(jnp.float32)
+    )
+    bias = jnp.where(allowed, 0.0, -jnp.inf).astype(jnp.float32)
 
     pieces = [keyval]
     for d in range(1, back + 1):
         up = flat_pairs(sizes, lambda g, s, c: (g, s + d, c) if s + d < shards else None)
         pieces.append(lax.ppermute(keyval, ALL, up))
-    return attend(queries, allowed, pieces)
+    return attend(queries, bias, pieces)
 
 
 def solution(mesh):

time: 130 us -> 119 us (0.915)
  local copies, waits for them, and re-layouts: 13.8 us -> 5.21 us
  waiting for transfers between devices: 77.9 us -> 72.5 us
  starting transfers between devices: 17.7 us -> 19.6 us
  Pallas kernels: 16.5 us -> 17.9 us
    ppermute x1 -> x8, starting transfers between devices: 0.07 us -> 6.7 us  [the longest x2 2.66 us: exchanged(): lax.ppermute(to_z, ALL, over_z)]
    slice x9 -> x0, local copies, waits for them, and re-layouts: 5.42 us -> none  [the longest x8 5.41 us: gather_by_steps(): ids = [piece[d][depth:depth + 1] for d in order]]
    all_to_all x1 -> x0, starting transfers between devices: 4.3 us -> none  [on_device(): partial = lax.all_to_all(partial, BLOCK, 0, 0, tiled=True)]
    all_to_all x1 -> x0, waiting for transfers between devices: 3.72 us -> none  [on_device(): partial = lax.all_to_all(partial, BLOCK, 0, 0, tiled=True)]
    unnamed x16 -> x9, local copies, waits for them, and re-layouts: 3.46 us -> 0.02 us
    ppermute x9, waiting for transfers between devices: 53.6 us -> 50.2 us  [send(): return lax.ppermute(value, ALL, flat_pairs(sizes, move))]
    ppermute x1 -> x8, waiting for transfers between devices: 2.65 us -> 4.72 us  [the longest x2 3.68 us: exchanged(): lax.ppermute(to_x, ALL, over_x)]
    pallas_call x1, Pallas kernels: 1.79 us -> 3.13 us  [scaled_weight(): pl.pallas_call(scale_kernel, in_specs=[pl.BlockSpec(memory_space=pltpu.SM...]
  transfers between devices with their start and end apart: 16 -> 22, of which waited for: 12 -> 12; matrix products, arithmetic and copies ran while one was open for 8% -> 5% of each run, Pallas kernels for 1% -> 10%
where the time goes in v4:
time: 119 us
  waiting for transfers between devices  72.5 us (61%)
  starting transfers between devices  19.6 us (16%)
  Pallas kernels  17.9 us (15%)
  local copies, waits for them, and re-layouts  5.21 us (4%)
  other arithmetic  3.1 us (3%)
    ppermute x9, waiting for transfers between devices, send(): return lax.ppermute(value, ALL, flat_pairs(sizes, move))  50.2 us
    ppermute x5, waiting for transfers between devices, on_device(): pieces.append(lax.ppermute(keyval, ALL, up))  17.6 us
    pallas_call x2, Pallas kernels, project_heads(): pl.pallas_call(functools.partial(head_kernel, [c[:2] for c in copies], he...  8.3 us
    ppermute x9, starting transfers between devices, send(): return lax.ppermute(value, ALL, flat_pairs(sizes, move))  6.46 us
    ppermute x5, starting transfers between devices, on_device(): pieces.append(lax.ppermute(keyval, ALL, up))  6.46 us
    pallas_call x1, Pallas kernels, attend(): pl.pallas_call(functools.partial(attend_kernel, len(pieces), QPK, stack),...  6.26 us
    ppermute x2, waiting for transfers between devices, exchanged(): lax.ppermute(to_x, ALL, over_x)  3.68 us
    pallas_call x1, Pallas kernels, scaled_weight(): pl.pallas_call(scale_kernel, in_specs=[pl.BlockSpec(memory_space=pltpu.SM...  3.13 us
  transfers between devices with their start and end apart: 22, of which 12 were waited for; matrix products, arithmetic and copies ran while one was open for 5% of the time, Pallas kernels for 10%

profile of v4, /device:TPU:28, one launch (start us, length us, event | category | flops | bytes accessed | tf_op | source)
XLA Modules:
  0.0 118.5 jit_solution(4183753349268898468)
XLA Ops:
  0.0 2.4 %constant_dynamic-slice_fusion.2 = bf16[128,4096]{1,0:T(8,128)(2,1)} fusion(bf16[128,8192]{1,0:T(8,128)(2,1)} %refs_0_.3, s32[]{:T(128)S(6)} %select_n.39), kind=kLoop, calls=%fused_computation.16 | loop fusion | bytes 2097156 | tf_op jit(solution)/shard_map/dynamic_slice | solution.py:114
  2.4 1.5 %collective-permute-start = (bf16[128,4096]{1,0:T(8,128)(2,1)}, bf16[128,4096]{1,0:T(8,128)(2,1)S(1)}, u32[]{:S(2)}, u32[]{:S(2)}) collective-permute-start(bf16[128,4096]{1,0:T(8,128)(2,1)} %constant_dynamic-slice_fusion.2), channel_id=1, source_target_pairs={{0,16},{1,17},{2,18},{3,19},{4,20},{5,21},{6,22},{7,23},{8,24},{9,... | collective-permute-start | bytes 3145736 | tf_op jit(solution)/shard_map/ppermute | solution.py:106
  3.9 0.6 pad_add_fusion.first_ref
  4.6 3.1 %scale.1 = (bf16[2064,128]{1,0:T(8,128)(2,1)}, bf16[2064,128]{1,0:T(8,128)(2,1)}, bf16[2064,128]{1,0:T(8,128)(2,1)}) custom-call(s32[3]{0:T(128)} %pad_add_fusion.first_ref, bf16[8192,128]{1,0:T(8,128)(2,1)} %codes_ref.1, f32[8,64]{1,0:T(8,128)} %bitcast.27, s32[1,128]{1,0:T(1,128)} %bitcast.28), custom_call_target="tpu_custom_call" | custom-call | tf_op jit(solution)/shard_map/scale/pallas_call | solution.py:79
  8.2 1.3 %collective-permute-start.4 = (bf16[2064,128]{1,0:T(8,128)(2,1)}, bf16[2064,128]{1,0:T(8,128)(2,1)}, u32[]{:S(2)}, u32[]{:S(2)}) collective-permute-start(bf16[2064,128]{1,0:T(8,128)(2,1)} %get-tuple-element.23), channel_id=1, source_target_pairs={{0,12},{1,13},{2,14},{3,15},{4,8},{5,9},{6,10},{7,11},{8,4},{9,5},... | collective-permute-start | bytes 1585160 | tf_op jit(solution)/shard_map/ppermute | solution.py:106
  9.6 0.9 constant_dynamic-slice_fusion.1
  10.4 21.1 %collective-permute-done.2.refs_3_.refs_0_ = bf16[2064,128]{1,0:T(8,128)(2,1)} collective-permute-done((bf16[2064,128]{1,0:T(8,128)(2,1)}, bf16[2064,128]{1,0:T(8,128)(2,1)}, u32[]{:S(2)}, u32[]{:S(2)}) %collective-permute-start.2) | collective-permute-done | bytes 528416 | tf_op jit(solution)/shard_map/ppermute | solution.py:106
  32.1 2.1 %pad_maximum_fusion = bf16[256,2048]{1,0:T(8,128)(2,1)} fusion(bf16[128,2048]{1,0:T(8,128)(2,1)S(1)} %constant_dynamic-slice_fusion, bf16[128,2048]{1,0:T(8,128)(2,1)} %constant_dynamic-slice_fusion.1), kind=kLoop, calls=%fused_computation.3 | loop fusion | flops 2097152 | bytes 2097152 | tf_op jit(solution)/shard_map/concatenate | solution.py:121
  34.3 1.5 %collective-permute-start.6 = (bf16[2064,128]{1,0:T(8,128)(2,1)}, bf16[2064,128]{1,0:T(8,128)(2,1)}, u32[]{:S(2)}, u32[]{:S(2)}) collective-permute-start(bf16[2064,128]{1,0:T(8,128)(2,1)} %get-tuple-element.24.refs_7_), channel_id=1, source_target_pairs={{0,2},{1,3},{2,0},{3,1},{4,6},{5,7},{6,4},{7,5},{8,10},{9,11},{10,... | collective-permute-start | bytes 1585160 | tf_op jit(solution)/shard_map/ppermute | solution.py:106
  35.8 0.6 gather_fusion
  36.6 10.3 %collective-permute-done.3.refs_0_.refs_4_ = bf16[2064,128]{1,0:T(8,128)(2,1)} collective-permute-done((bf16[2064,128]{1,0:T(8,128)(2,1)}, bf16[2064,128]{1,0:T(8,128)(2,1)}, u32[]{:S(2)}, u32[]{:S(2)}) %collective-permute-start.3) | collective-permute-done | bytes 528416 | tf_op jit(solution)/shard_map/ppermute | solution.py:106
  47.4 9.4 %collective-permute-done.7.refs_3_ = bf16[2064,128]{1,0:T(8,128)(2,1)} collective-permute-done((bf16[2064,128]{1,0:T(8,128)(2,1)}, bf16[2064,128]{1,0:T(8,128)(2,1)}, u32[]{:S(2)}, u32[]{:S(2)}) %collective-permute-start.7) | collective-permute-done | bytes 528416 | tf_op jit(solution)/shard_map/ppermute | solution.py:106
  57.3 4.3 %collective-permute-done.5.refs_6_ = bf16[2064,128]{1,0:T(8,128)(2,1)S(1)} collective-permute-done((bf16[2064,128]{1,0:T(8,128)(2,1)}, bf16[2064,128]{1,0:T(8,128)(2,1)S(1)}, u32[]{:S(2)}, u32[]{:S(2)}) %collective-permute-start.5) | collective-permute-done | bytes 528416 | tf_op jit(solution)/shard_map/ppermute | solution.py:106
  61.7 5.1 %collective-permute-done.1.refs_2_ = bf16[256,2048]{1,0:T(8,128)(2,1)} collective-permute-done((bf16[256,2048]{1,0:T(8,128)(2,1)}, bf16[256,2048]{1,0:T(8,128)(2,1)}, u32[]{:S(2)}, u32[]{:S(2)}) %collective-permute-start.1) | collective-permute-done | bytes 1048608 | tf_op jit(solution)/shard_map/ppermute | solution.py:106
  66.7 5.5 %project_early.1 = (f32[4,128,256]{2,1,0:T(8,128)S(1)}, f32[4,128,256]{2,1,0:T(8,128)S(1)}, f32[4,128,256]{2,1,0:T(8,128)S(1)}, bf16[6,16,128]{2,1,0:T(8,128)(2,1)S(1)}) custom-call(s32[6]{0:T(128)S(1)} %stack.35.table_ref, bf16[128,8192]{1,0:T(8,128)(2,1)S(1)} %copy-done, bf16[128,4096]{1,0:T(8,128)(2,1)S(1)} %collective-permute-done.refs_1_, ...), custom_call_target="tpu_custom_call" | custom-call | tf_op jit(solution)/shard_map/project_early/pallas_call | solution.py:213
  72.3 2.8 %project_late.1 = (f32[4,128,256]{2,1,0:T(8,128)S(1)}, f32[4,128,256]{2,1,0:T(8,128)S(1)}, bf16[2,16,128]{2,1,0:T(8,128)(2,1)S(1)}) custom-call(s32[6]{0:T(128)S(1)} %stack.35.table_ref, bf16[128,8192]{1,0:T(8,128)(2,1)S(1)} %copy-done, bf16[128,4096]{1,0:T(8,128)(2,1)S(1)} %collective-permute-done.refs_1_, ...), custom_call_target="tpu_custom_call" | custom-call | flops 53687091200 | bytes 3145728 | tf_op jit(solution)/shard_map/project_late/pallas_call | solution.py:213
  76.4 2.1 %collective-permute-start.12 = (bf16[128,384]{1,0:T(8,128)(2,1)S(1)}, bf16[128,384]{1,0:T(8,128)(2,1)S(1)}, u32[]{:S(2)}, u32[]{:S(2)}) collective-permute-start(bf16[128,384]{1,0:T(8,128)(2,1)S(1)} %get-tuple-element.35), channel_id=1, source_target_pairs={{0,4},{1,5},{2,6},{3,7},{4,0},{5,1},{6,2},{7,3},{8,12},{9,13},{10,... | collective-permute-start | bytes 294920 | tf_op jit(solution)/shard_map/ppermute | solution.py:303
  78.5 1.0 collective-permute-start.16
  79.5 1.1 collective-permute-start.13
  80.6 0.9 collective-permute-start.14
  81.5 1.0 collective-permute-done.11.refs_1_
  84.2 1.6 %collective-permute-done.16.refs_7_ = bf16[128,384]{1,0:T(8,128)(2,1)S(1)} collective-permute-done((bf16[128,384]{1,0:T(8,128)(2,1)S(1)}, bf16[128,384]{1,0:T(8,128)(2,1)S(1)}, u32[]{:S(2)}, u32[]{:S(2)}) %collective-permute-start.16) | collective-permute-done | bytes 98336 | tf_op jit(solution)/shard_map/ppermute | solution.py:304
  85.9 2.1 %collective-permute-done.13.refs_3_ = bf16[128,384]{1,0:T(8,128)(2,1)S(1)} collective-permute-done((bf16[128,384]{1,0:T(8,128)(2,1)S(1)}, bf16[128,384]{1,0:T(8,128)(2,1)S(1)}, u32[]{:S(2)}, u32[]{:S(2)}) %collective-permute-start.13) | collective-permute-done | bytes 98336 | tf_op jit(solution)/shard_map/ppermute | solution.py:304
  88.0 1.3 %collective-permute-start.17 = (bf16[128,512]{1,0:T(8,128)(2,1)S(1)}, bf16[128,512]{1,0:T(8,128)(2,1)S(1)}, u32[]{:S(2)}, u32[]{:S(2)}) collective-permute-start(bf16[128,512]{1,0:T(8,128)(2,1)S(1)} %sum.1.refs_0_), channel_id=1, source_target_pairs={{0,2},{1,3},{2,4},{3,5},{4,6},{5,7},{6,8},{7,9},{8,10},{9,11},{10,... | collective-permute-start | bytes 393224 | tf_op jit(solution)/shard_map/ppermute | solution.py:560
  89.3 1.3 %collective-permute-start.18 = (bf16[128,512]{1,0:T(8,128)(2,1)S(1)}, bf16[128,512]{1,0:T(8,128)(2,1)S(1)}, u32[]{:S(2)}, u32[]{:S(2)}) collective-permute-start(bf16[128,512]{1,0:T(8,128)(2,1)S(1)} %sum.1.refs_0_), channel_id=1, source_target_pairs={{0,4},{1,5},{2,6},{3,7},{4,8},{5,9},{6,10},{7,11},{8,12},{9,13},{1... | collective-permute-start | bytes 393224 | tf_op jit(solution)/shard_map/ppermute | solution.py:560
  90.6 1.3 %collective-permute-start.19 = (bf16[128,512]{1,0:T(8,128)(2,1)S(1)}, bf16[128,512]{1,0:T(8,128)(2,1)S(1)}, u32[]{:S(2)}, u32[]{:S(2)}) collective-permute-start(bf16[128,512]{1,0:T(8,128)(2,1)S(1)} %sum.1.refs_0_), channel_id=1, source_target_pairs={{0,6},{1,7},{2,8},{3,9},{4,10},{5,11},{6,12},{7,13},{8,14},{9,15},... | collective-permute-start | bytes 393224 | tf_op jit(solution)/shard_map/ppermute | solution.py:560
  91.9 1.3 %collective-permute-start.20 = (bf16[128,512]{1,0:T(8,128)(2,1)S(1)}, bf16[128,512]{1,0:T(8,128)(2,1)S(1)}, u32[]{:S(2)}, u32[]{:S(2)}) collective-permute-start(bf16[128,512]{1,0:T(8,128)(2,1)S(1)} %sum.1.refs_0_), channel_id=1, source_target_pairs={{0,8},{1,9},{2,10},{3,11},{4,12},{5,13},{6,14},{7,15},{16,24},{17,... | collective-permute-start | bytes 393224 | tf_op jit(solution)/shard_map/ppermute | solution.py:560
  93.2 1.3 %collective-permute-start.21 = (bf16[128,512]{1,0:T(8,128)(2,1)S(1)}, bf16[128,512]{1,0:T(8,128)(2,1)S(1)}, u32[]{:S(2)}, u32[]{:S(2)}) collective-permute-start(bf16[128,512]{1,0:T(8,128)(2,1)S(1)} %sum.1.refs_0_), channel_id=1, source_target_pairs={{0,10},{1,11},{2,12},{3,13},{4,14},{5,15},{16,26},{17,27},{18,28},... | collective-permute-start | bytes 393224 | tf_op jit(solution)/shard_map/ppermute | solution.py:560
  94.9 3.3 %collective-permute-done.18.refs_2_ = bf16[128,512]{1,0:T(8,128)(2,1)S(1)} collective-permute-done((bf16[128,512]{1,0:T(8,128)(2,1)S(1)}, bf16[128,512]{1,0:T(8,128)(2,1)S(1)}, u32[]{:S(2)}, u32[]{:S(2)}) %collective-permute-start.18) | collective-permute-done | bytes 131104 | tf_op jit(solution)/shard_map/ppermute | solution.py:560
  98.2 3.9 %collective-permute-done.19.refs_3_ = bf16[128,512]{1,0:T(8,128)(2,1)S(1)} collective-permute-done((bf16[128,512]{1,0:T(8,128)(2,1)S(1)}, bf16[128,512]{1,0:T(8,128)(2,1)S(1)}, u32[]{:S(2)}, u32[]{:S(2)}) %collective-permute-start.19) | collective-permute-done | bytes 131104 | tf_op jit(solution)/shard_map/ppermute | solution.py:560
  102.1 10.2 %collective-permute-done.20.refs_4_ = bf16[128,512]{1,0:T(8,128)(2,1)S(1)} collective-permute-done((bf16[128,512]{1,0:T(8,128)(2,1)S(1)}, bf16[128,512]{1,0:T(8,128)(2,1)S(1)}, u32[]{:S(2)}, u32[]{:S(2)}) %collective-permute-start.20) | collective-permute-done | bytes 131104 | tf_op jit(solution)/shard_map/ppermute | solution.py:560
  112.3 6.3 %attend.1 = bf16[128,4096]{1,0:T(8,128)(2,1)} custom-call(bf16[128,4096]{1,0:T(8,128)(2,1)S(1)} %copy-done.1, f32[128,768]{1,0:T(8,128)S(1)} %and_select_fusion.bias_ref, bf16[128,512]{1,0:T(8,128)(2,1)S(1)} %sum.1.refs_0_, bf16[128,512]{1,0:T(8,128)(2,1)S(1)} %collective-permute-done.17.refs_1_, bf16[128,512]{1,0:T(8,128)(2,1)S(1)} %collective-permute-done.18.refs_2_, ...), custom_call_target="tpu_custom_call" | custom-call | tf_op jit(solution)/shard_map/attend/pallas_call | solution.py:505
  (52 shorter events, 5.8 us)
Async XLA Ops:
  0.0 9.6 %copy-start = (bf16[128,8192]{1,0:T(8,128)(2,1)S(1)}, bf16[128,8192]{1,0:T(8,128)(2,1)}, u32[]{:S(2)}) copy-start(bf16[128,8192]{1,0:T(8,128)(2,1)} %refs_0_.3) | copy-start | bytes 6291460
  2.4 29.7 %collective-permute-start = (bf16[128,4096]{1,0:T(8,128)(2,1)}, bf16[128,4096]{1,0:T(8,128)(2,1)S(1)}, u32[]{:S(2)}, u32[]{:S(2)}) collective-permute-start(bf16[128,4096]{1,0:T(8,128)(2,1)} %constant_dynamic-slice_fusion.2), channel_id=1, source_target_pairs={{0,16},{1,17},{2,18},{3,19},{4,20},{5,21},{6,22},{7,23},{8,24},{9,... | collective-permute-start | bytes 3145736 | tf_op jit(solution)/shard_map/ppermute | solution.py:106
  7.7 23.8 %collective-permute-start.2 = (bf16[2064,128]{1,0:T(8,128)(2,1)}, bf16[2064,128]{1,0:T(8,128)(2,1)}, u32[]{:S(2)}, u32[]{:S(2)}) collective-permute-start(bf16[2064,128]{1,0:T(8,128)(2,1)} %get-tuple-element.23), channel_id=1, source_target_pairs={{0,4},{1,5},{2,6},{3,7},{4,0},{5,1},{6,2},{7,3},{8,12},{9,13},{10,... | collective-permute-start | bytes 1585160 | tf_op jit(solution)/shard_map/ppermute | solution.py:106
  8.2 28.4 %collective-permute-start.4 = (bf16[2064,128]{1,0:T(8,128)(2,1)}, bf16[2064,128]{1,0:T(8,128)(2,1)}, u32[]{:S(2)}, u32[]{:S(2)}) collective-permute-start(bf16[2064,128]{1,0:T(8,128)(2,1)} %get-tuple-element.23), channel_id=1, source_target_pairs={{0,12},{1,13},{2,14},{3,15},{4,8},{5,9},{6,10},{7,11},{8,4},{9,5},... | collective-permute-start | bytes 1585160 | tf_op jit(solution)/shard_map/ppermute | solution.py:106
  31.5 4.3 %copy-start.3 = (s32[128]{0:T(128)S(1)}, s32[128]{0:T(128)}, u32[]{:S(2)}) copy-start(s32[128]{0:T(128)} %param.10) | copy-start | bytes 1540
  31.5 4.3 %copy-start.2 = (s32[8]{0:T(128)S(1)}, s32[8]{0:T(128)}, u32[]{:S(2)}) copy-start(s32[8]{0:T(128)} %constant.66.clone) | copy-start | bytes 100
  31.5 25.3 %collective-permute-start.7 = (bf16[2064,128]{1,0:T(8,128)(2,1)}, bf16[2064,128]{1,0:T(8,128)(2,1)}, u32[]{:S(2)}, u32[]{:S(2)}) collective-permute-start(bf16[2064,128]{1,0:T(8,128)(2,1)} %gate.3), channel_id=1, source_target_pairs={{0,8},{1,9},{2,10},{3,11},{4,12},{5,13},{6,14},{7,15},{8,0},{9,1},... | collective-permute-start | bytes 1585160 | tf_op jit(solution)/shard_map/ppermute | solution.py:106
  31.5 15.3 %collective-permute-start.3 = (bf16[2064,128]{1,0:T(8,128)(2,1)}, bf16[2064,128]{1,0:T(8,128)(2,1)}, u32[]{:S(2)}, u32[]{:S(2)}) collective-permute-start(bf16[2064,128]{1,0:T(8,128)(2,1)} %collective-permute-done.2.refs_3_.refs_0_), channel_id=1, source_target_pairs={{0,2},{1,3},{2,0},{3,1},{4,6},{5,7},{6,4},{7,5},{8,10},{9,11},{10,... | collective-permute-start | bytes 1585160 | tf_op jit(solution)/shard_map/ppermute | solution.py:106
  34.3 32.5 %collective-permute-start.1 = (bf16[256,2048]{1,0:T(8,128)(2,1)}, bf16[256,2048]{1,0:T(8,128)(2,1)}, u32[]{:S(2)}, u32[]{:S(2)}) collective-permute-start(bf16[256,2048]{1,0:T(8,128)(2,1)} %pad_maximum_fusion), channel_id=1, source_target_pairs={{0,4},{1,5},{2,6},{3,7},{4,0},{5,1},{6,2},{7,3},{8,12},{9,13},{10,... | collective-permute-start | bytes 3145736 | tf_op jit(solution)/shard_map/ppermute | solution.py:106
  34.3 23.1 %collective-permute-start.6 = (bf16[2064,128]{1,0:T(8,128)(2,1)}, bf16[2064,128]{1,0:T(8,128)(2,1)}, u32[]{:S(2)}, u32[]{:S(2)}) collective-permute-start(bf16[2064,128]{1,0:T(8,128)(2,1)} %get-tuple-element.24.refs_7_), channel_id=1, source_target_pairs={{0,2},{1,3},{2,0},{3,1},{4,6},{5,7},{6,4},{7,5},{8,10},{9,11},{10,... | collective-permute-start | bytes 1585160 | tf_op jit(solution)/shard_map/ppermute | solution.py:106
  46.9 14.8 %collective-permute-start.5 = (bf16[2064,128]{1,0:T(8,128)(2,1)}, bf16[2064,128]{1,0:T(8,128)(2,1)S(1)}, u32[]{:S(2)}, u32[]{:S(2)}) collective-permute-start(bf16[2064,128]{1,0:T(8,128)(2,1)} %gate.2.refs_5_), channel_id=1, source_target_pairs={{0,2},{1,3},{2,0},{3,1},{4,6},{5,7},{6,4},{7,5},{8,10},{9,11},{10,... | collective-permute-start | bytes 1585160 | tf_op jit(solution)/shard_map/ppermute | solution.py:106
  56.8 15.5 %collective-permute-start.8 = (bf16[2064,128]{1,0:T(8,128)(2,1)}, bf16[2064,128]{1,0:T(8,128)(2,1)S(1)}, u32[]{:S(2)}, u32[]{:S(2)}) collective-permute-start(bf16[2064,128]{1,0:T(8,128)(2,1)} %collective-permute-done.7.refs_3_), channel_id=1, source_target_pairs={{0,2},{1,3},{2,0},{3,1},{4,6},{5,7},{6,4},{7,5},{8,10},{9,11},{10,... | collective-permute-start | bytes 1585160 | tf_op jit(solution)/shard_map/ppermute | solution.py:106
  72.2 3.6 %collective-permute-start.10 = (f32[4,128,256]{2,1,0:T(8,128)S(1)}, f32[4,128,256]{2,1,0:T(8,128)S(1)}, u32[]{:S(2)}, u32[]{:S(2)}) collective-permute-start(f32[4,128,256]{2,1,0:T(8,128)S(1)} %get-tuple-element.33), channel_id=1, source_target_pairs={{0,1},{1,0},{2,3},{3,2},{4,5},{5,4},{6,7},{7,6},{8,9},{9,8},{10,11... | collective-permute-start | bytes 1572872 | tf_op jit(solution)/shard_map/ppermute | solution.py:299
  75.1 37.1 %copy-start.1 = (bf16[128,4096]{1,0:T(8,128)(2,1)S(1)}, bf16[128,4096]{1,0:T(8,128)(2,1)}, u32[]{:S(2)}) copy-start(bf16[128,4096]{1,0:T(8,128)(2,1)} %query_ref.1) | copy-start | bytes 3145732
  75.2 4.3 %collective-permute-start.9 = (f32[4,128,256]{2,1,0:T(8,128)S(1)}, f32[4,128,256]{2,1,0:T(8,128)S(1)}, u32[]{:S(2)}, u32[]{:S(2)}) collective-permute-start(f32[4,128,256]{2,1,0:T(8,128)S(1)} %get-tuple-element.30), channel_id=1, source_target_pairs={{0,1},{1,0},{2,3},{3,2},{4,5},{5,4},{6,7},{7,6},{8,9},{9,8},{10,11... | collective-permute-start | bytes 1572872 | tf_op jit(solution)/shard_map/ppermute | solution.py:299
  75.9 6.6 %collective-permute-start.11 = (bf16[128,384]{1,0:T(8,128)(2,1)S(1)}, bf16[128,384]{1,0:T(8,128)(2,1)S(1)}, u32[]{:S(2)}, u32[]{:S(2)}) collective-permute-start(bf16[128,384]{1,0:T(8,128)(2,1)S(1)} %get-tuple-element.34), channel_id=1, source_target_pairs={{0,20},{1,21},{2,22},{3,23},{4,16},{5,17},{6,18},{7,19},{8,28},{9,... | collective-permute-start | bytes 294920 | tf_op jit(solution)/shard_map/ppermute | solution.py:302
  76.4 7.9 %collective-permute-start.12 = (bf16[128,384]{1,0:T(8,128)(2,1)S(1)}, bf16[128,384]{1,0:T(8,128)(2,1)S(1)}, u32[]{:S(2)}, u32[]{:S(2)}) collective-permute-start(bf16[128,384]{1,0:T(8,128)(2,1)S(1)} %get-tuple-element.35), channel_id=1, source_target_pairs={{0,4},{1,5},{2,6},{3,7},{4,0},{5,1},{6,2},{7,3},{8,12},{9,13},{10,... | collective-permute-start | bytes 294920 | tf_op jit(solution)/shard_map/ppermute | solution.py:303
  78.5 7.4 %collective-permute-start.16 = (bf16[128,384]{1,0:T(8,128)(2,1)S(1)}, bf16[128,384]{1,0:T(8,128)(2,1)S(1)}, u32[]{:S(2)}, u32[]{:S(2)}) collective-permute-start(bf16[128,384]{1,0:T(8,128)(2,1)S(1)} %get-tuple-element.40), channel_id=1, source_target_pairs={{0,16},{1,17},{2,18},{3,19},{4,20},{5,21},{6,22},{7,23},{8,24},{9,... | collective-permute-start | bytes 294920 | tf_op jit(solution)/shard_map/ppermute | solution.py:304
  79.5 8.4 %collective-permute-start.13 = (bf16[128,384]{1,0:T(8,128)(2,1)S(1)}, bf16[128,384]{1,0:T(8,128)(2,1)S(1)}, u32[]{:S(2)}, u32[]{:S(2)}) collective-permute-start(bf16[128,384]{1,0:T(8,128)(2,1)S(1)} %get-tuple-element.36), channel_id=1, source_target_pairs={{0,16},{1,17},{2,18},{3,19},{4,20},{5,21},{6,22},{7,23},{8,24},{9,... | collective-permute-start | bytes 294920 | tf_op jit(solution)/shard_map/ppermute | solution.py:304
  80.6 7.3 %collective-permute-start.14 = (bf16[128,384]{1,0:T(8,128)(2,1)S(1)}, bf16[128,384]{1,0:T(8,128)(2,1)S(1)}, u32[]{:S(2)}, u32[]{:S(2)}) collective-permute-start(bf16[128,384]{1,0:T(8,128)(2,1)S(1)} %get-tuple-element.38), channel_id=1, source_target_pairs={{0,20},{1,21},{2,22},{3,23},{4,16},{5,17},{6,18},{7,19},{8,28},{9,... | collective-permute-start | bytes 294920 | tf_op jit(solution)/shard_map/ppermute | solution.py:302
  82.5 5.4 %collective-permute-start.15 = (bf16[128,384]{1,0:T(8,128)(2,1)S(1)}, bf16[128,384]{1,0:T(8,128)(2,1)S(1)}, u32[]{:S(2)}, u32[]{:S(2)}) collective-permute-start(bf16[128,384]{1,0:T(8,128)(2,1)S(1)} %get-tuple-element.39), channel_id=1, source_target_pairs={{0,4},{1,5},{2,6},{3,7},{4,0},{5,1},{6,2},{7,3},{8,12},{9,13},{10,... | collective-permute-start | bytes 294920 | tf_op jit(solution)/shard_map/ppermute | solution.py:303
  88.0 6.9 %collective-permute-start.17 = (bf16[128,512]{1,0:T(8,128)(2,1)S(1)}, bf16[128,512]{1,0:T(8,128)(2,1)S(1)}, u32[]{:S(2)}, u32[]{:S(2)}) collective-permute-start(bf16[128,512]{1,0:T(8,128)(2,1)S(1)} %sum.1.refs_0_), channel_id=1, source_target_pairs={{0,2},{1,3},{2,4},{3,5},{4,6},{5,7},{6,8},{7,9},{8,10},{9,11},{10,... | collective-permute-start | bytes 393224 | tf_op jit(solution)/shard_map/ppermute | solution.py:560
  89.3 8.8 %collective-permute-start.18 = (bf16[128,512]{1,0:T(8,128)(2,1)S(1)}, bf16[128,512]{1,0:T(8,128)(2,1)S(1)}, u32[]{:S(2)}, u32[]{:S(2)}) collective-permute-start(bf16[128,512]{1,0:T(8,128)(2,1)S(1)} %sum.1.refs_0_), channel_id=1, source_target_pairs={{0,4},{1,5},{2,6},{3,7},{4,8},{5,9},{6,10},{7,11},{8,12},{9,13},{1... | collective-permute-start | bytes 393224 | tf_op jit(solution)/shard_map/ppermute | solution.py:560
  90.6 11.5 %collective-permute-start.19 = (bf16[128,512]{1,0:T(8,128)(2,1)S(1)}, bf16[128,512]{1,0:T(8,128)(2,1)S(1)}, u32[]{:S(2)}, u32[]{:S(2)}) collective-permute-start(bf16[128,512]{1,0:T(8,128)(2,1)S(1)} %sum.1.refs_0_), channel_id=1, source_target_pairs={{0,6},{1,7},{2,8},{3,9},{4,10},{5,11},{6,12},{7,13},{8,14},{9,15},... | collective-permute-start | bytes 393224 | tf_op jit(solution)/shard_map/ppermute | solution.py:560
  91.9 20.3 %collective-permute-start.20 = (bf16[128,512]{1,0:T(8,128)(2,1)S(1)}, bf16[128,512]{1,0:T(8,128)(2,1)S(1)}, u32[]{:S(2)}, u32[]{:S(2)}) collective-permute-start(bf16[128,512]{1,0:T(8,128)(2,1)S(1)} %sum.1.refs_0_), channel_id=1, source_target_pairs={{0,8},{1,9},{2,10},{3,11},{4,12},{5,13},{6,14},{7,15},{16,24},{17,... | collective-permute-start | bytes 393224 | tf_op jit(solution)/shard_map/ppermute | solution.py:560
  93.2 19.0 %collective-permute-start.21 = (bf16[128,512]{1,0:T(8,128)(2,1)S(1)}, bf16[128,512]{1,0:T(8,128)(2,1)S(1)}, u32[]{:S(2)}, u32[]{:S(2)}) collective-permute-start(bf16[128,512]{1,0:T(8,128)(2,1)S(1)} %sum.1.refs_0_), channel_id=1, source_target_pairs={{0,10},{1,11},{2,12},{3,13},{4,14},{5,15},{16,26},{17,27},{18,28},... | collective-permute-start | bytes 393224 | tf_op jit(solution)/shard_map/ppermute | solution.py:560

commit v5 on v4

--- a/solution.py
+++ b/solution.py
@@ -33,6 +33,7 @@
         out_specs=hbm,
         out_shape=jax.ShapeDtypeStruct(value.shape, value.dtype),
         input_output_aliases={0: 0},
+        compiler_params=pltpu.CompilerParams(vmem_limit_bytes=MIB),
         name="gate",
     )(value, *others)
 
@@ -111,8 +112,12 @@
     near, far, later = scaled_weight(
         codes, scales, segment_ids, depth, group, zz, shard * codes.shape[1] // BLK
     )
-    sent = lax.dynamic_slice_in_dim(hidden, (1 - group) * 2 * depth, 2 * depth, 1)
-    across = send(sent, lambda g, s, c: (1 - g, s, c))
+    def quarter(dg, dz):
+        first = (jnp.bitwise_xor(group, dg) * 2 + jnp.bitwise_xor(zz, dz)) * depth
+        return lax.dynamic_slice_in_dim(hidden, first, depth, 1)
+
+    across = send(quarter(1, 1), lambda g, s, c: (1 - g, s, c))
+    stays = send(quarter(1, 0), lambda g, s, c: (1 - g, s, c))
     piece = {0: near}
     piece[6] = send(far, along_shard(6))
     piece[2] = send(far, along_shard(2))
@@ -121,7 +126,7 @@
     pair = jnp.concatenate(
         [
             lax.dynamic_slice_in_dim(hidden, (group * 2 + 1 - zz) * depth, depth, 1),
-            lax.dynamic_slice_in_dim(across, (1 - zz) * depth, depth, 1),
+            across,
         ],
         axis=0,
     )
@@ -130,8 +135,8 @@
     piece[6] = gate(piece[6], piece[3])
     piece[7] = send(piece[6], along_shard(1))
     piece[5] = send(piece[4], along_shard(1))
-    arrays = [hidden, across, pair]
-    copies = [(0, 0, member * depth), (2, 0, 0), (1, 0, zz * depth), (2, rows, 0)]
+    arrays = [hidden, stays, pair]
+    copies = [(0, 0, member * depth), (2, 0, 0), (1, 0, 0), (2, rows, 0)]
     return arrays, copies, piece
 
 

time: 119 us -> 115 us (0.966)
  local copies, waits for them, and re-layouts: 5.21 us -> 2.86 us
  waiting for transfers between devices: 72.5 us -> 70.7 us
  starting transfers between devices: 19.6 us -> 21.2 us
    dynamic_slice x2 -> x0, local copies, waits for them, and re-layouts: 2.47 us -> none  [the longest x1 2.44 us: gather_by_steps(): lax.dynamic_slice_in_dim(hidden, (1 - group) * 2 * depth, 2 * depth, 1)]
    ppermute x9 -> x10, waiting for transfers between devices: 50.2 us -> 48.4 us  [send(): return lax.ppermute(value, ALL, flat_pairs(sizes, move))]
    ppermute x9 -> x10, starting transfers between devices: 6.46 us -> 7.97 us  [send(): return lax.ppermute(value, ALL, flat_pairs(sizes, move))]
  transfers between devices with their start and end apart: 22 -> 23, of which waited for: 12 -> 12; matrix products, arithmetic and copies ran while one was open for 5% -> 4% of each run, Pallas kernels for 10% -> 7%
where the time goes in v5:
time: 115 us
  waiting for transfers between devices  70.7 us (61%)
  starting transfers between devices  21.2 us (18%)
  Pallas kernels  17.6 us (15%)
  local copies, waits for them, and re-layouts  2.86 us (2%)
  other arithmetic  2.09 us (2%)
    ppermute x10, waiting for transfers between devices, send(): return lax.ppermute(value, ALL, flat_pairs(sizes, move))  48.4 us
    ppermute x5, waiting for transfers between devices, on_device(): pieces.append(lax.ppermute(keyval, ALL, up))  17.6 us
    pallas_call x2, Pallas kernels, project_heads(): pl.pallas_call(functools.partial(head_kernel, [c[:2] for c in copies], he...  7.99 us
    ppermute x10, starting transfers between devices, send(): return lax.ppermute(value, ALL, flat_pairs(sizes, move))  7.97 us
    ppermute x5, starting transfers between devices, on_device(): pieces.append(lax.ppermute(keyval, ALL, up))  6.46 us
    pallas_call x1, Pallas kernels, attend(): pl.pallas_call(functools.partial(attend_kernel, len(pieces), QPK, stack),...  6.26 us
    ppermute x2, waiting for transfers between devices, exchanged(): lax.ppermute(to_x, ALL, over_x)  3.42 us
    pallas_call x1, Pallas kernels, scaled_weight(): pl.pallas_call(scale_kernel, in_specs=[pl.BlockSpec(memory_space=pltpu.SM...  3.18 us
  transfers between devices with their start and end apart: 23, of which 12 were waited for; matrix products, arithmetic and copies ran while one was open for 4% of the time, Pallas kernels for 7%

profile of v5, /device:TPU:28, one launch (start us, length us, event | category | flops | bytes accessed | tf_op | source)
XLA Modules:
  0.0 114.7 jit_solution(206397160892575953)
XLA Ops:
  0.0 0.7 pad_add_fusion.first_ref
  0.7 3.2 %scale.1 = (bf16[2064,128]{1,0:T(8,128)(2,1)}, bf16[2064,128]{1,0:T(8,128)(2,1)}, bf16[2064,128]{1,0:T(8,128)(2,1)}) custom-call(s32[3]{0:T(128)} %pad_add_fusion.first_ref, bf16[8192,128]{1,0:T(8,128)(2,1)} %codes_ref.1, f32[8,64]{1,0:T(8,128)} %bitcast.26, s32[1,128]{1,0:T(1,128)} %bitcast.27), custom_call_target="tpu_custom_call" | custom-call | tf_op jit(solution)/shard_map/scale/pallas_call | solution.py:80
  4.4 1.0 constant_dynamic-slice_fusion.1
  5.3 1.5 %collective-permute-start.1 = (bf16[128,2048]{1,0:T(8,128)(2,1)S(1)}, bf16[128,2048]{1,0:T(8,128)(2,1)S(1)}, u32[]{:S(2)}, u32[]{:S(2)}) collective-permute-start(bf16[128,2048]{1,0:T(8,128)(2,1)S(1)} %get-tuple-element.42), channel_id=1, source_target_pairs={{0,16},{1,17},{2,18},{3,19},{4,20},{5,21},{6,22},{7,23},{8,24},{9,... | collective-permute-start | bytes 1572872 | tf_op jit(solution)/shard_map/ppermute | solution.py:107
  6.8 1.3 %collective-permute-start.5 = (bf16[2064,128]{1,0:T(8,128)(2,1)}, bf16[2064,128]{1,0:T(8,128)(2,1)}, u32[]{:S(2)}, u32[]{:S(2)}) collective-permute-start(bf16[2064,128]{1,0:T(8,128)(2,1)} %get-tuple-element.23), channel_id=1, source_target_pairs={{0,12},{1,13},{2,14},{3,15},{4,8},{5,9},{6,10},{7,11},{8,4},{9,5},... | collective-permute-start | bytes 1585160 | tf_op jit(solution)/shard_map/ppermute | solution.py:107
  8.2 20.0 %collective-permute-done.3.refs_3_.refs_0_ = bf16[2064,128]{1,0:T(8,128)(2,1)S(1)} collective-permute-done((bf16[2064,128]{1,0:T(8,128)(2,1)}, bf16[2064,128]{1,0:T(8,128)(2,1)S(1)}, u32[]{:S(2)}, u32[]{:S(2)}) %collective-permute-start.3) | collective-permute-done | bytes 528416 | tf_op jit(solution)/shard_map/ppermute | solution.py:107
  28.7 1.1 pad_maximum_fusion
  29.8 1.5 %collective-permute-start.7 = (bf16[2064,128]{1,0:T(8,128)(2,1)}, bf16[2064,128]{1,0:T(8,128)(2,1)}, u32[]{:S(2)}, u32[]{:S(2)}) collective-permute-start(bf16[2064,128]{1,0:T(8,128)(2,1)} %get-tuple-element.24.refs_7_), channel_id=1, source_target_pairs={{0,2},{1,3},{2,0},{3,1},{4,6},{5,7},{6,4},{7,5},{8,10},{9,11},{10,... | collective-permute-start | bytes 1585160 | tf_op jit(solution)/shard_map/ppermute | solution.py:107
  31.3 0.6 gather_fusion
  32.1 1.6 %collective-permute-start = (bf16[128,2048]{1,0:T(8,128)(2,1)}, bf16[128,2048]{1,0:T(8,128)(2,1)S(1)}, u32[]{:S(2)}, u32[]{:S(2)}) collective-permute-start(bf16[128,2048]{1,0:T(8,128)(2,1)} %get-tuple-element.43), channel_id=1, source_target_pairs={{0,16},{1,17},{2,18},{3,19},{4,20},{5,21},{6,22},{7,23},{8,24},{9,... | collective-permute-start | bytes 1572872 | tf_op jit(solution)/shard_map/ppermute | solution.py:107
  33.6 9.1 %collective-permute-done.4.refs_0_.refs_4_ = bf16[2064,128]{1,0:T(8,128)(2,1)S(1)} collective-permute-done((bf16[2064,128]{1,0:T(8,128)(2,1)S(1)}, bf16[2064,128]{1,0:T(8,128)(2,1)S(1)}, u32[]{:S(2)}, u32[]{:S(2)}) %collective-permute-start.4) | collective-permute-done | bytes 528416 | tf_op jit(solution)/shard_map/ppermute | solution.py:107
  43.3 12.1 %collective-permute-done.8.refs_3_ = bf16[2064,128]{1,0:T(8,128)(2,1)} collective-permute-done((bf16[2064,128]{1,0:T(8,128)(2,1)}, bf16[2064,128]{1,0:T(8,128)(2,1)}, u32[]{:S(2)}, u32[]{:S(2)}) %collective-permute-start.8) | collective-permute-done | bytes 528416 | tf_op jit(solution)/shard_map/ppermute | solution.py:107
  56.0 7.1 %collective-permute-done.2.refs_2_ = bf16[256,2048]{1,0:T(8,128)(2,1)} collective-permute-done((bf16[256,2048]{1,0:T(8,128)(2,1)}, bf16[256,2048]{1,0:T(8,128)(2,1)}, u32[]{:S(2)}, u32[]{:S(2)}) %collective-permute-start.2) | collective-permute-done | bytes 1048608 | tf_op jit(solution)/shard_map/ppermute | solution.py:107
  63.1 5.2 %project_early.1 = (f32[4,128,256]{2,1,0:T(8,128)S(1)}, f32[4,128,256]{2,1,0:T(8,128)S(1)}, f32[4,128,256]{2,1,0:T(8,128)S(1)}, bf16[6,16,128]{2,1,0:T(8,128)(2,1)S(1)}) custom-call(s32[6]{0:T(128)S(1)} %stack.31.table_ref, bf16[128,8192]{1,0:T(8,128)(2,1)S(1)} %copy-done, bf16[128,2048]{1,0:T(8,128)(2,1)S(1)} %collective-permute-done.refs_1_, ...), custom_call_target="tpu_custom_call" | custom-call | tf_op jit(solution)/shard_map/project_early/pallas_call | solution.py:218
  68.4 2.8 %project_late.1 = (f32[4,128,256]{2,1,0:T(8,128)S(1)}, f32[4,128,256]{2,1,0:T(8,128)S(1)}, bf16[2,16,128]{2,1,0:T(8,128)(2,1)S(1)}) custom-call(s32[6]{0:T(128)S(1)} %stack.31.table_ref, bf16[128,8192]{1,0:T(8,128)(2,1)S(1)} %copy-done, bf16[128,2048]{1,0:T(8,128)(2,1)S(1)} %collective-permute-done.refs_1_, ...), custom_call_target="tpu_custom_call" | custom-call | flops 53687091200 | bytes 3145728 | tf_op jit(solution)/shard_map/project_late/pallas_call | solution.py:218
  72.0 1.5 %collective-permute-start.12 = (bf16[128,384]{1,0:T(8,128)(2,1)S(1)}, bf16[128,384]{1,0:T(8,128)(2,1)S(1)}, u32[]{:S(2)}, u32[]{:S(2)}) collective-permute-start(bf16[128,384]{1,0:T(8,128)(2,1)S(1)} %get-tuple-element.34), channel_id=1, source_target_pairs={{0,20},{1,21},{2,22},{3,23},{4,16},{5,17},{6,18},{7,19},{8,28},{9,... | collective-permute-start | bytes 294920 | tf_op jit(solution)/shard_map/ppermute | solution.py:307
  73.5 1.5 %collective-permute-start.13 = (bf16[128,384]{1,0:T(8,128)(2,1)S(1)}, bf16[128,384]{1,0:T(8,128)(2,1)S(1)}, u32[]{:S(2)}, u32[]{:S(2)}) collective-permute-start(bf16[128,384]{1,0:T(8,128)(2,1)S(1)} %get-tuple-element.35), channel_id=1, source_target_pairs={{0,4},{1,5},{2,6},{3,7},{4,0},{5,1},{6,2},{7,3},{8,12},{9,13},{10,... | collective-permute-start | bytes 294920 | tf_op jit(solution)/shard_map/ppermute | solution.py:308
  75.6 1.6 %collective-permute-start.14 = (bf16[128,384]{1,0:T(8,128)(2,1)S(1)}, bf16[128,384]{1,0:T(8,128)(2,1)S(1)}, u32[]{:S(2)}, u32[]{:S(2)}) collective-permute-start(bf16[128,384]{1,0:T(8,128)(2,1)S(1)} %get-tuple-element.36), channel_id=1, source_target_pairs={{0,16},{1,17},{2,18},{3,19},{4,20},{5,21},{6,22},{7,23},{8,24},{9,... | collective-permute-start | bytes 294920 | tf_op jit(solution)/shard_map/ppermute | solution.py:309
  77.7 0.9 collective-permute-done.12.refs_1_
  79.2 0.6 gather_fusion.1
  79.7 0.6 gather_fusion.2
  80.7 1.2 %collective-permute-done.17.refs_7_ = bf16[128,384]{1,0:T(8,128)(2,1)S(1)} collective-permute-done((bf16[128,384]{1,0:T(8,128)(2,1)S(1)}, bf16[128,384]{1,0:T(8,128)(2,1)S(1)}, u32[]{:S(2)}, u32[]{:S(2)}) %collective-permute-start.17) | collective-permute-done | bytes 98336 | tf_op jit(solution)/shard_map/ppermute | solution.py:309
  81.9 2.2 %collective-permute-done.14.refs_3_ = bf16[128,384]{1,0:T(8,128)(2,1)S(1)} collective-permute-done((bf16[128,384]{1,0:T(8,128)(2,1)S(1)}, bf16[128,384]{1,0:T(8,128)(2,1)S(1)}, u32[]{:S(2)}, u32[]{:S(2)}) %collective-permute-start.14) | collective-permute-done | bytes 98336 | tf_op jit(solution)/shard_map/ppermute | solution.py:309
  84.2 1.3 %collective-permute-start.18 = (bf16[128,512]{1,0:T(8,128)(2,1)S(1)}, bf16[128,512]{1,0:T(8,128)(2,1)S(1)}, u32[]{:S(2)}, u32[]{:S(2)}) collective-permute-start(bf16[128,512]{1,0:T(8,128)(2,1)S(1)} %sum.1.refs_0_), channel_id=1, source_target_pairs={{0,2},{1,3},{2,4},{3,5},{4,6},{5,7},{6,8},{7,9},{8,10},{9,11},{10,... | collective-permute-start | bytes 393224 | tf_op jit(solution)/shard_map/ppermute | solution.py:565
  85.5 1.3 %collective-permute-start.19 = (bf16[128,512]{1,0:T(8,128)(2,1)S(1)}, bf16[128,512]{1,0:T(8,128)(2,1)S(1)}, u32[]{:S(2)}, u32[]{:S(2)}) collective-permute-start(bf16[128,512]{1,0:T(8,128)(2,1)S(1)} %sum.1.refs_0_), channel_id=1, source_target_pairs={{0,4},{1,5},{2,6},{3,7},{4,8},{5,9},{6,10},{7,11},{8,12},{9,13},{1... | collective-permute-start | bytes 393224 | tf_op jit(solution)/shard_map/ppermute | solution.py:565
  86.8 1.3 %collective-permute-start.20 = (bf16[128,512]{1,0:T(8,128)(2,1)S(1)}, bf16[128,512]{1,0:T(8,128)(2,1)S(1)}, u32[]{:S(2)}, u32[]{:S(2)}) collective-permute-start(bf16[128,512]{1,0:T(8,128)(2,1)S(1)} %sum.1.refs_0_), channel_id=1, source_target_pairs={{0,6},{1,7},{2,8},{3,9},{4,10},{5,11},{6,12},{7,13},{8,14},{9,15},... | collective-permute-start | bytes 393224 | tf_op jit(solution)/shard_map/ppermute | solution.py:565
  88.1 1.3 %collective-permute-start.21 = (bf16[128,512]{1,0:T(8,128)(2,1)S(1)}, bf16[128,512]{1,0:T(8,128)(2,1)S(1)}, u32[]{:S(2)}, u32[]{:S(2)}) collective-permute-start(bf16[128,512]{1,0:T(8,128)(2,1)S(1)} %sum.1.refs_0_), channel_id=1, source_target_pairs={{0,8},{1,9},{2,10},{3,11},{4,12},{5,13},{6,14},{7,15},{16,24},{17,... | collective-permute-start | bytes 393224 | tf_op jit(solution)/shard_map/ppermute | solution.py:565
  89.4 1.3 %collective-permute-start.22 = (bf16[128,512]{1,0:T(8,128)(2,1)S(1)}, bf16[128,512]{1,0:T(8,128)(2,1)S(1)}, u32[]{:S(2)}, u32[]{:S(2)}) collective-permute-start(bf16[128,512]{1,0:T(8,128)(2,1)S(1)} %sum.1.refs_0_), channel_id=1, source_target_pairs={{0,10},{1,11},{2,12},{3,13},{4,14},{5,15},{16,26},{17,27},{18,28},... | collective-permute-start | bytes 393224 | tf_op jit(solution)/shard_map/ppermute | solution.py:565
  91.1 3.3 %collective-permute-done.19.refs_2_ = bf16[128,512]{1,0:T(8,128)(2,1)S(1)} collective-permute-done((bf16[128,512]{1,0:T(8,128)(2,1)S(1)}, bf16[128,512]{1,0:T(8,128)(2,1)S(1)}, u32[]{:S(2)}, u32[]{:S(2)}) %collective-permute-start.19) | collective-permute-done | bytes 131104 | tf_op jit(solution)/shard_map/ppermute | solution.py:565
  94.4 3.7 %collective-permute-done.20.refs_3_ = bf16[128,512]{1,0:T(8,128)(2,1)S(1)} collective-permute-done((bf16[128,512]{1,0:T(8,128)(2,1)S(1)}, bf16[128,512]{1,0:T(8,128)(2,1)S(1)}, u32[]{:S(2)}, u32[]{:S(2)}) %collective-permute-start.20) | collective-permute-done | bytes 131104 | tf_op jit(solution)/shard_map/ppermute | solution.py:565
  98.1 10.4 %collective-permute-done.21.refs_4_ = bf16[128,512]{1,0:T(8,128)(2,1)S(1)} collective-permute-done((bf16[128,512]{1,0:T(8,128)(2,1)S(1)}, bf16[128,512]{1,0:T(8,128)(2,1)S(1)}, u32[]{:S(2)}, u32[]{:S(2)}) %collective-permute-start.21) | collective-permute-done | bytes 131104 | tf_op jit(solution)/shard_map/ppermute | solution.py:565
  108.5 6.3 %attend.1 = bf16[128,4096]{1,0:T(8,128)(2,1)} custom-call(bf16[128,4096]{1,0:T(8,128)(2,1)S(1)} %copy-done.1, f32[128,768]{1,0:T(8,128)S(1)} %and_select_fusion.bias_ref, bf16[128,512]{1,0:T(8,128)(2,1)S(1)} %sum.1.refs_0_, bf16[128,512]{1,0:T(8,128)(2,1)S(1)} %collective-permute-done.18.refs_1_, bf16[128,512]{1,0:T(8,128)(2,1)S(1)} %collective-permute-done.19.refs_2_, ...), custom_call_target="tpu_custom_call" | custom-call | tf_op jit(solution)/shard_map/attend/pallas_call | solution.py:510
  (53 shorter events, 5.6 us)
Async XLA Ops:
  0.0 4.4 %copy-start = (bf16[128,8192]{1,0:T(8,128)(2,1)S(1)}, bf16[128,8192]{1,0:T(8,128)(2,1)}, u32[]{:S(2)}) copy-start(bf16[128,8192]{1,0:T(8,128)(2,1)} %refs_0_.3) | copy-start | bytes 6291460
  3.8 24.3 %collective-permute-start.3 = (bf16[2064,128]{1,0:T(8,128)(2,1)}, bf16[2064,128]{1,0:T(8,128)(2,1)S(1)}, u32[]{:S(2)}, u32[]{:S(2)}) collective-permute-start(bf16[2064,128]{1,0:T(8,128)(2,1)} %get-tuple-element.23), channel_id=1, source_target_pairs={{0,4},{1,5},{2,6},{3,7},{4,0},{5,1},{6,2},{7,3},{8,12},{9,13},{10,... | collective-permute-start | bytes 1585160 | tf_op jit(solution)/shard_map/ppermute | solution.py:107
  5.3 26.0 %copy-start.3 = (s32[128]{0:T(128)S(1)}, s32[128]{0:T(128)}, u32[]{:S(2)}) copy-start(s32[128]{0:T(128)} %param.10) | copy-start | bytes 1540
  5.3 26.0 %copy-start.2 = (s32[8]{0:T(128)S(1)}, s32[8]{0:T(128)}, u32[]{:S(2)}) copy-start(s32[8]{0:T(128)} %constant.64.clone) | copy-start | bytes 100
  5.3 23.3 %collective-permute-start.1 = (bf16[128,2048]{1,0:T(8,128)(2,1)S(1)}, bf16[128,2048]{1,0:T(8,128)(2,1)S(1)}, u32[]{:S(2)}, u32[]{:S(2)}) collective-permute-start(bf16[128,2048]{1,0:T(8,128)(2,1)S(1)} %get-tuple-element.42), channel_id=1, source_target_pairs={{0,16},{1,17},{2,18},{3,19},{4,20},{5,21},{6,22},{7,23},{8,24},{9,... | collective-permute-start | bytes 1572872 | tf_op jit(solution)/shard_map/ppermute | solution.py:107
  6.8 25.2 %collective-permute-start.5 = (bf16[2064,128]{1,0:T(8,128)(2,1)}, bf16[2064,128]{1,0:T(8,128)(2,1)}, u32[]{:S(2)}, u32[]{:S(2)}) collective-permute-start(bf16[2064,128]{1,0:T(8,128)(2,1)} %get-tuple-element.23), channel_id=1, source_target_pairs={{0,12},{1,13},{2,14},{3,15},{4,8},{5,9},{6,10},{7,11},{8,4},{9,5},... | collective-permute-start | bytes 1585160 | tf_op jit(solution)/shard_map/ppermute | solution.py:107
  28.2 27.3 %collective-permute-start.8 = (bf16[2064,128]{1,0:T(8,128)(2,1)}, bf16[2064,128]{1,0:T(8,128)(2,1)}, u32[]{:S(2)}, u32[]{:S(2)}) collective-permute-start(bf16[2064,128]{1,0:T(8,128)(2,1)} %gate.3), channel_id=1, source_target_pairs={{0,8},{1,9},{2,10},{3,11},{4,12},{5,13},{6,14},{7,15},{8,0},{9,1},... | collective-permute-start | bytes 1585160 | tf_op jit(solution)/shard_map/ppermute | solution.py:107
  28.2 14.6 %collective-permute-start.4 = (bf16[2064,128]{1,0:T(8,128)(2,1)S(1)}, bf16[2064,128]{1,0:T(8,128)(2,1)S(1)}, u32[]{:S(2)}, u32[]{:S(2)}) collective-permute-start(bf16[2064,128]{1,0:T(8,128)(2,1)S(1)} %collective-permute-done.3.refs_3_.refs_0_), channel_id=1, source_target_pairs={{0,2},{1,3},{2,0},{3,1},{4,6},{5,7},{6,4},{7,5},{8,10},{9,11},{10,... | collective-permute-start | bytes 1585160 | tf_op jit(solution)/shard_map/ppermute | solution.py:107
  29.8 33.3 %collective-permute-start.2 = (bf16[256,2048]{1,0:T(8,128)(2,1)}, bf16[256,2048]{1,0:T(8,128)(2,1)}, u32[]{:S(2)}, u32[]{:S(2)}) collective-permute-start(bf16[256,2048]{1,0:T(8,128)(2,1)} %pad_maximum_fusion), channel_id=1, source_target_pairs={{0,4},{1,5},{2,6},{3,7},{4,0},{5,1},{6,2},{7,3},{8,12},{9,13},{10,... | collective-permute-start | bytes 3145736 | tf_op jit(solution)/shard_map/ppermute | solution.py:107
  29.8 26.2 %collective-permute-start.7 = (bf16[2064,128]{1,0:T(8,128)(2,1)}, bf16[2064,128]{1,0:T(8,128)(2,1)}, u32[]{:S(2)}, u32[]{:S(2)}) collective-permute-start(bf16[2064,128]{1,0:T(8,128)(2,1)} %get-tuple-element.24.refs_7_), channel_id=1, source_target_pairs={{0,2},{1,3},{2,0},{3,1},{4,6},{5,7},{6,4},{7,5},{8,10},{9,11},{10,... | collective-permute-start | bytes 1585160 | tf_op jit(solution)/shard_map/ppermute | solution.py:107
  32.1 23.9 %collective-permute-start = (bf16[128,2048]{1,0:T(8,128)(2,1)}, bf16[128,2048]{1,0:T(8,128)(2,1)S(1)}, u32[]{:S(2)}, u32[]{:S(2)}) collective-permute-start(bf16[128,2048]{1,0:T(8,128)(2,1)} %get-tuple-element.43), channel_id=1, source_target_pairs={{0,16},{1,17},{2,18},{3,19},{4,20},{5,21},{6,22},{7,23},{8,24},{9,... | collective-permute-start | bytes 1572872 | tf_op jit(solution)/shard_map/ppermute | solution.py:107
  42.8 20.3 %collective-permute-start.6 = (bf16[2064,128]{1,0:T(8,128)(2,1)}, bf16[2064,128]{1,0:T(8,128)(2,1)S(1)}, u32[]{:S(2)}, u32[]{:S(2)}) collective-permute-start(bf16[2064,128]{1,0:T(8,128)(2,1)} %gate.2.refs_5_), channel_id=1, source_target_pairs={{0,2},{1,3},{2,0},{3,1},{4,6},{5,7},{6,4},{7,5},{8,10},{9,11},{10,... | collective-permute-start | bytes 1585160 | tf_op jit(solution)/shard_map/ppermute | solution.py:107
  55.4 12.9 %collective-permute-start.9 = (bf16[2064,128]{1,0:T(8,128)(2,1)}, bf16[2064,128]{1,0:T(8,128)(2,1)S(1)}, u32[]{:S(2)}, u32[]{:S(2)}) collective-permute-start(bf16[2064,128]{1,0:T(8,128)(2,1)} %collective-permute-done.8.refs_3_), channel_id=1, source_target_pairs={{0,2},{1,3},{2,0},{3,1},{4,6},{5,7},{6,4},{7,5},{8,10},{9,11},{10,... | collective-permute-start | bytes 1585160 | tf_op jit(solution)/shard_map/ppermute | solution.py:107
  68.3 3.6 %collective-permute-start.11 = (f32[4,128,256]{2,1,0:T(8,128)S(1)}, f32[4,128,256]{2,1,0:T(8,128)S(1)}, u32[]{:S(2)}, u32[]{:S(2)}) collective-permute-start(f32[4,128,256]{2,1,0:T(8,128)S(1)} %get-tuple-element.33), channel_id=1, source_target_pairs={{0,1},{1,0},{2,3},{3,2},{4,5},{5,4},{6,7},{7,6},{8,9},{9,8},{10,11... | collective-permute-start | bytes 1572872 | tf_op jit(solution)/shard_map/ppermute | solution.py:304
  71.2 37.3 %copy-start.1 = (bf16[128,4096]{1,0:T(8,128)(2,1)S(1)}, bf16[128,4096]{1,0:T(8,128)(2,1)}, u32[]{:S(2)}) copy-start(bf16[128,4096]{1,0:T(8,128)(2,1)} %query_ref.1) | copy-start | bytes 3145732
  71.2 4.3 %collective-permute-start.10 = (f32[4,128,256]{2,1,0:T(8,128)S(1)}, f32[4,128,256]{2,1,0:T(8,128)S(1)}, u32[]{:S(2)}, u32[]{:S(2)}) collective-permute-start(f32[4,128,256]{2,1,0:T(8,128)S(1)} %get-tuple-element.30), channel_id=1, source_target_pairs={{0,1},{1,0},{2,3},{3,2},{4,5},{5,4},{6,7},{7,6},{8,9},{9,8},{10,11... | collective-permute-start | bytes 1572872 | tf_op jit(solution)/shard_map/ppermute | solution.py:304
  72.0 6.6 %collective-permute-start.12 = (bf16[128,384]{1,0:T(8,128)(2,1)S(1)}, bf16[128,384]{1,0:T(8,128)(2,1)S(1)}, u32[]{:S(2)}, u32[]{:S(2)}) collective-permute-start(bf16[128,384]{1,0:T(8,128)(2,1)S(1)} %get-tuple-element.34), channel_id=1, source_target_pairs={{0,20},{1,21},{2,22},{3,23},{4,16},{5,17},{6,18},{7,19},{8,28},{9,... | collective-permute-start | bytes 294920 | tf_op jit(solution)/shard_map/ppermute | solution.py:307
  73.5 7.2 %collective-permute-start.13 = (bf16[128,384]{1,0:T(8,128)(2,1)S(1)}, bf16[128,384]{1,0:T(8,128)(2,1)S(1)}, u32[]{:S(2)}, u32[]{:S(2)}) collective-permute-start(bf16[128,384]{1,0:T(8,128)(2,1)S(1)} %get-tuple-element.35), channel_id=1, source_target_pairs={{0,4},{1,5},{2,6},{3,7},{4,0},{5,1},{6,2},{7,3},{8,12},{9,13},{10,... | collective-permute-start | bytes 294920 | tf_op jit(solution)/shard_map/ppermute | solution.py:308
  75.0 6.9 %collective-permute-start.17 = (bf16[128,384]{1,0:T(8,128)(2,1)S(1)}, bf16[128,384]{1,0:T(8,128)(2,1)S(1)}, u32[]{:S(2)}, u32[]{:S(2)}) collective-permute-start(bf16[128,384]{1,0:T(8,128)(2,1)S(1)} %get-tuple-element.40), channel_id=1, source_target_pairs={{0,16},{1,17},{2,18},{3,19},{4,20},{5,21},{6,22},{7,23},{8,24},{9,... | collective-permute-start | bytes 294920 | tf_op jit(solution)/shard_map/ppermute | solution.py:309
  75.6 8.6 %collective-permute-start.14 = (bf16[128,384]{1,0:T(8,128)(2,1)S(1)}, bf16[128,384]{1,0:T(8,128)(2,1)S(1)}, u32[]{:S(2)}, u32[]{:S(2)}) collective-permute-start(bf16[128,384]{1,0:T(8,128)(2,1)S(1)} %get-tuple-element.36), channel_id=1, source_target_pairs={{0,16},{1,17},{2,18},{3,19},{4,20},{5,21},{6,22},{7,23},{8,24},{9,... | collective-permute-start | bytes 294920 | tf_op jit(solution)/shard_map/ppermute | solution.py:309
  77.1 7.0 %collective-permute-start.15 = (bf16[128,384]{1,0:T(8,128)(2,1)S(1)}, bf16[128,384]{1,0:T(8,128)(2,1)S(1)}, u32[]{:S(2)}, u32[]{:S(2)}) collective-permute-start(bf16[128,384]{1,0:T(8,128)(2,1)S(1)} %get-tuple-element.38), channel_id=1, source_target_pairs={{0,20},{1,21},{2,22},{3,23},{4,16},{5,17},{6,18},{7,19},{8,28},{9,... | collective-permute-start | bytes 294920 | tf_op jit(solution)/shard_map/ppermute | solution.py:307
  78.6 5.6 %collective-permute-start.16 = (bf16[128,384]{1,0:T(8,128)(2,1)S(1)}, bf16[128,384]{1,0:T(8,128)(2,1)S(1)}, u32[]{:S(2)}, u32[]{:S(2)}) collective-permute-start(bf16[128,384]{1,0:T(8,128)(2,1)S(1)} %get-tuple-element.39), channel_id=1, source_target_pairs={{0,4},{1,5},{2,6},{3,7},{4,0},{5,1},{6,2},{7,3},{8,12},{9,13},{10,... | collective-permute-start | bytes 294920 | tf_op jit(solution)/shard_map/ppermute | solution.py:308
  84.2 6.9 %collective-permute-start.18 = (bf16[128,512]{1,0:T(8,128)(2,1)S(1)}, bf16[128,512]{1,0:T(8,128)(2,1)S(1)}, u32[]{:S(2)}, u32[]{:S(2)}) collective-permute-start(bf16[128,512]{1,0:T(8,128)(2,1)S(1)} %sum.1.refs_0_), channel_id=1, source_target_pairs={{0,2},{1,3},{2,4},{3,5},{4,6},{5,7},{6,8},{7,9},{8,10},{9,11},{10,... | collective-permute-start | bytes 393224 | tf_op jit(solution)/shard_map/ppermute | solution.py:565
  85.5 8.8 %collective-permute-start.19 = (bf16[128,512]{1,0:T(8,128)(2,1)S(1)}, bf16[128,512]{1,0:T(8,128)(2,1)S(1)}, u32[]{:S(2)}, u32[]{:S(2)}) collective-permute-start(bf16[128,512]{1,0:T(8,128)(2,1)S(1)} %sum.1.refs_0_), channel_id=1, source_target_pairs={{0,4},{1,5},{2,6},{3,7},{4,8},{5,9},{6,10},{7,11},{8,12},{9,13},{1... | collective-permute-start | bytes 393224 | tf_op jit(solution)/shard_map/ppermute | solution.py:565
  86.8 11.3 %collective-permute-start.20 = (bf16[128,512]{1,0:T(8,128)(2,1)S(1)}, bf16[128,512]{1,0:T(8,128)(2,1)S(1)}, u32[]{:S(2)}, u32[]{:S(2)}) collective-permute-start(bf16[128,512]{1,0:T(8,128)(2,1)S(1)} %sum.1.refs_0_), channel_id=1, source_target_pairs={{0,6},{1,7},{2,8},{3,9},{4,10},{5,11},{6,12},{7,13},{8,14},{9,15},... | collective-permute-start | bytes 393224 | tf_op jit(solution)/shard_map/ppermute | solution.py:565
  88.1 20.3 %collective-permute-start.21 = (bf16[128,512]{1,0:T(8,128)(2,1)S(1)}, bf16[128,512]{1,0:T(8,128)(2,1)S(1)}, u32[]{:S(2)}, u32[]{:S(2)}) collective-permute-start(bf16[128,512]{1,0:T(8,128)(2,1)S(1)} %sum.1.refs_0_), channel_id=1, source_target_pairs={{0,8},{1,9},{2,10},{3,11},{4,12},{5,13},{6,14},{7,15},{16,24},{17,... | collective-permute-start | bytes 393224 | tf_op jit(solution)/shard_map/ppermute | solution.py:565
  89.4 19.0 %collective-permute-start.22 = (bf16[128,512]{1,0:T(8,128)(2,1)S(1)}, bf16[128,512]{1,0:T(8,128)(2,1)S(1)}, u32[]{:S(2)}, u32[]{:S(2)}) collective-permute-start(bf16[128,512]{1,0:T(8,128)(2,1)S(1)} %sum.1.refs_0_), channel_id=1, source_target_pairs={{0,10},{1,11},{2,12},{3,13},{4,14},{5,15},{16,26},{17,27},{18,28},... | collective-permute-start | bytes 393224 | tf_op jit(solution)/shard_map/ppermute | solution.py:565

commit v6 on v5

--- a/solution.py
+++ b/solution.py
@@ -50,50 +50,55 @@
     return pairs
 
 
-def scale_kernel(first_ref, codes_ref, scales_ref, ids_ref, near_ref, far_ref, copy_ref, held, sems):
+def scale_kernel(codes_ref, scales_ref, ids_ref, near_ref, far_ref, copy_ref, held, factors, sems):
     depth = near_ref.shape[0] - PAD
+    width = near_ref.shape[1]
     blocks = depth // BLK
-    own, column, block = first_ref[0], first_ref[1], first_ref[2]
-    copies = []
+    own = lax.axis_index("zz")
+    shard = (lax.axis_index("hi") * lax.axis_size("zz") + own) * lax.axis_size("y") + lax.axis_index("y")
+    column = shard * width // BLK
+    block = lax.axis_index("groups") * 2 * blocks
+    copies = [pltpu.make_async_copy(scales_ref, factors, sems.at[2])]
     for k, which in enumerate((1 - own, own)):
         row = pl.multiple_of((block + which * blocks) * BLK, BLK)
         copies.append(
             pltpu.make_async_copy(codes_ref.at[pl.ds(row, depth), :], held.at[k], sems.at[k])
         )
-        copies[k].start()
+    for copy in copies:
+        copy.start()
     ids = ids_ref[...].astype(jnp.float32)
     ids = jnp.broadcast_to(ids, (PAD, ids.shape[1])).astype(jnp.bfloat16)
+    copies[0].wait()
     for k, (out_ref, which) in enumerate(((far_ref, 1 - own), (near_ref, own))):
-        copies[k].wait()
+        copies[k + 1].wait()
         for b in range(blocks):
-            scale = scales_ref[column, block + which * blocks + b]
+            scale = factors[column, block + which * blocks + b]
             part = held[k, b * BLK : (b + 1) * BLK, :].astype(jnp.float32) * scale
             out_ref[b * BLK : (b + 1) * BLK, :] = part.astype(jnp.bfloat16)
         out_ref[depth:, :] = ids
     copy_ref[...] = near_ref[...]
 
 
-def scaled_weight(codes, scales, segment_ids, depth, group, zz, column):
+def scaled_weight(codes, scales, segment_ids, depth):
     width = codes.shape[1]
-    first = jnp.stack([zz, column, group * (2 * depth // BLK)]).astype(jnp.int32)
     out = jax.ShapeDtypeStruct((depth + PAD, width), jnp.bfloat16)
     return pl.pallas_call(
         scale_kernel,
         in_specs=[
-            pl.BlockSpec(memory_space=pltpu.SMEM),
             pl.BlockSpec(memory_space=pltpu.HBM),
-            pl.BlockSpec(memory_space=pltpu.SMEM),
+            pl.BlockSpec(memory_space=pltpu.HBM),
             pl.BlockSpec(memory_space=pltpu.VMEM),
         ],
         out_specs=[pl.BlockSpec(memory_space=pltpu.VMEM)] * 3,
         out_shape=[out, out, out],
         scratch_shapes=[
             pltpu.VMEM((2, depth, width), jnp.bfloat16),
-            pltpu.SemaphoreType.DMA((2,)),
+            pltpu.SMEM(scales.shape[::-1], jnp.float32),
+            pltpu.SemaphoreType.DMA((3,)),
         ],
         compiler_params=pltpu.CompilerParams(vmem_limit_bytes=56 * MIB),
         name="scale",
-    )(first, codes, scales.T, segment_ids.reshape(1, -1))
+    )(codes, scales.T, segment_ids.reshape(1, -1))
 
 
 def gather_by_steps(sizes, hidden, codes, scales, segment_ids):
@@ -109,19 +114,17 @@
     def along_shard(distance):
         return lambda g, s, c: (g, s ^ distance, c)
 
-    near, far, later = scaled_weight(
-        codes, scales, segment_ids, depth, group, zz, shard * codes.shape[1] // BLK
-    )
+    near, far, later = scaled_weight(codes, scales, segment_ids, depth)
+    piece = {0: near}
     def quarter(dg, dz):
         first = (jnp.bitwise_xor(group, dg) * 2 + jnp.bitwise_xor(zz, dz)) * depth
         return lax.dynamic_slice_in_dim(hidden, first, depth, 1)
 
     across = send(quarter(1, 1), lambda g, s, c: (1 - g, s, c))
     stays = send(quarter(1, 0), lambda g, s, c: (1 - g, s, c))
-    piece = {0: near}
     piece[6] = send(far, along_shard(6))
+    piece[1] = send(near, along_shard(1))
     piece[2] = send(far, along_shard(2))
-    piece[1] = send(near, along_shard(1))
     piece[4] = send(gate(later, piece[2]), along_shard(4))
     pair = jnp.concatenate(
         [
@@ -130,10 +133,11 @@
         ],
         axis=0,
     )
-    pair = send(pair, along_shard(2))
+    pair = send(gate(pair, piece[1]), along_shard(2))
     piece[3] = send(piece[2], along_shard(1))
-    piece[6] = gate(piece[6], piece[3])
+    piece[6] = gate(piece[6], piece[3], stays)
     piece[7] = send(piece[6], along_shard(1))
+    piece[4] = gate(piece[4], stays)
     piece[5] = send(piece[4], along_shard(1))
     arrays = [hidden, stays, pair]
     copies = [(0, 0, member * depth), (2, 0, 0), (1, 0, 0), (2, rows, 0)]
@@ -146,11 +150,11 @@
     if early:
         mine_ref, other_ref, own_ref, ids_ref, left, right, sems = refs
     else:
-        own_ref, mine_ref, other_ref, ids_ref, left, right, sems = refs
+        own_ref, left, mine_ref, other_ref, ids_ref, right, sems = refs
     rows, depth = mine_ref.shape[1], left.shape[1]
     count = len(copies)
     started = []
-    for k, (at, row) in enumerate(copies):
+    for k, (at, row) in enumerate(copies if early else []):
         first = pl.multiple_of(table_ref[k], HD)
         started.append(
             pltpu.make_async_copy(
@@ -174,11 +178,12 @@
         )
     for copy in started:
         copy.start()
-    for copy in started[:count]:
+    moved = count if early else 0
+    for copy in started[:moved]:
         copy.wait()
 
     def head(h):
-        for copy in started[count + 2 * h : count + 2 * h + 2]:
+        for copy in started[moved + 2 * h : moved + 2 * h + 2]:
             copy.wait()
         total = jnp.dot(left[...], right[h], preferred_element_type=jnp.float32)
         return total.reshape(mine_ref.shape)
@@ -202,28 +207,27 @@
         own_ref[...] = head(2)
     else:
         put(mine_ref, other_ref, own_ref[...], head(0))
-    for copy in started[count + 2 * heads :]:
+    for copy in started[moved + 2 * heads :]:
         copy.wait()
 
 
-def project_heads(early, arrays, copies, pieces, table, rows, own=None):
+def project_heads(early, arrays, copies, pieces, table, rows, held=()):
     heads = len(pieces) // 2
     depth = arrays[-1].shape[1]
     members = len(copies)
     out = jax.ShapeDtypeStruct((members, rows, 2 * HD), jnp.float32)
     ids = jax.ShapeDtypeStruct((len(pieces), PAD, HD), jnp.bfloat16)
     vmem = pl.BlockSpec(memory_space=pltpu.VMEM)
-    extra = [] if early else [own]
-    results = [out] * (3 if early else 2) + [ids]
+    rows_of = jax.ShapeDtypeStruct((members * rows, depth), jnp.bfloat16)
+    results = [out] * (3 if early else 2) + [ids] + [rows_of] * early
     return pl.pallas_call(
         functools.partial(head_kernel, [c[:2] for c in copies], heads, early),
         in_specs=[pl.BlockSpec(memory_space=pltpu.SMEM)]
         + [pl.BlockSpec(memory_space=pl.ANY)] * (len(arrays) + len(pieces))
-        + [vmem] * len(extra),
+        + [vmem] * len(held),
         out_specs=[vmem] * len(results),
         out_shape=results,
         scratch_shapes=[
-            pltpu.VMEM((members * rows, depth), jnp.bfloat16),
             pltpu.VMEM((heads, depth, 2 * HD), jnp.bfloat16),
             pltpu.SemaphoreType.DMA((members + 2 * len(pieces),)),
         ],
@@ -234,7 +238,7 @@
             transcendentals=0,
         ),
         name="project_early" if early else "project_late",
-    )(table, *arrays, *pieces, *extra)
+    )(table, *arrays, *pieces, *held)
 
 
 def share_kernel(mine_ref, got_ref, own_ref, *out_refs):
@@ -310,12 +314,12 @@
         )
 
     order = (2, 3, 6, 7, 0, 1)
-    mine, other, own, ids = project_heads(
+    mine, other, own, ids, left = project_heads(
         True, arrays, copies, [piece[d] for d in order], table, rows
     )
     flipped = exchanged(mine, other)
     mine, other, last = project_heads(
-        False, arrays, copies, [piece[4], piece[5]], table, rows, own
+        False, arrays, copies, [piece[4], piece[5]], table, rows, (own, left)
     )
     straight = exchanged(mine, other)
     keyval = summed(

time: 115 us -> 114 us (level)
  no operation moved by 1% of the time
where the time goes in v6:
time: 114 us
  waiting for transfers between devices  71.7 us (63%)
  starting transfers between devices  20.3 us (18%)
  Pallas kernels  17.7 us (16%)
  local copies, waits for them, and re-layouts  2.82 us (2%)
  other arithmetic  1.43 us (1%)
    ppermute x10, waiting for transfers between devices, send(): return lax.ppermute(value, ALL, flat_pairs(sizes, move))  49.4 us
    ppermute x5, waiting for transfers between devices, on_device(): pieces.append(lax.ppermute(keyval, ALL, up))  17.6 us
    pallas_call x2, Pallas kernels, project_heads(): pl.pallas_call(functools.partial(head_kernel, [c[:2] for c in copies], he...  7.95 us
    ppermute x10, starting transfers between devices, send(): return lax.ppermute(value, ALL, flat_pairs(sizes, move))  7 us
    ppermute x5, starting transfers between devices, on_device(): pieces.append(lax.ppermute(keyval, ALL, up))  6.46 us
    pallas_call x1, Pallas kernels, attend(): pl.pallas_call(functools.partial(attend_kernel, len(pieces), QPK, stack),...  6.25 us
    ppermute x2, waiting for transfers between devices, exchanged(): lax.ppermute(to_x, ALL, over_x)  3.42 us
    pallas_call x1, Pallas kernels, scaled_weight(): pl.pallas_call(scale_kernel, in_specs=[pl.BlockSpec(memory_space=pltpu.HB...  3.24 us
  transfers between devices with their start and end apart: 23, of which 12 were waited for; matrix products, arithmetic and copies ran while one was open for 4% of the time, Pallas kernels for 7%

profile of v6, /device:TPU:28, one launch (start us, length us, event | category | flops | bytes accessed | tf_op | source)
XLA Modules:
  0.0 114.1 jit_solution(4814162816440577800)
XLA Ops:
  0.0 3.2 %scale.1 = (bf16[2064,128]{1,0:T(8,128)(2,1)}, bf16[2064,128]{1,0:T(8,128)(2,1)}, bf16[2064,128]{1,0:T(8,128)(2,1)}) custom-call(bf16[8192,128]{1,0:T(8,128)(2,1)} %codes_ref.1, f32[8,64]{1,0:T(8,128)} %bitcast.24, s32[1,128]{1,0:T(1,128)} %bitcast.25), custom_call_target="tpu_custom_call" | custom-call | tf_op jit(solution)/shard_map/scale/pallas_call | solution.py:85
  3.8 0.9 constant_dynamic-slice_fusion.1
  4.7 1.5 %collective-permute-start.1 = (bf16[128,2048]{1,0:T(8,128)(2,1)S(1)}, bf16[128,2048]{1,0:T(8,128)(2,1)S(1)}, u32[]{:S(2)}, u32[]{:S(2)}) collective-permute-start(bf16[128,2048]{1,0:T(8,128)(2,1)S(1)} %get-tuple-element.44), channel_id=1, source_target_pairs={{0,16},{1,17},{2,18},{3,19},{4,20},{5,21},{6,22},{7,23},{8,24},{9,... | collective-permute-start | bytes 1572872 | tf_op jit(solution)/shard_map/ppermute | solution.py:112
  6.7 1.3 %collective-permute-start.6 = (bf16[2064,128]{1,0:T(8,128)(2,1)}, bf16[2064,128]{1,0:T(8,128)(2,1)}, u32[]{:S(2)}, u32[]{:S(2)}) collective-permute-start(bf16[2064,128]{1,0:T(8,128)(2,1)} %get-tuple-element.25), channel_id=1, source_target_pairs={{0,12},{1,13},{2,14},{3,15},{4,8},{5,9},{6,10},{7,11},{8,4},{9,5},... | collective-permute-start | bytes 1585160 | tf_op jit(solution)/shard_map/ppermute | solution.py:112
  8.6 19.1 %collective-permute-done.4.refs_3_.refs_0_ = bf16[2064,128]{1,0:T(8,128)(2,1)} collective-permute-done((bf16[2064,128]{1,0:T(8,128)(2,1)}, bf16[2064,128]{1,0:T(8,128)(2,1)}, u32[]{:S(2)}, u32[]{:S(2)}) %collective-permute-start.4) | collective-permute-done | bytes 528416 | tf_op jit(solution)/shard_map/ppermute | solution.py:112
  27.7 0.6 collective-permute-start.5
  28.3 1.1 pad_maximum_fusion.value_ref
  29.4 0.6 gather_fusion
  30.2 12.2 %collective-permute-done.5.refs_0_.refs_4_ = bf16[2064,128]{1,0:T(8,128)(2,1)} collective-permute-done((bf16[2064,128]{1,0:T(8,128)(2,1)}, bf16[2064,128]{1,0:T(8,128)(2,1)}, u32[]{:S(2)}, u32[]{:S(2)}) %collective-permute-start.5) | collective-permute-done | bytes 528416 | tf_op jit(solution)/shard_map/ppermute | solution.py:112
  42.9 12.1 %collective-permute-done.8.value_ref = bf16[2064,128]{1,0:T(8,128)(2,1)} collective-permute-done((bf16[2064,128]{1,0:T(8,128)(2,1)}, bf16[2064,128]{1,0:T(8,128)(2,1)}, u32[]{:S(2)}, u32[]{:S(2)}) %collective-permute-start.8) | collective-permute-done | bytes 528416 | tf_op jit(solution)/shard_map/ppermute | solution.py:112
  55.0 1.5 %collective-permute-start.9 = (bf16[2064,128]{1,0:T(8,128)(2,1)}, bf16[2064,128]{1,0:T(8,128)(2,1)S(1)}, u32[]{:S(2)}, u32[]{:S(2)}) collective-permute-start(bf16[2064,128]{1,0:T(8,128)(2,1)} %gate.7.refs_3_), channel_id=1, source_target_pairs={{0,2},{1,3},{2,0},{3,1},{4,6},{5,7},{6,4},{7,5},{8,10},{9,11},{10,... | collective-permute-start | bytes 1585160 | tf_op jit(solution)/shard_map/ppermute | solution.py:112
  56.6 5.9 %collective-permute-done.3.refs_2_ = bf16[256,2048]{1,0:T(8,128)(2,1)} collective-permute-done((bf16[256,2048]{1,0:T(8,128)(2,1)}, bf16[256,2048]{1,0:T(8,128)(2,1)}, u32[]{:S(2)}, u32[]{:S(2)}) %collective-permute-start.3) | collective-permute-done | bytes 1048608 | tf_op jit(solution)/shard_map/ppermute | solution.py:112
  62.5 5.5 %project_early.1 = (f32[4,128,256]{2,1,0:T(8,128)S(1)}, f32[4,128,256]{2,1,0:T(8,128)S(1)}, f32[4,128,256]{2,1,0:T(8,128)S(1)}, bf16[6,16,128]{2,1,0:T(8,128)(2,1)S(1)}, bf16[512,2048]{1,0:T(8,128)(2,1)S(1)}) custom-call(s32[6]{0:T(128)S(1)} %stack.19.table_ref, bf16[128,8192]{1,0:T(8,128)(2,1)S(1)} %copy-done, ...), custom_call_target="tpu_custom_call" | custom-call | tf_op jit(solution)/shard_map/project_early/pallas_call | solution.py:223
  68.1 2.4 %project_late.1 = (f32[4,128,256]{2,1,0:T(8,128)S(1)}, f32[4,128,256]{2,1,0:T(8,128)S(1)}, bf16[2,16,128]{2,1,0:T(8,128)(2,1)S(1)}) custom-call(s32[6]{0:T(128)S(1)} %stack.19.table_ref, bf16[128,8192]{1,0:T(8,128)(2,1)S(1)} %copy-done, bf16[128,2048]{1,0:T(8,128)(2,1)S(1)} %collective-permute-done.refs_1_.refs_0_, ...), custom_call_target="tpu_custom_call" | custom-call | flops 53687091200 | bytes 3145728 | tf_op jit(solution)/shard_map/project_late/pallas_call | solution.py:223
  71.3 1.5 %collective-permute-start.12 = (bf16[128,384]{1,0:T(8,128)(2,1)S(1)}, bf16[128,384]{1,0:T(8,128)(2,1)S(1)}, u32[]{:S(2)}, u32[]{:S(2)}) collective-permute-start(bf16[128,384]{1,0:T(8,128)(2,1)S(1)} %get-tuple-element.36), channel_id=1, source_target_pairs={{0,20},{1,21},{2,22},{3,23},{4,16},{5,17},{6,18},{7,19},{8,28},{9,... | collective-permute-start | bytes 294920 | tf_op jit(solution)/shard_map/ppermute | solution.py:311
  72.9 1.5 %collective-permute-start.13 = (bf16[128,384]{1,0:T(8,128)(2,1)S(1)}, bf16[128,384]{1,0:T(8,128)(2,1)S(1)}, u32[]{:S(2)}, u32[]{:S(2)}) collective-permute-start(bf16[128,384]{1,0:T(8,128)(2,1)S(1)} %get-tuple-element.37), channel_id=1, source_target_pairs={{0,4},{1,5},{2,6},{3,7},{4,0},{5,1},{6,2},{7,3},{8,12},{9,13},{10,... | collective-permute-start | bytes 294920 | tf_op jit(solution)/shard_map/ppermute | solution.py:312
  75.0 1.6 %collective-permute-start.14 = (bf16[128,384]{1,0:T(8,128)(2,1)S(1)}, bf16[128,384]{1,0:T(8,128)(2,1)S(1)}, u32[]{:S(2)}, u32[]{:S(2)}) collective-permute-start(bf16[128,384]{1,0:T(8,128)(2,1)S(1)} %get-tuple-element.38), channel_id=1, source_target_pairs={{0,16},{1,17},{2,18},{3,19},{4,20},{5,21},{6,22},{7,23},{8,24},{9,... | collective-permute-start | bytes 294920 | tf_op jit(solution)/shard_map/ppermute | solution.py:313
  77.0 0.9 collective-permute-done.12.refs_1_
  78.0 0.6 collective-permute-start.16
  78.5 0.6 gather_fusion.1
  79.1 0.6 gather_fusion.2
  80.1 1.2 %collective-permute-done.17.refs_7_ = bf16[128,384]{1,0:T(8,128)(2,1)S(1)} collective-permute-done((bf16[128,384]{1,0:T(8,128)(2,1)S(1)}, bf16[128,384]{1,0:T(8,128)(2,1)S(1)}, u32[]{:S(2)}, u32[]{:S(2)}) %collective-permute-start.17) | collective-permute-done | bytes 98336 | tf_op jit(solution)/shard_map/ppermute | solution.py:313
  81.3 2.2 %collective-permute-done.14.refs_3_ = bf16[128,384]{1,0:T(8,128)(2,1)S(1)} collective-permute-done((bf16[128,384]{1,0:T(8,128)(2,1)S(1)}, bf16[128,384]{1,0:T(8,128)(2,1)S(1)}, u32[]{:S(2)}, u32[]{:S(2)}) %collective-permute-start.14) | collective-permute-done | bytes 98336 | tf_op jit(solution)/shard_map/ppermute | solution.py:313
  83.6 1.3 %collective-permute-start.18 = (bf16[128,512]{1,0:T(8,128)(2,1)S(1)}, bf16[128,512]{1,0:T(8,128)(2,1)S(1)}, u32[]{:S(2)}, u32[]{:S(2)}) collective-permute-start(bf16[128,512]{1,0:T(8,128)(2,1)S(1)} %sum.1.refs_0_), channel_id=1, source_target_pairs={{0,2},{1,3},{2,4},{3,5},{4,6},{5,7},{6,8},{7,9},{8,10},{9,11},{10,... | collective-permute-start | bytes 393224 | tf_op jit(solution)/shard_map/ppermute | solution.py:569
  84.9 1.3 %collective-permute-start.19 = (bf16[128,512]{1,0:T(8,128)(2,1)S(1)}, bf16[128,512]{1,0:T(8,128)(2,1)S(1)}, u32[]{:S(2)}, u32[]{:S(2)}) collective-permute-start(bf16[128,512]{1,0:T(8,128)(2,1)S(1)} %sum.1.refs_0_), channel_id=1, source_target_pairs={{0,4},{1,5},{2,6},{3,7},{4,8},{5,9},{6,10},{7,11},{8,12},{9,13},{1... | collective-permute-start | bytes 393224 | tf_op jit(solution)/shard_map/ppermute | solution.py:569
  86.2 1.3 %collective-permute-start.20 = (bf16[128,512]{1,0:T(8,128)(2,1)S(1)}, bf16[128,512]{1,0:T(8,128)(2,1)S(1)}, u32[]{:S(2)}, u32[]{:S(2)}) collective-permute-start(bf16[128,512]{1,0:T(8,128)(2,1)S(1)} %sum.1.refs_0_), channel_id=1, source_target_pairs={{0,6},{1,7},{2,8},{3,9},{4,10},{5,11},{6,12},{7,13},{8,14},{9,15},... | collective-permute-start | bytes 393224 | tf_op jit(solution)/shard_map/ppermute | solution.py:569
  87.5 1.3 %collective-permute-start.21 = (bf16[128,512]{1,0:T(8,128)(2,1)S(1)}, bf16[128,512]{1,0:T(8,128)(2,1)S(1)}, u32[]{:S(2)}, u32[]{:S(2)}) collective-permute-start(bf16[128,512]{1,0:T(8,128)(2,1)S(1)} %sum.1.refs_0_), channel_id=1, source_target_pairs={{0,8},{1,9},{2,10},{3,11},{4,12},{5,13},{6,14},{7,15},{16,24},{17,... | collective-permute-start | bytes 393224 | tf_op jit(solution)/shard_map/ppermute | solution.py:569
  88.8 1.3 %collective-permute-start.22 = (bf16[128,512]{1,0:T(8,128)(2,1)S(1)}, bf16[128,512]{1,0:T(8,128)(2,1)S(1)}, u32[]{:S(2)}, u32[]{:S(2)}) collective-permute-start(bf16[128,512]{1,0:T(8,128)(2,1)S(1)} %sum.1.refs_0_), channel_id=1, source_target_pairs={{0,10},{1,11},{2,12},{3,13},{4,14},{5,15},{16,26},{17,27},{18,28},... | collective-permute-start | bytes 393224 | tf_op jit(solution)/shard_map/ppermute | solution.py:569
  90.5 3.3 %collective-permute-done.19.refs_2_ = bf16[128,512]{1,0:T(8,128)(2,1)S(1)} collective-permute-done((bf16[128,512]{1,0:T(8,128)(2,1)S(1)}, bf16[128,512]{1,0:T(8,128)(2,1)S(1)}, u32[]{:S(2)}, u32[]{:S(2)}) %collective-permute-start.19) | collective-permute-done | bytes 131104 | tf_op jit(solution)/shard_map/ppermute | solution.py:569
  93.7 3.7 %collective-permute-done.20.refs_3_ = bf16[128,512]{1,0:T(8,128)(2,1)S(1)} collective-permute-done((bf16[128,512]{1,0:T(8,128)(2,1)S(1)}, bf16[128,512]{1,0:T(8,128)(2,1)S(1)}, u32[]{:S(2)}, u32[]{:S(2)}) %collective-permute-start.20) | collective-permute-done | bytes 131104 | tf_op jit(solution)/shard_map/ppermute | solution.py:569
  97.5 10.4 %collective-permute-done.21.refs_4_ = bf16[128,512]{1,0:T(8,128)(2,1)S(1)} collective-permute-done((bf16[128,512]{1,0:T(8,128)(2,1)S(1)}, bf16[128,512]{1,0:T(8,128)(2,1)S(1)}, u32[]{:S(2)}, u32[]{:S(2)}) %collective-permute-start.21) | collective-permute-done | bytes 131104 | tf_op jit(solution)/shard_map/ppermute | solution.py:569
  107.9 6.3 %attend.1 = bf16[128,4096]{1,0:T(8,128)(2,1)} custom-call(bf16[128,4096]{1,0:T(8,128)(2,1)S(1)} %copy-done.1, f32[128,768]{1,0:T(8,128)S(1)} %and_select_fusion.bias_ref, bf16[128,512]{1,0:T(8,128)(2,1)S(1)} %sum.1.refs_0_, bf16[128,512]{1,0:T(8,128)(2,1)S(1)} %collective-permute-done.18.refs_1_, bf16[128,512]{1,0:T(8,128)(2,1)S(1)} %collective-permute-done.19.refs_2_, ...), custom_call_target="tpu_custom_call" | custom-call | tf_op jit(solution)/shard_map/attend/pallas_call | solution.py:514
  (58 shorter events, 5.1 us)
Async XLA Ops:
  0.0 3.8 %copy-start = (bf16[128,8192]{1,0:T(8,128)(2,1)S(1)}, bf16[128,8192]{1,0:T(8,128)(2,1)}, u32[]{:S(2)}) copy-start(bf16[128,8192]{1,0:T(8,128)(2,1)} %refs_0_.3) | copy-start | bytes 6291460
  3.2 24.5 %collective-permute-start.4 = (bf16[2064,128]{1,0:T(8,128)(2,1)}, bf16[2064,128]{1,0:T(8,128)(2,1)}, u32[]{:S(2)}, u32[]{:S(2)}) collective-permute-start(bf16[2064,128]{1,0:T(8,128)(2,1)} %get-tuple-element.25), channel_id=1, source_target_pairs={{0,4},{1,5},{2,6},{3,7},{4,0},{5,1},{6,2},{7,3},{8,12},{9,13},{10,... | collective-permute-start | bytes 1585160 | tf_op jit(solution)/shard_map/ppermute | solution.py:112
  3.8 2.4 %copy-start.2 = (bf16[2064,128]{1,0:T(8,128)(2,1)S(1)}, bf16[2064,128]{1,0:T(8,128)(2,1)}, u32[]{:S(2)}) copy-start(bf16[2064,128]{1,0:T(8,128)(2,1)} %get-tuple-element.24.refs_7_) | copy-start | bytes 1585156
  4.7 23.0 %collective-permute-start.1 = (bf16[128,2048]{1,0:T(8,128)(2,1)S(1)}, bf16[128,2048]{1,0:T(8,128)(2,1)S(1)}, u32[]{:S(2)}, u32[]{:S(2)}) collective-permute-start(bf16[128,2048]{1,0:T(8,128)(2,1)S(1)} %get-tuple-element.44), channel_id=1, source_target_pairs={{0,16},{1,17},{2,18},{3,19},{4,20},{5,21},{6,22},{7,23},{8,24},{9,... | collective-permute-start | bytes 1572872 | tf_op jit(solution)/shard_map/ppermute | solution.py:112
  6.2 23.2 %collective-permute-start.2 = (bf16[2064,128]{1,0:T(8,128)(2,1)S(1)}, bf16[2064,128]{1,0:T(8,128)(2,1)S(1)}, u32[]{:S(2)}, u32[]{:S(2)}) collective-permute-start(bf16[2064,128]{1,0:T(8,128)(2,1)S(1)} %copy-done.2), channel_id=1, source_target_pairs={{0,2},{1,3},{2,0},{3,1},{4,6},{5,7},{6,4},{7,5},{8,10},{9,11},{10,... | collective-permute-start | bytes 1585160 | tf_op jit(solution)/shard_map/ppermute | solution.py:112
  6.7 23.5 %collective-permute-start.6 = (bf16[2064,128]{1,0:T(8,128)(2,1)}, bf16[2064,128]{1,0:T(8,128)(2,1)}, u32[]{:S(2)}, u32[]{:S(2)}) collective-permute-start(bf16[2064,128]{1,0:T(8,128)(2,1)} %get-tuple-element.25), channel_id=1, source_target_pairs={{0,12},{1,13},{2,14},{3,15},{4,8},{5,9},{6,10},{7,11},{8,4},{9,5},... | collective-permute-start | bytes 1585160 | tf_op jit(solution)/shard_map/ppermute | solution.py:112
  8.0 22.1 %collective-permute-start = (bf16[128,2048]{1,0:T(8,128)(2,1)}, bf16[128,2048]{1,0:T(8,128)(2,1)S(1)}, u32[]{:S(2)}, u32[]{:S(2)}) collective-permute-start(bf16[128,2048]{1,0:T(8,128)(2,1)} %get-tuple-element.45), channel_id=1, source_target_pairs={{0,16},{1,17},{2,18},{3,19},{4,20},{5,21},{6,22},{7,23},{8,24},{9,... | collective-permute-start | bytes 1572872 | tf_op jit(solution)/shard_map/ppermute | solution.py:112
  27.7 27.3 %collective-permute-start.8 = (bf16[2064,128]{1,0:T(8,128)(2,1)}, bf16[2064,128]{1,0:T(8,128)(2,1)}, u32[]{:S(2)}, u32[]{:S(2)}) collective-permute-start(bf16[2064,128]{1,0:T(8,128)(2,1)} %gate.6), channel_id=1, source_target_pairs={{0,8},{1,9},{2,10},{3,11},{4,12},{5,13},{6,14},{7,15},{8,0},{9,1},... | collective-permute-start | bytes 1585160 | tf_op jit(solution)/shard_map/ppermute | solution.py:112
  27.7 14.7 %collective-permute-start.5 = (bf16[2064,128]{1,0:T(8,128)(2,1)}, bf16[2064,128]{1,0:T(8,128)(2,1)}, u32[]{:S(2)}, u32[]{:S(2)}) collective-permute-start(bf16[2064,128]{1,0:T(8,128)(2,1)} %collective-permute-done.4.refs_3_.refs_0_), channel_id=1, source_target_pairs={{0,2},{1,3},{2,0},{3,1},{4,6},{5,7},{6,4},{7,5},{8,10},{9,11},{10,... | collective-permute-start | bytes 1585160 | tf_op jit(solution)/shard_map/ppermute | solution.py:112
  28.3 1.1 copy-start.5
  28.3 1.2 %copy-start.4 = (s32[8]{0:T(128)S(1)}, s32[8]{0:T(128)}, u32[]{:S(2)}) copy-start(s32[8]{0:T(128)} %constant.49.clone) | copy-start | bytes 100
  29.4 33.1 %collective-permute-start.3 = (bf16[256,2048]{1,0:T(8,128)(2,1)}, bf16[256,2048]{1,0:T(8,128)(2,1)}, u32[]{:S(2)}, u32[]{:S(2)}) collective-permute-start(bf16[256,2048]{1,0:T(8,128)(2,1)} %gate.4), channel_id=1, source_target_pairs={{0,4},{1,5},{2,6},{3,7},{4,0},{5,1},{6,2},{7,3},{8,12},{9,13},{10,... | collective-permute-start | bytes 3145736 | tf_op jit(solution)/shard_map/ppermute | solution.py:112
  30.2 32.3 %copy-start.3 = (bf16[2064,128]{1,0:T(8,128)(2,1)S(1)}, bf16[2064,128]{1,0:T(8,128)(2,1)}, u32[]{:S(2)}) copy-start(bf16[2064,128]{1,0:T(8,128)(2,1)} %get-tuple-element.24.refs_7_) | copy-start | bytes 1585156
  42.4 20.1 %collective-permute-start.7 = (bf16[2064,128]{1,0:T(8,128)(2,1)}, bf16[2064,128]{1,0:T(8,128)(2,1)S(1)}, u32[]{:S(2)}, u32[]{:S(2)}) collective-permute-start(bf16[2064,128]{1,0:T(8,128)(2,1)} %gate.5.refs_5_), channel_id=1, source_target_pairs={{0,2},{1,3},{2,0},{3,1},{4,6},{5,7},{6,4},{7,5},{8,10},{9,11},{10,... | collective-permute-start | bytes 1585160 | tf_op jit(solution)/shard_map/ppermute | solution.py:112
  55.0 13.1 %collective-permute-start.9 = (bf16[2064,128]{1,0:T(8,128)(2,1)}, bf16[2064,128]{1,0:T(8,128)(2,1)S(1)}, u32[]{:S(2)}, u32[]{:S(2)}) collective-permute-start(bf16[2064,128]{1,0:T(8,128)(2,1)} %gate.7.refs_3_), channel_id=1, source_target_pairs={{0,2},{1,3},{2,0},{3,1},{4,6},{5,7},{6,4},{7,5},{8,10},{9,11},{10,... | collective-permute-start | bytes 1585160 | tf_op jit(solution)/shard_map/ppermute | solution.py:112
  68.0 3.2 %collective-permute-start.11 = (f32[4,128,256]{2,1,0:T(8,128)S(1)}, f32[4,128,256]{2,1,0:T(8,128)S(1)}, u32[]{:S(2)}, u32[]{:S(2)}) collective-permute-start(f32[4,128,256]{2,1,0:T(8,128)S(1)} %get-tuple-element.35), channel_id=1, source_target_pairs={{0,1},{1,0},{2,3},{3,2},{4,5},{5,4},{6,7},{7,6},{8,9},{9,8},{10,11... | collective-permute-start | bytes 1572872 | tf_op jit(solution)/shard_map/ppermute | solution.py:308
  70.6 37.3 %copy-start.1 = (bf16[128,4096]{1,0:T(8,128)(2,1)S(1)}, bf16[128,4096]{1,0:T(8,128)(2,1)}, u32[]{:S(2)}) copy-start(bf16[128,4096]{1,0:T(8,128)(2,1)} %query_ref.1) | copy-start | bytes 3145732
  70.6 4.3 %collective-permute-start.10 = (f32[4,128,256]{2,1,0:T(8,128)S(1)}, f32[4,128,256]{2,1,0:T(8,128)S(1)}, u32[]{:S(2)}, u32[]{:S(2)}) collective-permute-start(f32[4,128,256]{2,1,0:T(8,128)S(1)} %get-tuple-element.32), channel_id=1, source_target_pairs={{0,1},{1,0},{2,3},{3,2},{4,5},{5,4},{6,7},{7,6},{8,9},{9,8},{10,11... | collective-permute-start | bytes 1572872 | tf_op jit(solution)/shard_map/ppermute | solution.py:308
  71.3 6.6 %collective-permute-start.12 = (bf16[128,384]{1,0:T(8,128)(2,1)S(1)}, bf16[128,384]{1,0:T(8,128)(2,1)S(1)}, u32[]{:S(2)}, u32[]{:S(2)}) collective-permute-start(bf16[128,384]{1,0:T(8,128)(2,1)S(1)} %get-tuple-element.36), channel_id=1, source_target_pairs={{0,20},{1,21},{2,22},{3,23},{4,16},{5,17},{6,18},{7,19},{8,28},{9,... | collective-permute-start | bytes 294920 | tf_op jit(solution)/shard_map/ppermute | solution.py:311
  72.9 7.2 %collective-permute-start.13 = (bf16[128,384]{1,0:T(8,128)(2,1)S(1)}, bf16[128,384]{1,0:T(8,128)(2,1)S(1)}, u32[]{:S(2)}, u32[]{:S(2)}) collective-permute-start(bf16[128,384]{1,0:T(8,128)(2,1)S(1)} %get-tuple-element.37), channel_id=1, source_target_pairs={{0,4},{1,5},{2,6},{3,7},{4,0},{5,1},{6,2},{7,3},{8,12},{9,13},{10,... | collective-permute-start | bytes 294920 | tf_op jit(solution)/shard_map/ppermute | solution.py:312
  74.4 6.9 %collective-permute-start.17 = (bf16[128,384]{1,0:T(8,128)(2,1)S(1)}, bf16[128,384]{1,0:T(8,128)(2,1)S(1)}, u32[]{:S(2)}, u32[]{:S(2)}) collective-permute-start(bf16[128,384]{1,0:T(8,128)(2,1)S(1)} %get-tuple-element.42), channel_id=1, source_target_pairs={{0,16},{1,17},{2,18},{3,19},{4,20},{5,21},{6,22},{7,23},{8,24},{9,... | collective-permute-start | bytes 294920 | tf_op jit(solution)/shard_map/ppermute | solution.py:313
  75.0 8.5 %collective-permute-start.14 = (bf16[128,384]{1,0:T(8,128)(2,1)S(1)}, bf16[128,384]{1,0:T(8,128)(2,1)S(1)}, u32[]{:S(2)}, u32[]{:S(2)}) collective-permute-start(bf16[128,384]{1,0:T(8,128)(2,1)S(1)} %get-tuple-element.38), channel_id=1, source_target_pairs={{0,16},{1,17},{2,18},{3,19},{4,20},{5,21},{6,22},{7,23},{8,24},{9,... | collective-permute-start | bytes 294920 | tf_op jit(solution)/shard_map/ppermute | solution.py:313
  76.5 7.0 %collective-permute-start.15 = (bf16[128,384]{1,0:T(8,128)(2,1)S(1)}, bf16[128,384]{1,0:T(8,128)(2,1)S(1)}, u32[]{:S(2)}, u32[]{:S(2)}) collective-permute-start(bf16[128,384]{1,0:T(8,128)(2,1)S(1)} %get-tuple-element.40), channel_id=1, source_target_pairs={{0,20},{1,21},{2,22},{3,23},{4,16},{5,17},{6,18},{7,19},{8,28},{9,... | collective-permute-start | bytes 294920 | tf_op jit(solution)/shard_map/ppermute | solution.py:311
  78.0 5.6 %collective-permute-start.16 = (bf16[128,384]{1,0:T(8,128)(2,1)S(1)}, bf16[128,384]{1,0:T(8,128)(2,1)S(1)}, u32[]{:S(2)}, u32[]{:S(2)}) collective-permute-start(bf16[128,384]{1,0:T(8,128)(2,1)S(1)} %get-tuple-element.41), channel_id=1, source_target_pairs={{0,4},{1,5},{2,6},{3,7},{4,0},{5,1},{6,2},{7,3},{8,12},{9,13},{10,... | collective-permute-start | bytes 294920 | tf_op jit(solution)/shard_map/ppermute | solution.py:312
  83.6 6.9 %collective-permute-start.18 = (bf16[128,512]{1,0:T(8,128)(2,1)S(1)}, bf16[128,512]{1,0:T(8,128)(2,1)S(1)}, u32[]{:S(2)}, u32[]{:S(2)}) collective-permute-start(bf16[128,512]{1,0:T(8,128)(2,1)S(1)} %sum.1.refs_0_), channel_id=1, source_target_pairs={{0,2},{1,3},{2,4},{3,5},{4,6},{5,7},{6,8},{7,9},{8,10},{9,11},{10,... | collective-permute-start | bytes 393224 | tf_op jit(solution)/shard_map/ppermute | solution.py:569
  84.9 8.8 %collective-permute-start.19 = (bf16[128,512]{1,0:T(8,128)(2,1)S(1)}, bf16[128,512]{1,0:T(8,128)(2,1)S(1)}, u32[]{:S(2)}, u32[]{:S(2)}) collective-permute-start(bf16[128,512]{1,0:T(8,128)(2,1)S(1)} %sum.1.refs_0_), channel_id=1, source_target_pairs={{0,4},{1,5},{2,6},{3,7},{4,8},{5,9},{6,10},{7,11},{8,12},{9,13},{1... | collective-permute-start | bytes 393224 | tf_op jit(solution)/shard_map/ppermute | solution.py:569
  86.2 11.3 %collective-permute-start.20 = (bf16[128,512]{1,0:T(8,128)(2,1)S(1)}, bf16[128,512]{1,0:T(8,128)(2,1)S(1)}, u32[]{:S(2)}, u32[]{:S(2)}) collective-permute-start(bf16[128,512]{1,0:T(8,128)(2,1)S(1)} %sum.1.refs_0_), channel_id=1, source_target_pairs={{0,6},{1,7},{2,8},{3,9},{4,10},{5,11},{6,12},{7,13},{8,14},{9,15},... | collective-permute-start | bytes 393224 | tf_op jit(solution)/shard_map/ppermute | solution.py:569
  87.5 20.3 %collective-permute-start.21 = (bf16[128,512]{1,0:T(8,128)(2,1)S(1)}, bf16[128,512]{1,0:T(8,128)(2,1)S(1)}, u32[]{:S(2)}, u32[]{:S(2)}) collective-permute-start(bf16[128,512]{1,0:T(8,128)(2,1)S(1)} %sum.1.refs_0_), channel_id=1, source_target_pairs={{0,8},{1,9},{2,10},{3,11},{4,12},{5,13},{6,14},{7,15},{16,24},{17,... | collective-permute-start | bytes 393224 | tf_op jit(solution)/shard_map/ppermute | solution.py:569
  88.8 19.0 %collective-permute-start.22 = (bf16[128,512]{1,0:T(8,128)(2,1)S(1)}, bf16[128,512]{1,0:T(8,128)(2,1)S(1)}, u32[]{:S(2)}, u32[]{:S(2)}) collective-permute-start(bf16[128,512]{1,0:T(8,128)(2,1)S(1)} %sum.1.refs_0_), channel_id=1, source_target_pairs={{0,10},{1,11},{2,12},{3,13},{4,14},{5,15},{16,26},{17,27},{18,28},... | collective-permute-start | bytes 393224 | tf_op jit(solution)/shard_map/ppermute | solution.py:569
